TPU v7x, 256 devices: a whole 4x4x8 slice. The times are simulated.
256 devices in a mesh: dp: 8 (over z), ctx: 8 (over x, core), seq: 4 (over y).
Axes of the slice: x: 4, y: 4, z: 8, core: 2. Of those that a mesh axis runs over, the one named last changes fastest.
Arguments:
- query_nope: bfloat16 [8, 2048, 16, 128], P('dp', ('ctx', 'seq')), may hold values from -6 to 6
- query_rope: bfloat16 [8, 2048, 16, 64], P('dp', ('ctx', 'seq')), may hold values from -8 to 8
- latent: bfloat16 [8, 2048, 512], P('dp', ('ctx', 'seq')), may hold values from -6 to 6
- key_rope: bfloat16 [8, 2048, 64], P('dp', ('ctx', 'seq')), may hold values from -8 to 8
- out_grad: bfloat16 [8, 2048, 2048], P('dp', ('ctx', 'seq')), may hold values from -6 to 6
- key_weight: bfloat16 [512, 2048], P(None, 'ctx'), may hold values from -0.25 to 0.25
- value_weight: bfloat16 [512, 2048], P(None, 'ctx'), may hold values from -0.25 to 0.25
- block_doc: int32 [8, 32], P('dp'), may hold values from 0 to 3, never falling along the last dimension, each value on 1 to 16 neighbouring positions
- block_image: int32 [8, 32], P('dp'), may hold values from 0 to 15, never falling along the last dimension, each value on 1 to 4 neighbouring positions
- block_flag: int32 [8, 32], P('dp'), may hold values 0 or 1
Outputs:
- attended: bfloat16 [8, 2048, 2048], P('dp', ('ctx', 'seq'))
- query_nope_grad: bfloat16 [8, 2048, 16, 128], P('dp', ('ctx', 'seq'))
- query_rope_grad: bfloat16 [8, 2048, 16, 64], P('dp', ('ctx', 'seq'))
- latent_grad: bfloat16 [8, 2048, 512], P('dp', ('ctx', 'seq'))
- key_rope_grad: bfloat16 [8, 2048, 64], P('dp', ('ctx', 'seq'))
- key_weight_grad: float32 [512, 2048], P(('dp', 'seq'), 'ctx')
- value_weight_grad: float32 [512, 2048], P(('dp', 'seq'), 'ctx')
Inputs may be any that keep to these rules, and one draw needn't show every extreme that they name: `block_doc`: never falls along a sequence; each document spans 1 to 16 blocks, one exactly that many. `block_image`: never falls along a sequence; each segment spans 1 to 4 blocks.
All inputs are finite; a program needn't handle non-finite values. No bound on the sum of `block_flag` on one device may be relied on, other than what follows from the above.
Results may differ from a plain program's by a relative error of at most 0.0095.
Values may be sent and summed in bfloat16 or wider, within the bound.
A program may use at most 64 MiB of HBM per device.

v0:
```python
import math

import jax
import jax.numpy as jnp
from jax import lax
from jax.sharding import PartitionSpec as P

NEG = -1e30


def on_device(
    query_nope,
    query_rope,
    latent,
    key_rope,
    out_grad,
    key_weight,
    value_weight,
    block_doc,
    block_image,
    block_flag,
):
    ctx_count = lax.axis_size("ctx")
    seq_count = lax.axis_size("seq")
    seq_index = lax.axis_index("seq")
    tok_rows = query_nope.shape[1]
    head_total = query_nope.shape[2]
    width_n = query_nope.shape[3]
    width_r = query_rope.shape[3]
    block_total = block_doc.shape[1]
    seq_total = tok_rows * ctx_count * seq_count
    block_len = seq_total // block_total
    head_dev = head_total // ctx_count
    score_scale = 1.0 / math.sqrt(width_n + width_r)
    high = lax.Precision.HIGHEST
    grad_in = out_grad[0].reshape(tok_rows, head_total, width_n)
    query_n, query_r, grad_o = (
        lax.all_to_all(query_nope[0], "ctx", split_axis=1, concat_axis=0, tiled=True),
        lax.all_to_all(query_rope[0], "ctx", split_axis=1, concat_axis=0, tiled=True),
        lax.all_to_all(grad_in, "ctx", split_axis=1, concat_axis=0, tiled=True),
    )
    query_rows = tok_rows * ctx_count
    lat_all, rope_keys = (
        lax.all_gather(latent[0], ("ctx", "seq"), axis=0, tiled=True),
        lax.all_gather(key_rope[0], ("ctx", "seq"), axis=0, tiled=True),
    )
    keys_n = (
        jnp.dot(lat_all, key_weight, preferred_element_type=jnp.float32)
        .astype(jnp.bfloat16)
        .reshape(seq_total, head_dev, width_n)
    )
    values = (
        jnp.dot(lat_all, value_weight, preferred_element_type=jnp.float32)
        .astype(jnp.bfloat16)
        .reshape(seq_total, head_dev, width_n)
    )
    counter = jnp.arange(query_rows, dtype=jnp.int32)
    query_pos = (counter // tok_rows * seq_count + seq_index) * tok_rows + counter % tok_rows
    key_pos = jnp.arange(seq_total, dtype=jnp.int32)
    table_ids = jnp.arange(block_total, dtype=jnp.int32)

    def lookup(positions, table):
        hit = (positions // block_len)[:, None] == table_ids[None, :]
        return jnp.sum(jnp.where(hit, table[None, :], 0), axis=1)

    query_doc = lookup(query_pos, block_doc[0])
    query_img = lookup(query_pos, block_image[0])
    query_flag = lookup(query_pos, block_flag[0])
    key_doc = lookup(key_pos, block_doc[0])
    key_img = lookup(key_pos, block_image[0])
    key_flag = lookup(key_pos, block_flag[0])
    key_span = math.gcd(seq_total, 512)
    span_count = seq_total // key_span

    def key_tile(step_index):
        offset = step_index * key_span
        kn_blk = lax.dynamic_slice_in_dim(keys_n, offset, key_span, 0)
        val_blk = lax.dynamic_slice_in_dim(values, offset, key_span, 0)
        kr_blk = lax.dynamic_slice_in_dim(rope_keys, offset, key_span, 0)
        doc_blk = lax.dynamic_slice_in_dim(key_doc, offset, key_span, 0)
        img_blk = lax.dynamic_slice_in_dim(key_img, offset, key_span, 0)
        flag_blk = lax.dynamic_slice_in_dim(key_flag, offset, key_span, 0)
        pos_blk = lax.dynamic_slice_in_dim(key_pos, offset, key_span, 0)
        scores = (
            jnp.einsum("qhd,khd->hqk", query_n, kn_blk, preferred_element_type=jnp.float32)
            + jnp.einsum("qhd,kd->hqk", query_r, kr_blk, preferred_element_type=jnp.float32)
        ) * score_scale
        bidir = (
            (query_flag[:, None] == 1)
            & (flag_blk[None, :] == 1)
            & (query_img[:, None] == img_blk[None, :])
        )
        allowed = (query_doc[:, None] == doc_blk[None, :]) & (
            (pos_blk[None, :] <= query_pos[:, None]) | bidir
        )
        return (scores, allowed[None], kn_blk, val_blk, kr_blk)

    steps_all = jnp.arange(span_count, dtype=jnp.int32)

    def max_step(carry, step_index):
        run_max, run_sum = carry
        scores, allowed, kn_blk, val_blk, kr_blk = key_tile(step_index)
        new_max = jnp.maximum(run_max, jnp.max(jnp.where(allowed, scores, NEG), axis=2))
        run_sum = run_sum * jnp.exp(run_max - new_max) + jnp.sum(
            jnp.where(allowed, jnp.exp(scores - new_max[:, :, None]), 0.0), axis=2
        )
        return ((new_max, run_sum), None)

    start_max = jnp.full((head_dev, query_rows), NEG, jnp.float32)
    (run_max, run_sum), unused = lax.scan(
        max_step, (start_max, jnp.zeros((head_dev, query_rows), jnp.float32)), steps_all
    )
    log_total = run_max + jnp.log(run_sum)

    def probs_of(scores, allowed):
        probs = jnp.where(allowed, jnp.exp(scores - log_total[:, :, None]), 0.0)
        return (probs, probs.astype(jnp.bfloat16))

    def out_step(output, step_index):
        scores, allowed, kn_blk, val_blk, kr_blk = key_tile(step_index)
        probs, probs_b = probs_of(scores, allowed)
        return (
            output
            + jnp.einsum("hqk,khd->qhd", probs_b, val_blk, preferred_element_type=jnp.float32),
            None,
        )

    output, unused = lax.scan(
        out_step, jnp.zeros((query_rows, head_dev, width_n), jnp.float32), steps_all
    )
    row_delta = jnp.sum(grad_o.astype(jnp.float32) * output, axis=2).T

    def grad_step(carry, step_index):
        qn_acc, qr_acc = carry
        scores, allowed, kn_blk, val_blk, kr_blk = key_tile(step_index)
        probs, probs_b = probs_of(scores, allowed)
        grad_probs = jnp.einsum("qhd,khd->hqk", grad_o, val_blk, preferred_element_type=jnp.float32)
        score_grad = (score_scale * probs * (grad_probs - row_delta[:, :, None])).astype(
            jnp.bfloat16
        )
        vg_blk = jnp.einsum("hqk,qhd->khd", probs_b, grad_o, preferred_element_type=jnp.float32)
        qn_acc = qn_acc + jnp.einsum(
            "hqk,khd->qhd", score_grad, kn_blk, preferred_element_type=jnp.float32
        )
        qr_acc = qr_acc + jnp.einsum(
            "hqk,kd->qhd", score_grad, kr_blk, preferred_element_type=jnp.float32
        )
        kn_blk_grad = jnp.einsum(
            "hqk,qhd->khd", score_grad, query_n, preferred_element_type=jnp.float32
        )
        kr_blk_grad = jnp.einsum(
            "hqk,qhd->kd", score_grad, query_r, preferred_element_type=jnp.float32
        )
        return ((qn_acc, qr_acc), (kn_blk_grad, vg_blk, kr_blk_grad))

    start_grads = (
        jnp.zeros((query_rows, head_dev, width_n), jnp.float32),
        jnp.zeros((query_rows, head_dev, width_r), jnp.float32),
    )
    (qn_acc, qr_acc), (kn_grads, vg_grads, kr_grads) = lax.scan(grad_step, start_grads, steps_all)
    kn_flat = kn_grads.reshape(seq_total, head_dev * width_n)
    vg_flat = vg_grads.reshape(seq_total, head_dev * width_n)
    kr_flat = kr_grads.reshape(seq_total, width_r)
    out_back, qn_back, qr_back = (
        lax.all_to_all(output.astype(jnp.bfloat16), "ctx", split_axis=0, concat_axis=1, tiled=True),
        lax.all_to_all(qn_acc.astype(jnp.bfloat16), "ctx", split_axis=0, concat_axis=1, tiled=True),
        lax.all_to_all(qr_acc.astype(jnp.bfloat16), "ctx", split_axis=0, concat_axis=1, tiled=True),
    )
    attended = out_back.reshape(1, tok_rows, head_total * width_n)
    weight_k32 = key_weight.astype(jnp.float32)
    weight_v32 = value_weight.astype(jnp.float32)
    lat_terms = jnp.dot(kn_flat, weight_k32.T, precision=high) + jnp.dot(
        vg_flat, weight_v32.T, precision=high
    )
    lat_grad, kr_grad = (
        lax.psum_scatter(lat_terms, ("ctx", "seq"), scatter_dimension=0, tiled=True),
        lax.psum_scatter(kr_flat, ("ctx", "seq"), scatter_dimension=0, tiled=True),
    )
    lat32 = lat_all.astype(jnp.float32)
    wk_grad, wv_grad = (
        lax.psum_scatter(
            jnp.dot(lat32.T, kn_flat, precision=high),
            ("dp", "seq"),
            scatter_dimension=0,
            tiled=True,
        ),
        lax.psum_scatter(
            jnp.dot(lat32.T, vg_flat, precision=high),
            ("dp", "seq"),
            scatter_dimension=0,
            tiled=True,
        ),
    )
    return (
        attended,
        qn_back[None],
        qr_back[None],
        lat_grad.astype(jnp.bfloat16)[None],
        kr_grad.astype(jnp.bfloat16)[None],
        wk_grad,
        wv_grad,
    )


def solution(mesh):
    return jax.shard_map(
        on_device,
        mesh=mesh,
        in_specs=(
            P("dp", ("ctx", "seq"), None, None),
            P("dp", ("ctx", "seq"), None, None),
            P("dp", ("ctx", "seq"), None),
            P("dp", ("ctx", "seq"), None),
            P("dp", ("ctx", "seq"), None),
            P(None, "ctx"),
            P(None, "ctx"),
            P("dp", None),
            P("dp", None),
            P("dp", None),
        ),
        out_specs=(
            P("dp", ("ctx", "seq"), None),
            P("dp", ("ctx", "seq"), None, None),
            P("dp", ("ctx", "seq"), None, None),
            P("dp", ("ctx", "seq"), None),
            P("dp", ("ctx", "seq"), None),
            P(("dp", "seq"), "ctx"),
            P(("dp", "seq"), "ctx"),
        ),
        check_vma=False,
    )
```

profile of v0, /device:TPU:2, one launch (start us, length us, event | category | flops | bytes accessed | tf_op | source)
XLA Modules:
  0.0 857.2 jit_solution(16024788980335818229)
XLA Ops:
  9.8 5.5 all-to-all-start.1
  16.2 1.7 copy.229
  19.7 42.1 %all-gather.1 = bf16[1,2048,64]{2,0,1:T(2,128)(2,1)S(1)} all-gather(bf16[1,64,64]{2,0,1:T(2,128)(2,1)S(1)} %copy.160), channel_id=3, replica_groups=mesh['dp'=8,'ctx'=8,'seq'=4] {'ctx','seq'}, dimensions={1}, use_global_device_ids=true | all-gather | bytes 270336 | tf_op jit(solution)/shard_map/all_gather | solution.py:45
  61.8 1.7 copy.161
  63.5 7.2 all-to-all-start
  70.8 6.0 all-to-all-done
  76.8 4.8 all-to-all-start.3
  83.0 4.6 all-to-all-done.3
  87.7 2.3 convolution_convert_fusion
  92.5 39.3 %while.43 = (s32[]{:T(128)}, f32[2,512]{1,0:T(2,128)S(1)}, f32[2,512]{1,0:T(2,128)}, s32[512]{0:T(512)S(1)}, s32[4]{0:T(128)}, /*index=5*/s32[2048]{0:T(1024)}, ...) while((s32[]{:T(128)}, f32[2,512]{1,0:T(2,128)S(1)}, ...), condition=%wide.region_9.10_spmd.clone, body=%wide.region_6.9_spmd.clone.sunk | while | flops 206845952 | bytes 10015062 | solution.py:110
  92.5 1.4 dynamic_slice.155
  98.2 1.4 fusion.196
  99.6 1.5 select_reduce_fusion.10
  108.0 1.4 fusion.196
  109.4 1.5 select_reduce_fusion.10
  117.8 1.4 fusion.196
  119.2 1.5 select_reduce_fusion.10
  127.6 1.4 fusion.196
  129.0 1.5 select_reduce_fusion.10
  133.1 2.7 convolution_convert_fusion.1
  136.9 42.1 %while.44 = (s32[]{:T(128)}, f32[512,2,128]{0,2,1:T(8,128)}, s32[4]{0:T(128)}, bf16[2048,2,128]{0,2,1:T(8,128)(2,1)}, s32[512]{0:T(512)S(1)}, /*index=5*/s32[204...) while((s32[]{:T(128)}, f32[512,2,128]{0,2,1:T(8,128)}, ...), condition=%wide.region_11.12_spmd.clone, body=%wide.region_10.11_spmd.clone.sunk | while | flops 340272128 | bytes 6788896 | solution.py:128
  143.1 1.4 fusion.204
  144.5 2.9 fusion.206
  153.5 1.4 fusion.204
  154.9 3.0 fusion.206
  164.1 1.4 fusion.204
  165.5 3.0 fusion.206
  174.7 1.4 fusion.204
  176.0 3.0 fusion.206
  180.6 54.5 %while.45 = (s32[]{:T(128)}, f32[512,2,128]{0,2,1:T(8,128)S(1)}, f32[512,2,64]{0,2,1:T(8,128)}, f32[4,512,2,128]{3,2,1,0:T(2,128)}, f32[4,512,2,128]{3,2,1,0:T(2...) while((s32[]{:T(128)}, f32[512,2,128]{0,2,1:T(8,128)S(1)}, ...), condition=%wide.region_14.15_spmd.clone, body=%wide.region_13.14_spmd.clone.sunk | while | flops 879371264 | bytes 26517948 | solution.py:160
  184.8 1.4 fusion.223
  187.5 1.5 fusion.226
  189.4 1.4 fusion.227
  192.4 1.8 copy_dynamic-update-slice_fusion.3
  198.5 1.4 fusion.223
  201.1 1.5 fusion.226
  203.0 1.4 fusion.227
  206.0 1.8 copy_dynamic-update-slice_fusion.3
  212.1 1.4 fusion.223
  214.8 1.5 fusion.226
  216.6 1.4 fusion.227
  219.6 1.8 copy_dynamic-update-slice_fusion.3
  225.7 1.4 fusion.223
  228.4 1.5 fusion.226
  230.2 1.4 fusion.227
  233.2 1.8 copy_dynamic-update-slice_fusion.3
  235.1 2.5 copy.181
  237.9 1.9 fusion.99
  239.8 3.9 convolution_add_fusion
  243.8 1.5 copy-done.2
  245.3 3.4 fusion.109
  249.8 4.3 fusion.114
  254.2 2.1 copy.192
  257.4 4.7 all-to-all-start.5
  263.1 3.8 all-to-all-done.5
  266.8 4.8 all-to-all-start.2
  272.5 5.2 all-to-all-done.2
  277.7 4.8 all-to-all-start.4
  284.8 3.8 all-to-all-done.4
  289.5 34.3 %reduce-scatter.11.cloned.1.call-done = f32[64,64]{1,0:T(8,128)} async-done(((f32[2048,64]{1,0:T(8,128)}), f32[64,64]{1,0:T(8,128)}) %reduce-scatter.11.cloned.1.call-update) | async-done | bytes 16400 | tf_op jit(solution)/shard_map/reduce_scatter | solution.py:177
  325.2 92.1 %reduce-scatter.9.cloned.1.call-done = f32[64,512]{1,0:T(8,128)} async-done(((f32[2048,512]{1,0:T(8,128)}), f32[64,512]{1,0:T(8,128)}) %reduce-scatter.9.cloned.1.call-update) | async-done | bytes 131088 | tf_op jit(solution)/shard_map/reduce_scatter | solution.py:176
  417.3 1.5 convert_bitcast_fusion
  418.8 215.6 %reduce-scatter.13.cloned.1.call-done = f32[16,256]{1,0:T(8,128)} async-done(((f32[512,256]{1,0:T(8,128)}), f32[16,256]{1,0:T(8,128)}) %reduce-scatter.13.cloned.1.call-update) | async-done | bytes 16400
  634.4 216.2 %reduce-scatter.15.cloned.1.call-done = f32[16,256]{1,0:T(8,128)} async-done(((f32[512,256]{1,0:T(8,128)}), f32[16,256]{1,0:T(8,128)}) %reduce-scatter.15.cloned.1.call-update) | async-done | bytes 16400
  (245 shorter events, 94.4 us)
Async XLA Ops:
  7.2 80.5 %copy-start = (bf16[512,256]{1,0:T(8,128)(2,1)S(1)}, bf16[512,256]{1,0:T(8,128)(2,1)}, u32[]{:S(2)}) copy-start(bf16[512,256]{1,0:T(8,128)(2,1)} %param.21) | copy-start | bytes 786436
  7.2 80.5 %all-gather.4.cloned.1.call-start = ((), (), s32[]{:S(2)}) async-start(), calls=%async_computation.12 | async-start | bytes 2162688 | tf_op jit(solution)/shard_map/all_gather | solution.py:44
  9.8 53.7 %all-to-all-start.1 = ((bf16[8,2,4096]{2,1,0:T(2,128)(2,1)}), bf16[8,2,4096]{2,1,0:T(2,128)(2,1)S(1)}, u32[]{:S(2)}, u32[]{:S(2)}) async-start(bf16[8,2,4096]{2,1,0:T(2,128)(2,1)} %reshape.464), calls=%async_computation.1 | async-start | bytes 262144 | tf_op jit(solution)/shard_map/all_to_all | solution.py:39
  17.9 52.8 %copy-start.14 = (s32[1,32]{1,0:T(1,128)S(1)}, s32[1,32]{1,0:T(1,128)}, u32[]{:S(2)}) copy-start(s32[1,32]{1,0:T(1,128)} %param.24) | copy-start | bytes 388
  17.9 52.8 %copy-start.15 = (s32[1,32]{1,0:T(1,128)S(1)}, s32[1,32]{1,0:T(1,128)}, u32[]{:S(2)}) copy-start(s32[1,32]{1,0:T(1,128)} %param.25) | copy-start | bytes 388
  17.9 52.8 %copy-start.16 = (s32[1,32]{1,0:T(1,128)S(1)}, s32[1,32]{1,0:T(1,128)}, u32[]{:S(2)}) copy-start(s32[1,32]{1,0:T(1,128)} %param.23) | copy-start | bytes 388
  63.5 13.3 %all-to-all-start = ((bf16[64,16,128]{2,0,1:T(8,128)(2,1)}), bf16[64,16,128]{2,0,1:T(8,128)(2,1)S(1)}, u32[]{:S(2)}, u32[]{:S(2)}) async-start(bf16[64,16,128]{2,0,1:T(8,128)(2,1)} %bitcast.196), calls=%async_computation | async-start | bytes 524288 | tf_op jit(solution)/shard_map/all_to_all | solution.py:38
  76.8 10.9 %all-to-all-start.3 = ((bf16[64,16,128]{2,0,1:T(8,128)(2,1)}), bf16[64,16,128]{2,0,1:T(8,128)(2,1)S(1)}, u32[]{:S(2)}, u32[]{:S(2)}) async-start(bf16[64,16,128]{2,0,1:T(8,128)(2,1)} %copy.169), calls=%async_computation.3 | async-start | bytes 524288 | tf_op jit(solution)/shard_map/all_to_all | solution.py:40
  81.5 242.3 %reduce-scatter.11.cloned.1.call-start = ((), (), s32[]{:S(2)}) async-start(), calls=%async_computation.11 | async-start | bytes 1081344 | tf_op jit(solution)/shard_map/reduce_scatter | solution.py:177
  92.5 40.6 %copy-start.1 = (bf16[1,2048,512]{2,1,0:T(8,128)(2,1)S(1)}, bf16[1,2048,512]{2,1,0:T(8,128)(2,1)}, u32[]{:S(2)}) copy-start(bf16[1,2048,512]{2,1,0:T(8,128)(2,1)} %all-gather.4.cloned.1.call-done) | copy-start | bytes 6291460
  101.1 0.7 copy-start.11
  101.8 0.6 copy-start.12
  110.9 0.7 copy-start.11
  111.6 0.6 copy-start.12
  120.7 0.7 copy-start.11
  121.4 0.6 copy-start.12
  130.5 0.7 copy-start.11
  131.2 0.6 copy-start.12
  133.1 3.8 copy-start.13
  180.6 5.7 copy-start.8
  187.5 1.6 copy-start.3
  189.4 3.0 copy-start.4
  194.2 5.7 copy-start.8
  201.1 1.6 copy-start.3
  203.0 3.0 copy-start.4
  207.8 5.7 copy-start.8
  214.8 1.6 copy-start.3
  216.6 3.0 copy-start.4
  221.4 5.7 copy-start.8
  228.3 1.5 copy-start.3
  230.2 3.0 copy-start.4
  235.1 2.8 copy-start.6
  237.6 179.7 %reduce-scatter.9.cloned.1.call-start = ((), (), s32[]{:S(2)}) async-start(), calls=%async_computation.10 | async-start | bytes 4325376 | tf_op jit(solution)/shard_map/reduce_scatter | solution.py:176
  237.8 1.9 copy-start.7
  237.8 1.9 copy-start.10
  243.7 1.6 copy-start.2
  243.8 390.6 %reduce-scatter.13.cloned.1.call-start = ((), (), s32[]{:S(2)}) async-start(), calls=%async_computation.13 | async-start | bytes 540672
  249.8 6.5 copy-start.5
  249.8 600.8 %reduce-scatter.15.cloned.1.call-start = ((), (), s32[]{:S(2)}) async-start(), calls=%async_computation.14 | async-start | bytes 540672
  254.2 8.0 copy-start.9
  257.4 9.4 %all-to-all-start.5 = ((bf16[8,2,4096]{2,1,0:T(2,128)(2,1)}), bf16[8,2,4096]{2,1,0:T(2,128)(2,1)S(1)}, u32[]{:S(2)}, u32[]{:S(2)}) async-start(bf16[8,2,4096]{2,1,0:T(2,128)(2,1)} %reshape.466), calls=%async_computation.5 | async-start | bytes 262144 | tf_op jit(solution)/shard_map/all_to_all | solution.py:167
  266.8 10.9 %all-to-all-start.2 = ((bf16[512,2,128]{2,1,0:T(2,128)(2,1)}), bf16[512,2,128]{2,1,0:T(2,128)(2,1)S(1)}, u32[]{:S(2)}, u32[]{:S(2)}) async-start(bf16[512,2,128]{2,1,0:T(2,128)(2,1)} %copy.166), calls=%async_computation.2 | async-start | bytes 524288 | tf_op jit(solution)/shard_map/all_to_all | solution.py:165
  277.7 10.9 %all-to-all-start.4 = ((bf16[512,2,128]{2,1,0:T(2,128)(2,1)}), bf16[512,2,128]{2,1,0:T(2,128)(2,1)S(1)}, u32[]{:S(2)}, u32[]{:S(2)}) async-start(bf16[512,2,128]{2,1,0:T(2,128)(2,1)} %copy.174), calls=%async_computation.4 | async-start | bytes 524288 | tf_op jit(solution)/shard_map/all_to_all | solution.py:166
Sparse Core Ops, SparseCore 0:
  10.6 51.9 all-gather.3
  237.7 86.0 reduce-scatter.10
  328.3 88.9 reduce-scatter.8
  421.5 212.8 reduce-scatter.12
  639.1 211.4 reduce-scatter.14
where the time goes:
time: 861 us; the launch traced here: 857 us
  waiting for transfers between devices  582 us (68%)
  matrix products  77.5 us (9%)
  local copies, waits for them, and re-layouts  74 us (9%)
  blocking collectives  42.1 us (5%)
  starting transfers between devices  32.1 us (4%)
  other arithmetic  26.7 us (3%)
  between operations  14.1 us (2%)
    unnamed x7, waiting for transfers between devices  433 us
    reduce_scatter x1, waiting for transfers between devices, on_device(): lax.psum_scatter(lat_terms, ('ctx', 'seq'), scatter_dimension=0, tiled=True)  92.1 us
    all_gather x1, blocking collectives, on_device(): lax.all_gather(key_rope[0], ('ctx', 'seq'), axis=0, tiled=True)  42.1 us
    reduce_scatter x1, waiting for transfers between devices, on_device(): lax.psum_scatter(kr_flat, ('ctx', 'seq'), scatter_dimension=0, tiled=True)  34.3 us
  transfers between devices with their start and end apart: 11, of which 9 were waited for; matrix products, arithmetic and copies ran while one was open for 4% of the time, Pallas kernels for 0%

commit v1 on v0

v1 whole, which is shorter than its diff:
```python
import functools
import math

import jax
import jax.numpy as jnp
from jax import lax
from jax.experimental import pallas as pl
from jax.experimental.pallas import tpu as pltpu
from jax.sharding import PartitionSpec as P

NEG = -1e30
MESH = pl.DeviceIdType.MESH
VM = pl.BlockSpec(memory_space=pltpu.VMEM)
SM = pl.BlockSpec(memory_space=pltpu.SMEM)
ANY = pl.BlockSpec(memory_space=pl.ANY)
DMA = pltpu.SemaphoreType.DMA
BF = jnp.bfloat16
F32 = jnp.float32

NX, NC, NY, NZ = 4, 2, 4, 8
NCTX = NX * NC
TOK, HEADS, HD, RD, LAT = 64, 16, 128, 64, 512
PACK = 640
NQ = NCTX * TOK
NK = NX * NC * NY * TOK
CHUNK = 256
NCH = NK // CHUNK
SCALE = 1.0 / math.sqrt(HD + RD)
SCALE2 = SCALE * math.log2(math.e)


def rc(src, dst, send, recv, dev):
    return pltpu.make_async_remote_copy(
        src_ref=src, dst_ref=dst, send_sem=send, recv_sem=recv, device_id=dev, device_id_type=MESH
    )


def enter(axes):
    barrier = pltpu.get_barrier_semaphore()
    total = 0
    for axis, size in axes:
        me = lax.axis_index(axis)
        for d in range(1, size):
            pl.semaphore_signal(
                barrier, inc=1, device_id={axis: lax.rem(me + d, size)}, device_id_type=MESH
            )
            total += 1
    return barrier, total


def gather_kernel(
    qn_ref, qr_ref, do_ref, lat_ref, kr_ref, q_all, lat_all, comb, pack,
    xs, xr, us, ur, ds, dr, fs, fr, ws, wr, qs, qrs, loc,
):
    ctx = lax.axis_index("ctx")
    y = lax.axis_index("seq")
    x = ctx // NC
    k = lax.rem(ctx, NC)
    sib = {"ctx": x * NC + 1 - k}
    up = {"seq": lax.rem(y + 1, NY)}
    down = {"seq": lax.rem(y + NY - 1, NY)}
    barrier, total = enter((("ctx", NCTX), ("seq", NY)))
    comb[:, 0:LAT] = lat_ref[0]
    comb[:, LAT : LAT + RD] = kr_ref[0]
    comb[:, LAT + RD :] = kr_ref[0]
    pl.semaphore_wait(barrier, total)
    mine = lat_all.at[x, k, y]
    sends = []

    def go(copy):
        copy.start()
        sends.append(copy)
        return copy

    xcp = []
    for d in range(1, NX):
        dev = {"ctx": lax.rem(x + d, NX) * NC + k}
        xcp.append(go(rc(comb, mine, xs.at[d - 1], xr.at[d - 1], dev)))
    ups, downs = [], []
    ups.append(go(rc(comb, mine, us.at[0], ur.at[0], up)))
    downs.append(go(rc(comb, mine, ds.at[0], dr.at[0], down)))
    swaps = [go(rc(comb, mine, ws.at[0], wr.at[0], sib))]
    own = pltpu.make_async_copy(comb, mine, loc.at[0])
    own.start()
    qn = qn_ref[0].reshape(TOK, HEADS * HD)
    qr = qr_ref[0].reshape(TOK, HEADS * RD)
    for c in range(NCTX):
        pack[c, :, 0:256] = qn[:, c * 256 : (c + 1) * 256]
        pack[c, :, 256:512] = do_ref[0, :, c * 256 : (c + 1) * 256]
        pack[c, :, 512:640] = qr[:, c * 128 : (c + 1) * 128]
    qcp = []
    for d in range(1, NCTX):
        to = lax.rem(ctx + d, NCTX)
        qcp.append(go(rc(pack.at[to], q_all.at[ctx], qs.at[d - 1], qrs.at[d - 1], {"ctx": to})))
    ownq = pltpu.make_async_copy(pack.at[ctx], q_all.at[ctx], loc.at[1])
    ownq.start()

    def at(d, yy):
        return lat_all.at[lax.rem(x + NX - d, NX), k, yy]

    for d in range(1, NX):
        xcp[d - 1].wait_recv()
        blk = at(d, y)
        ups.append(go(rc(blk, blk, us.at[d], ur.at[d], up)))
        downs.append(go(rc(blk, blk, ds.at[d], dr.at[d], down)))
        swaps.append(go(rc(blk, blk, ws.at[d], wr.at[d], sib)))
    yd, yu, yo = lax.rem(y + NY - 1, NY), lax.rem(y + 1, NY), lax.rem(y + 2, NY)
    fwd = []
    for d in range(NX):
        ups[d].wait_recv()
        blk = at(d, yd)
        if d < 2:
            fwd.append(go(rc(blk, blk, fs.at[d], fr.at[d], up)))
        swaps.append(go(rc(blk, blk, ws.at[4 + d], wr.at[4 + d], sib)))
        downs[d].wait_recv()
        blk = at(d, yu)
        if d >= 2:
            fwd.append(go(rc(blk, blk, fs.at[d], fr.at[d], down)))
        swaps.append(go(rc(blk, blk, ws.at[8 + d], wr.at[8 + d], sib)))
    for d in range(NX):
        fwd[d].wait_recv()
        blk = at(d, yo)
        swaps.append(go(rc(blk, blk, ws.at[12 + d], wr.at[12 + d], sib)))
    for copy in swaps + qcp:
        copy.wait_recv()
    for copy in sends:
        copy.wait_send()
    own.wait()
    ownq.wait()


def gather(query_nope, query_rope, out_grad, latent, key_rope):
    return pl.pallas_call(
        gather_kernel,
        out_shape=(
            jax.ShapeDtypeStruct((NCTX, TOK, PACK), BF),
            jax.ShapeDtypeStruct((NX, NC, NY, TOK, PACK), BF),
        ),
        in_specs=[VM] * 5,
        out_specs=(ANY, ANY),
        scratch_shapes=[
            pltpu.VMEM((TOK, PACK), BF),
            pltpu.VMEM((NCTX, TOK, PACK), BF),
            DMA((3,)), DMA((3,)), DMA((4,)), DMA((4,)), DMA((4,)), DMA((4,)),
            DMA((4,)), DMA((4,)), DMA((16,)), DMA((16,)), DMA((7,)), DMA((7,)), DMA((2,)),
        ],
        compiler_params=pltpu.CompilerParams(
            collective_id=0, has_side_effects=True, vmem_limit_bytes=24 * 2**20
        ),
        name="gather",
    )(query_nope, query_rope, out_grad, latent, key_rope)


def dot(a, b):
    return jnp.dot(a, b, preferred_element_type=F32)


def attend_kernel(
    doc_ref, img_ref, flag_ref, q_ref, lat_ref, wk_ref, wv_ref, oq_ref, lk_ref, wg_ref,
    w_all, w_t, lat_t, kc, kct, v, vt, qc, qct, dot_t, sc, grads, o_t, dq_t,
):
    s = lax.axis_index("seq")
    w_all[:, 0:256] = wk_ref[...]
    w_all[:, 256:512] = wv_ref[...]
    w_t[...] = w_all[...].T
    lane_k = lax.broadcasted_iota(jnp.int32, (CHUNK, 128), 1)
    row_k = lax.broadcasted_iota(jnp.int32, (128, CHUNK), 0)
    zero = jnp.zeros((), BF)
    for j in range(NCH):
        r = slice(j * CHUNK, (j + 1) * CHUNK)
        lat = lat_ref[r, 0:LAT]
        kr = lat_ref[r, LAT:PACK]
        lat_t[:, r] = lat.T
        kv = dot(lat, w_all[...]).astype(BF)
        kvt = dot(w_t[...], lat_t[:, r]).astype(BF)
        krt = kr.T
        for h in range(2):
            kc[h, r, 0:128] = kv[:, h * 128 : (h + 1) * 128]
            kc[h, r, 128:256] = jnp.where((lane_k < RD) == (h == 0), kr, zero)
            kct[h, 0:128, r] = kvt[h * 128 : (h + 1) * 128]
            kct[h, 128:256, r] = jnp.where((row_k < RD) == (h == 0), krt, zero)
            v[h, r, :] = kv[:, 256 + h * 128 : 256 + (h + 1) * 128]
            vt[h, :, r] = kvt[256 + h * 128 : 256 + (h + 1) * 128]
    for h in range(2):
        qc[h, :, 0:128] = q_ref[:, h * 128 : (h + 1) * 128]
        qc[h, :, 128:256] = q_ref[:, 512:640]
        qct[h] = qc[h].T
        dot_t[h] = q_ref[:, 256 + h * 128 : 256 + (h + 1) * 128].T

    lane_q = lax.broadcasted_iota(jnp.int32, (1, NQ), 1)
    grp = lane_q // TOK
    qdoc = jnp.zeros((1, NQ), jnp.int32)
    qcode = jnp.zeros((1, NQ), jnp.int32)
    for c in range(NCTX):
        b = 4 * c + s
        qdoc = jnp.where(grp == c, doc_ref[0, b], qdoc)
        code = jnp.where(flag_ref[0, b] == 1, doc_ref[0, b] * 64 + img_ref[0, b], -1)
        qcode = jnp.where(grp == c, code, qcode)
    qpos = (4 * grp + s) * TOK + lane_q % TOK
    sub = lax.broadcasted_iota(jnp.int32, (TOK, 1), 0)

    spans = []
    for j in range(NCH):
        lo = max(0, j - 1) // 2 * 2
        hi = min(NCTX, (min(NCTX, j + 5) + 1) // 2 * 2)
        spans.append((lo * TOK, hi * TOK))

    neg = jnp.full((1, NQ), NEG, F32)
    mx = [neg, neg]
    for j in range(NCH):
        a, b = spans[j]
        r = slice(j * CHUNK, (j + 1) * CHUNK)
        thr = []
        for i in range(CHUNK // TOK):
            kb = j * (CHUNK // TOK) + i
            kcode = jnp.where(flag_ref[0, kb] == 1, doc_ref[0, kb] * 64 + img_ref[0, kb], -2)
            t = jnp.where(qdoc[:, a:b] == doc_ref[0, kb], qpos[:, a:b] - kb * TOK, -1)
            thr.append(jnp.where(qcode[:, a:b] == kcode, NK, t))
        for h in range(2):
            raw = dot(kc[h, r, :], qct[h, :, a:b])
            part = None
            for i in range(CHUNK // TOK):
                rows = slice(i * TOK, (i + 1) * TOK)
                m = jnp.where(sub <= thr[i], raw[rows] * SCALE2, NEG)
                sc[h, j * CHUNK + i * TOK : j * CHUNK + (i + 1) * TOK, a:b] = m
                top = jnp.max(m, axis=0, keepdims=True)
                part = top if part is None else jnp.maximum(part, top)
            new = jnp.maximum(mx[h][:, a:b], part)
            pieces = [mx[h][:, 0:a]] if a else []
            pieces.append(new)
            if b < NQ:
                pieces.append(mx[h][:, b:])
            mx[h] = jnp.concatenate(pieces, axis=1) if len(pieces) > 1 else new

    tot = [jnp.zeros((1, NQ), F32)] * 2
    o_t[...] = jnp.zeros_like(o_t)
    dq_t[...] = jnp.zeros_like(dq_t)
    for j in range(NCH):
        a, b = spans[j]
        r = slice(j * CHUNK, (j + 1) * CHUNK)
        for h in range(2):
            p = jnp.exp2(sc[h, r, a:b] - mx[h][:, a:b])
            sc[h, r, a:b] = p
            new = tot[h][:, a:b] + jnp.sum(p, axis=0, keepdims=True)
            pieces = [tot[h][:, 0:a]] if a else []
            pieces.append(new)
            if b < NQ:
                pieces.append(tot[h][:, b:])
            tot[h] = jnp.concatenate(pieces, axis=1) if len(pieces) > 1 else new
            o_t[h, :, a:b] += dot(vt[h, :, r], p.astype(BF))
    inv = [1.0 / tot[h] for h in range(2)]
    delta = []
    for h in range(2):
        out = o_t[h] * inv[h]
        oq_ref[:, h * 128 : (h + 1) * 128] = out.T.astype(BF)
        delta.append(jnp.sum(out * dot_t[h].astype(F32), axis=0, keepdims=True))

    for j in range(NCH):
        a, b = spans[j]
        r = slice(j * CHUNK, (j + 1) * CHUNK)
        kr_g = []
        for h in range(2):
            p = sc[h, r, a:b] * inv[h][:, a:b]
            dp = dot(v[h, r, :], dot_t[h, :, a:b])
            ds = (p * (dp - delta[h][:, a:b])).astype(BF)
            dv = dot(p.astype(BF), q_ref[a:b, 256 + h * 128 : 256 + (h + 1) * 128])
            dk = dot(ds, qc[h, a:b, :]) * SCALE
            dq_t[h, :, a:b] += dot(kct[h, :, r], ds)
            grads[r, h * 128 : (h + 1) * 128] = dk[:, 0:128].astype(BF)
            grads[r, 256 + h * 128 : 256 + (h + 1) * 128] = dv.astype(BF)
            kr_g.append(dk[:, 128:256])
        lk_ref[r, LAT:PACK] = jnp.where(lane_k < RD, kr_g[0], kr_g[1]).astype(BF)
        lk_ref[r, 0:LAT] = dot(grads[r, :], w_t[...]).astype(BF)
    for h in range(2):
        oq_ref[:, 256 + h * 128 : 256 + (h + 1) * 128] = (dq_t[h, 0:128, :] * SCALE).T.astype(BF)
    oq_ref[:, 512:640] = ((dq_t[0, 128:256, :] + dq_t[1, 128:256, :]) * SCALE).T.astype(BF)
    for i in range(2):
        rows = slice(i * 256, (i + 1) * 256)
        wg_ref[rows, :] = dot(lat_t[rows, :], grads[...]).astype(BF)


def attend(block_doc, block_image, block_flag, q_all, lat_all, key_weight, value_weight):
    return pl.pallas_call(
        attend_kernel,
        out_shape=(
            jax.ShapeDtypeStruct((NQ, PACK), BF),
            jax.ShapeDtypeStruct((NK, PACK), BF),
            jax.ShapeDtypeStruct((LAT, 512), BF),
        ),
        in_specs=[SM] * 3 + [VM] * 4,
        out_specs=(VM, VM, VM),
        scratch_shapes=[
            pltpu.VMEM((LAT, 512), BF),
            pltpu.VMEM((512, LAT), BF),
            pltpu.VMEM((LAT, NK), BF),
            pltpu.VMEM((2, NK, 256), BF),
            pltpu.VMEM((2, 256, NK), BF),
            pltpu.VMEM((2, NK, 128), BF),
            pltpu.VMEM((2, 128, NK), BF),
            pltpu.VMEM((2, NQ, 256), BF),
            pltpu.VMEM((2, 256, NQ), BF),
            pltpu.VMEM((2, 128, NQ), BF),
            pltpu.VMEM((2, NK, NQ), F32),
            pltpu.VMEM((NK, 512), BF),
            pltpu.VMEM((2, 128, NQ), F32),
            pltpu.VMEM((2, 256, NQ), F32),
        ],
        compiler_params=pltpu.CompilerParams(vmem_limit_bytes=52 * 2**20),
        name="attend",
    )(block_doc, block_image, block_flag, q_all, lat_all, key_weight, value_weight)


def scatter_kernel(
    oq_ref, lk_ref, wg_ref, att_ref, qn_ref, qr_ref, lat_ref, kr_ref, wk_ref, wv_ref,
    oq_in, sw_in, y_out, y_in, x_out, x_in, z_in, z_out, w_in, f_own,
    qs, qrs, ss, sr, ys, yr, xs, xr, zs, zr, ws, wr,
):
    ctx = lax.axis_index("ctx")
    y = lax.axis_index("seq")
    z = lax.axis_index("dp")
    x = ctx // NC
    k = lax.rem(ctx, NC)
    sib = {"ctx": x * NC + 1 - k}
    barrier, total = enter((("ctx", NCTX), ("seq", NY), ("dp", NZ)))
    pl.semaphore_wait(barrier, total)
    sends = []

    def go(copy):
        copy.start()
        sends.append(copy)
        return copy

    swap = []
    for d in (1, 2, 3, 0):
        yy = lax.rem(y + d, NY)
        swap.append(go(rc(lk_ref.at[:, 1 - k, yy], sw_in.at[d], ss.at[d], sr.at[d], sib)))
    zc = []
    for d in range(1, NZ):
        to = lax.rem(z + d, NZ)
        zc.append(go(rc(wg_ref.at[to], z_in.at[d - 1], zs.at[d - 1], zr.at[d - 1], {"dp": to})))
    qc = []
    for d in range(1, NCTX):
        to = lax.rem(ctx + d, NCTX)
        qc.append(go(rc(oq_ref.at[to], oq_in.at[ctx], qs.at[d - 1], qrs.at[d - 1], {"ctx": to})))
    oq_in[ctx] = oq_ref[ctx]
    yc = []
    for n, d in enumerate((1, 2, 3, 0)):
        yy = lax.rem(y + d, NY)
        swap[n].wait_recv()

        def add(i, carry, d=d, yy=yy):
            y_out[d, i] = (lk_ref[i, k, yy].astype(F32) + sw_in[d, i].astype(F32)).astype(BF)
            return carry

        lax.fori_loop(0, NX, add, 0)
        if d:
            yc.append(go(rc(y_out.at[d], y_in.at[d - 1], ys.at[d - 1], yr.at[d - 1], {"seq": yy})))
    for copy in yc:
        copy.wait_recv()

    def add_y(i, carry):
        t = y_out[0, i].astype(F32)
        for d in range(NY - 1):
            t = t + y_in[d, i].astype(F32)
        x_out[i] = t.astype(BF)
        return carry

    lax.fori_loop(0, NX, add_y, 0)
    xc = []
    for d in range(1, NX):
        to = lax.rem(x + d, NX)
        xc.append(
            go(rc(x_out.at[to], x_in.at[d - 1], xs.at[d - 1], xr.at[d - 1], {"ctx": to * NC + k}))
        )
    for copy in zc:
        copy.wait_recv()
    t = wg_ref[z].astype(F32)
    for d in range(NZ - 1):
        t = t + z_in[d].astype(F32)
    z_out[...] = t.astype(BF).reshape(NY, 16, 512)
    wc = []
    for d in range(1, NY):
        to = lax.rem(y + d, NY)
        wc.append(go(rc(z_out.at[to], w_in.at[d - 1], ws.at[d - 1], wr.at[d - 1], {"seq": to})))
    for copy in qc:
        copy.wait_recv()
    for c in range(NCTX):
        att_ref[0, :, c * 256 : (c + 1) * 256] = oq_in[c, :, 0:256]
        for h in range(2):
            qn_ref[0, :, 2 * c + h, :] = oq_in[c, :, 256 + h * 128 : 256 + (h + 1) * 128]
            qr_ref[0, :, 2 * c + h, :] = oq_in[c, :, 512 + h * RD : 512 + (h + 1) * RD]
    for copy in xc:
        copy.wait_recv()
    t = x_out[x].astype(F32)
    for d in range(NX - 1):
        t = t + x_in[d].astype(F32)
    lat_ref[0] = t[:, 0:LAT].astype(BF)
    kr_ref[0] = (t[:, LAT : LAT + RD] + t[:, LAT + RD :]).astype(BF)
    for copy in wc:
        copy.wait_recv()
    t = z_out[y].astype(F32)
    for d in range(NY - 1):
        t = t + w_in[d].astype(F32)
    wk_ref[...] = t[:, 0:256]
    wv_ref[...] = t[:, 256:512]
    for copy in sends:
        copy.wait_send()


def scatter(oq, lk, wg):
    return pl.pallas_call(
        scatter_kernel,
        out_shape=(
            jax.ShapeDtypeStruct((1, TOK, HEADS * HD), BF),
            jax.ShapeDtypeStruct((1, TOK, HEADS, HD), BF),
            jax.ShapeDtypeStruct((1, TOK, HEADS, RD), BF),
            jax.ShapeDtypeStruct((1, TOK, LAT), BF),
            jax.ShapeDtypeStruct((1, TOK, RD), BF),
            jax.ShapeDtypeStruct((16, 256), F32),
            jax.ShapeDtypeStruct((16, 256), F32),
        ),
        in_specs=[VM] * 3,
        out_specs=(VM,) * 7,
        scratch_shapes=[
            pltpu.VMEM((NCTX, TOK, PACK), BF),
            pltpu.VMEM((NY, NX, TOK, PACK), BF),
            pltpu.VMEM((NY, NX, TOK, PACK), BF),
            pltpu.VMEM((NY - 1, NX, TOK, PACK), BF),
            pltpu.VMEM((NX, TOK, PACK), BF),
            pltpu.VMEM((NX - 1, TOK, PACK), BF),
            pltpu.VMEM((NZ - 1, TOK, 512), BF),
            pltpu.VMEM((NY, 16, 512), BF),
            pltpu.VMEM((NY - 1, 16, 512), BF),
            pltpu.VMEM((8, 128), F32),
            DMA((7,)), DMA((7,)), DMA((4,)), DMA((4,)), DMA((3,)), DMA((3,)),
            DMA((3,)), DMA((3,)), DMA((7,)), DMA((7,)), DMA((3,)), DMA((3,)),
        ],
        compiler_params=pltpu.CompilerParams(
            collective_id=1, has_side_effects=True, vmem_limit_bytes=40 * 2**20
        ),
        name="scatter",
    )(
        oq.reshape(NCTX, TOK, PACK),
        lk.reshape(NX, NC, NY, TOK, PACK),
        wg.reshape(NZ, LAT // NZ, 512),
    )


def on_device(
    query_nope, query_rope, latent, key_rope, out_grad,
    key_weight, value_weight, block_doc, block_image, block_flag,
):
    q_all, lat_all = gather(query_nope, query_rope, out_grad, latent, key_rope)
    oq, lk, wg = attend(
        block_doc, block_image, block_flag,
        q_all.reshape(NQ, PACK), lat_all.reshape(NK, PACK), key_weight, value_weight,
    )
    return scatter(oq, lk, wg)


def solution(mesh):
    return jax.shard_map(
        on_device,
        mesh=mesh,
        in_specs=(
            P("dp", ("ctx", "seq"), None, None),
            P("dp", ("ctx", "seq"), None, None),
            P("dp", ("ctx", "seq"), None),
            P("dp", ("ctx", "seq"), None),
            P("dp", ("ctx", "seq"), None),
            P(None, "ctx"),
            P(None, "ctx"),
            P("dp", None),
            P("dp", None),
            P("dp", None),
        ),
        out_specs=(
            P("dp", ("ctx", "seq"), None),
            P("dp", ("ctx", "seq"), None, None),
            P("dp", ("ctx", "seq"), None, None),
            P("dp", ("ctx", "seq"), None),
            P("dp", ("ctx", "seq"), None),
            P(("dp", "seq"), "ctx"),
            P(("dp", "seq"), "ctx"),
        ),
        check_vma=False,
    )
```

time: 861 us -> 87.7 us (0.10)
  the two profiles are of different devices: /device:TPU:2 before, /device:TPU:1 now
where the time goes in v1:
time: 87.7 us; the launch traced here: 87.3 us
  Pallas kernels  69.7 us (79%)
  local copies, waits for them, and re-layouts  16.9 us (19%)
    pallas_call x1, Pallas kernels, scatter(): pl.pallas_call(scatter_kernel, out_shape=(jax.ShapeDtypeStruct((1, TOK, H...  32.3 us
    pallas_call x1, Pallas kernels, gather(): pl.pallas_call(gather_kernel, out_shape=(jax.ShapeDtypeStruct((NCTX, TOK,...  23.4 us
    unnamed x33, local copies, waits for them, and re-layouts  16.9 us
    pallas_call x1, Pallas kernels, attend(): pl.pallas_call(attend_kernel, out_shape=(jax.ShapeDtypeStruct((NQ, PACK),...  14 us

profile of v1, /device:TPU:1, one launch (start us, length us, event | category | flops | bytes accessed | tf_op | source)
XLA Modules:
  0.0 87.3 jit_solution(10189482766707085694)
XLA Ops:
  0.6 0.0 copy-start.5
  0.6 0.9 %copy-done.5 = bf16[1,64,16,128]{3,2,1,0:T(8,128)(2,1)S(1)} copy-done((bf16[1,64,16,128]{3,2,1,0:T(8,128)(2,1)S(1)}, bf16[1,64,16,128]{3,2,1,0:T(8,128)(2,1)}, u32[]{:S(2)}) %copy-start.5) | copy-done | bytes 262168
  1.6 0.0 copy-start.6
  1.6 0.9 %copy-done.6 = bf16[1,64,16,64]{3,2,1,0:T(8,128)(2,1)S(1)} copy-done((bf16[1,64,16,64]{3,2,1,0:T(8,128)(2,1)S(1)}, bf16[1,64,16,64]{3,2,1,0:T(8,128)(2,1)}, u32[]{:S(2)}) %copy-start.6) | copy-done | bytes 131096
  2.5 0.0 copy-start.7
  2.5 0.9 %copy-done.7 = bf16[1,64,2048]{2,1,0:T(8,128)(2,1)S(1)} copy-done((bf16[1,64,2048]{2,1,0:T(8,128)(2,1)S(1)}, bf16[1,64,2048]{2,1,0:T(8,128)(2,1)}, u32[]{:S(2)}) %copy-start.7) | copy-done | bytes 262168
  3.5 0.0 copy-start.8
  3.5 0.8 copy-done.8
  4.3 0.0 copy-start.9
  4.3 0.7 copy-done.9
  5.0 23.4 %gather.1 = (bf16[8,64,640]{2,1,0:T(8,128)(2,1)S(1)}, bf16[4,2,4,64,640]{4,3,2,1,0:T(8,128)(2,1)S(1)}) custom-call(bf16[1,64,16,128]{3,2,1,0:T(8,128)(2,1)S(1)} %copy-done.5, bf16[1,64,16,64]{3,2,1,0:T(8,128)(2,1)S(1)} %copy-done.6, bf16[1,64,2048]{2,1,0:T(8,128)(2,1)S(1)} %copy-done.7, bf16[1,64,512]{2,1,0:T(8,128)(2,1)S(1)} %copy-done.8, ...), custom_call_target="tpu_custom_call" | custom-call | tf_op jit(solution)/shard_map/gather/pallas_call | solution.py:133
  28.4 0.0 copy-start
  28.4 1.5 %copy-done = bf16[4,2,4,64,640]{4,3,2,1,0:T(8,128)(2,1)} copy-done((bf16[4,2,4,64,640]{4,3,2,1,0:T(8,128)(2,1)}, bf16[4,2,4,64,640]{4,3,2,1,0:T(8,128)(2,1)S(1)}, u32[]{:S(2)}) %copy-start) | copy-done | bytes 2621464
  29.9 0.0 copy-start.2
  29.9 0.9 copy-done.2
  30.8 0.0 copy-start.3
  30.8 0.9 %copy-done.3 = bf16[512,256]{1,0:T(8,128)(2,1)S(1)} copy-done((bf16[512,256]{1,0:T(8,128)(2,1)S(1)}, bf16[512,256]{1,0:T(8,128)(2,1)}, u32[]{:S(2)}) %copy-start.3) | copy-done | bytes 262168
  31.7 0.0 copy-start.4
  31.7 0.9 %copy-done.4 = bf16[512,256]{1,0:T(8,128)(2,1)S(1)} copy-done((bf16[512,256]{1,0:T(8,128)(2,1)S(1)}, bf16[512,256]{1,0:T(8,128)(2,1)}, u32[]{:S(2)}) %copy-start.4) | copy-done | bytes 262168
  32.7 0.0 copy-start.10
  32.7 0.7 copy-done.10
  33.3 0.0 copy-start.11
  33.3 0.7 copy-done.11
  34.0 0.0 copy-start.12
  34.0 0.7 copy-done.12
  34.6 14.0 %attend.1 = (bf16[512,640]{1,0:T(8,128)(2,1)S(1)}, bf16[2048,640]{1,0:T(8,128)(2,1)}, bf16[512,512]{1,0:T(8,128)(2,1)S(1)}) custom-call(s32[1,32]{1,0:T(1,128)S(1)} %copy-done.10, s32[1,32]{1,0:T(1,128)S(1)} %copy-done.11, s32[1,32]{1,0:T(1,128)S(1)} %copy-done.12, bf16[512,640]{1,0:T(8,128)(2,1)} %bitcast.7, bf16[2048,640]{1,0:T(8,128)(2,1)} %bitcast.5, ...), custom_call_target="tpu_custom_call" | custom-call | tf_op jit(solution)/shard_map/attend/pallas_call | solution.py:283
  48.7 0.0 copy-start.1
  48.7 1.7 %copy-done.1 = bf16[2048,640]{1,0:T(8,128)(2,1)S(1)} copy-done((bf16[2048,640]{1,0:T(8,128)(2,1)S(1)}, bf16[2048,640]{1,0:T(8,128)(2,1)}, u32[]{:S(2)}) %copy-start.1) | copy-done | bytes 2621464
  50.4 32.3 %scatter.1 = (bf16[1,64,2048]{2,1,0:T(8,128)(2,1)S(1)}, bf16[1,64,16,128]{3,2,1,0:T(8,128)(2,1)S(1)}, bf16[1,64,16,64]{3,2,1,0:T(8,128)(2,1)S(1)}, bf16[1,64,512...) custom-call(bf16[8,64,640]{2,1,0:T(8,128)(2,1)S(1)} %bitcast.8, ...), custom_call_target="tpu_custom_call" | custom-call | tf_op jit(solution)/shard_map/scatter/pallas_call | solution.py:411
  82.7 0.7 copy.24
  83.4 0.7 copy.25
  84.1 0.7 copy.26
  84.8 0.6 copy.27
  85.5 0.6 copy.28
  86.1 0.6 copy.29
  86.7 0.6 copy.30
Async XLA Ops:
  0.6 1.0 %copy-start.5 = (bf16[1,64,16,128]{3,2,1,0:T(8,128)(2,1)S(1)}, bf16[1,64,16,128]{3,2,1,0:T(8,128)(2,1)}, u32[]{:S(2)}) copy-start(bf16[1,64,16,128]{3,2,1,0:T(8,128)(2,1)} %qn_ref.1) | copy-start | bytes 786436
  1.6 0.9 %copy-start.6 = (bf16[1,64,16,64]{3,2,1,0:T(8,128)(2,1)S(1)}, bf16[1,64,16,64]{3,2,1,0:T(8,128)(2,1)}, u32[]{:S(2)}) copy-start(bf16[1,64,16,64]{3,2,1,0:T(8,128)(2,1)} %qr_ref.1) | copy-start | bytes 393220
  2.5 0.9 %copy-start.7 = (bf16[1,64,2048]{2,1,0:T(8,128)(2,1)S(1)}, bf16[1,64,2048]{2,1,0:T(8,128)(2,1)}, u32[]{:S(2)}) copy-start(bf16[1,64,2048]{2,1,0:T(8,128)(2,1)} %do_ref.1) | copy-start | bytes 786436
  3.5 0.8 copy-start.8
  4.3 0.7 copy-start.9
  28.4 1.5 %copy-start = (bf16[4,2,4,64,640]{4,3,2,1,0:T(8,128)(2,1)}, bf16[4,2,4,64,640]{4,3,2,1,0:T(8,128)(2,1)S(1)}, u32[]{:S(2)}) copy-start(bf16[4,2,4,64,640]{4,3,2,1,0:T(8,128)(2,1)S(1)} %get-tuple-element.13) | copy-start | bytes 7864324
  29.9 0.9 copy-start.2
  30.8 0.9 %copy-start.3 = (bf16[512,256]{1,0:T(8,128)(2,1)S(1)}, bf16[512,256]{1,0:T(8,128)(2,1)}, u32[]{:S(2)}) copy-start(bf16[512,256]{1,0:T(8,128)(2,1)} %wk_ref.1) | copy-start | bytes 786436
  31.7 0.9 %copy-start.4 = (bf16[512,256]{1,0:T(8,128)(2,1)S(1)}, bf16[512,256]{1,0:T(8,128)(2,1)}, u32[]{:S(2)}) copy-start(bf16[512,256]{1,0:T(8,128)(2,1)} %wv_ref.1) | copy-start | bytes 786436
  32.7 0.7 copy-start.10
  33.3 0.7 copy-start.11
  34.0 0.7 copy-start.12
  48.7 1.7 %copy-start.1 = (bf16[2048,640]{1,0:T(8,128)(2,1)S(1)}, bf16[2048,640]{1,0:T(8,128)(2,1)}, u32[]{:S(2)}) copy-start(bf16[2048,640]{1,0:T(8,128)(2,1)} %get-tuple-element.15) | copy-start | bytes 7864324

commit v2 on v0

v2 whole, which is shorter than its diff:
```python
import math

import jax
import jax.numpy as jnp
from jax import lax
from jax.experimental import pallas as pl
from jax.experimental.pallas import tpu as pltpu
from jax.sharding import PartitionSpec as P

NEG = -1e30
MESH = pl.DeviceIdType.MESH
ANY = pl.BlockSpec(memory_space=pl.ANY)
DMA = pltpu.SemaphoreType.DMA
BF = jnp.bfloat16
F32 = jnp.float32

NX, NC, NY, NZ = 4, 2, 4, 8
NCTX = NX * NC
TOK, HEADS, HD, RD, LAT = 64, 16, 128, 64, 512
PACK = 640
NQ = NCTX * TOK
NK = NX * NC * NY * TOK
CHUNK = 256
NCH = NK // CHUNK
SCALE = 1.0 / math.sqrt(HD + RD)
SCALE2 = SCALE * math.log2(math.e)


def rc(src, dst, send, recv, dev):
    return pltpu.make_async_remote_copy(
        src_ref=src, dst_ref=dst, send_sem=send, recv_sem=recv, device_id=dev, device_id_type=MESH
    )


def dot(a, b):
    return jnp.dot(a, b, preferred_element_type=F32)


class Exchange:
    def __init__(self, src, dst, relay, ss, rs, sends):
        ctx = lax.axis_index("ctx")
        self.me = ctx
        x, k = ctx // NC, lax.rem(ctx, NC)
        self.right, self.left = lax.rem(x + 1, NX) * NC, lax.rem(x + NX - 1, NX) * NC
        self.far = lax.rem(x + 2, NX) * NC
        self.x, self.k = x * NC, k
        self.src, self.dst, self.mid = src, dst, relay
        self.ss, self.rs, self.sends = ss, rs, sends
        self.slots = {}

    def go(self, slot, src, dst, send, recv, to):
        copy = rc(src, dst, self.ss.at[send], self.rs.at[recv], {"ctx": to})
        copy.start()
        self.sends.append(copy)
        self.slots[slot] = copy

    def start_far(self):
        k = self.k
        self.go(7, self.src(self.far + k), self.mid.at[0], 5, 7, self.right + k)
        self.go(8, self.src(self.far + 1 - k), self.mid.at[1], 6, 8, self.left + k)

    def start_near(self):
        k, me = self.k, self.me
        for slot, to in (
            (1, self.right + k), (3, self.left + k),
            (2, self.right + 1 - k), (4, self.left + 1 - k),
            (0, self.x + 1 - k),
        ):
            self.go(slot, self.src(to), self.dst(me), slot, slot, to)

    def relay(self):
        k = self.k
        self.slots[7].wait_recv()
        self.go(5, self.mid.at[0], self.dst(self.left + k), 7, 5, self.right + k)
        self.slots[8].wait_recv()
        self.go(6, self.mid.at[1], self.dst(self.right + k), 8, 6, self.left + 1 - k)

    def finish(self):
        for slot in range(7):
            self.slots[slot].wait_recv()


def core_kernel(
    qn_h, qr_h, do_h, lat_h, kr_h, wk_h, wv_h, doc_h, img_h, flag_h,
    att_h, qng_h, qrg_h, latg_h, krg_h, wkg_h, wvg_h,
    att_ref, qng_ref, qrg_ref, latg_ref, krg_ref, wkg_ref, wvg_ref, rows_n, rows_r, outs,
    qn_v, qr_v, do_v, lat_v, kr_v, wk_v, wv_v, doc_ref, img_ref, flag_ref,
    comb, pack, q_all, q_mid, lat_all,
    w_all, w_t, lat_t, kc, kct, v, vt, qc, qct, dot_t, sc, gk, gv, o_t, dq_t,
    o_out, o_in, o_mid, d_out, d_in, d_mid,
    lk, sw_in, yb, y_mid, y_up, y_dn, xb, x_mid, x_up, x_dn,
    zk_out, zv_out, zk_in, zv_in, z_out, w_in,
    loc, xs, xr, us, ur, ds, dr, fs, fr, ws, wr,
    qs, qrs, os, ors, gs, grs, ss, sr, ys, yr, x2s, x2r, zks, zkr, zvs, zvr, w2s, w2r,
):
    ctx = lax.axis_index("ctx")
    y = lax.axis_index("seq")
    z = lax.axis_index("dp")
    x = ctx // NC
    k = lax.rem(ctx, NC)
    xu, xd, xo = lax.rem(x + 1, NX), lax.rem(x + NX - 1, NX), lax.rem(x + 2, NX)
    yu, yd, yo = lax.rem(y + 1, NY), lax.rem(y + NY - 1, NY), lax.rem(y + 2, NY)
    sib = {"ctx": x * NC + 1 - k}
    right, left = {"ctx": xu * NC + k}, {"ctx": xd * NC + k}
    up, down = {"seq": yu}, {"seq": yd}

    loads = []
    for n, (a, b) in enumerate((
        (lat_h, lat_v), (kr_h, kr_v), (qn_h, qn_v), (qr_h, qr_v), (do_h, do_v),
        (wk_h, wk_v), (wv_h, wv_v), (doc_h, doc_ref), (img_h, img_ref), (flag_h, flag_ref),
    )):
        loads.append(pltpu.make_async_copy(a, b, loc.at[n]))
        loads[-1].start()

    barrier = pltpu.get_barrier_semaphore()
    greet = [sib, right, left, {"ctx": xu * NC + 1 - k}, {"ctx": xd * NC + 1 - k}]
    greet += [{"seq": lax.rem(y + d, NY)} for d in range(1, NY)]
    greet += [{"dp": lax.rem(z + d, NZ)} for d in range(1, NZ)]
    for dev in greet:
        pl.semaphore_signal(barrier, inc=1, device_id=dev, device_id_type=MESH)
    loads[0].wait()
    loads[1].wait()
    comb[:, 0:LAT] = lat_v[0]
    comb[:, LAT : LAT + RD] = kr_v[0]
    comb[:, LAT + RD :] = kr_v[0]
    lat_all[x, k, y] = comb[...]
    pl.semaphore_wait(barrier, len(greet))
    sends = []

    def go(copy):
        copy.start()
        sends.append(copy)
        return copy

    mine = lat_all.at[x, k, y]
    xc = [go(rc(comb, mine, xs.at[0], xr.at[0], right)), go(rc(comb, mine, xs.at[1], xr.at[1], left))]
    ups = [go(rc(comb, mine, us.at[0], ur.at[0], up))]
    downs = [go(rc(comb, mine, ds.at[0], dr.at[0], down))]
    swaps = {0: go(rc(comb, mine, ws.at[0], wr.at[0], sib))}
    for n in range(2, 5):
        loads[n].wait()
    rows_n[...] = qn_v[0].astype(F32).reshape(TOK * HEADS, HD)
    rows_r[:, 0:RD] = qr_v[0].astype(F32).reshape(TOK * HEADS, RD)
    lane_t = lax.broadcasted_iota(jnp.int32, (TOK, 128), 1)

    def head(n):
        return pl.ds(n, TOK, stride=HEADS)

    for c in range(NCTX):
        for h in range(2):
            pack[c, :, h * 128 : (h + 1) * 128] = rows_n[head(2 * c + h), :].astype(BF)
        pack[c, :, 256:512] = do_v[0, :, c * 256 : (c + 1) * 256]
        pair = jnp.where(
            lane_t < RD, rows_r[head(2 * c), :], pltpu.roll(rows_r[head(2 * c + 1), :], RD, 1)
        )
        pack[c, :, 512:640] = pair.astype(BF)
    qx = Exchange(lambda c: pack.at[c], lambda c: q_all.at[c], q_mid, qs, qrs, sends)
    qx.start_far()

    half = TOK // 2
    blocks = (x, xd, xu, xo)

    def blk(e, yy):
        return lat_all.at[blocks[e], k, yy]

    def spread(e):
        b = blk(e, y)
        ups.append(go(rc(b, b, us.at[e], ur.at[e], up)))
        downs.append(go(rc(b, b, ds.at[e], dr.at[e], down)))
        swaps[e] = go(rc(b, b, ws.at[e], wr.at[e], sib))

    xc[0].wait_recv()
    b = lat_all.at[xd, k, y, pl.ds(0, half)]
    xc.append(go(rc(b, b, xs.at[2], xr.at[2], right)))
    xc[1].wait_recv()
    b = lat_all.at[xu, k, y, pl.ds(half, half)]
    xc.append(go(rc(b, b, xs.at[3], xr.at[3], left)))
    spread(1)
    spread(2)
    qx.start_near()
    q_all[ctx] = pack[ctx]
    for n in range(5, 7):
        loads[n].wait()
    w_all[:, 0:256] = wk_v[...]
    w_all[:, 256:512] = wv_v[...]
    w_t[...] = w_all[...].T
    xc[2].wait_recv()
    xc[3].wait_recv()
    spread(3)

    lane_k = lax.broadcasted_iota(jnp.int32, (CHUNK, 128), 1)
    row_k = lax.broadcasted_iota(jnp.int32, (128, CHUNK), 0)
    zero = jnp.zeros((), BF)

    def project(xx, kk):
        j = xx * NC + kk
        lat = lat_all[xx, kk, :, :, 0:LAT].reshape(CHUNK, LAT)
        kr = lat_all[xx, kk, :, :, LAT:PACK].reshape(CHUNK, 128)
        lt = lat.T
        lat_t[:, pl.ds(pl.multiple_of(j * CHUNK, CHUNK), CHUNK)] = lt
        kv = dot(lat, w_all[...]).astype(BF)
        kvt = dot(w_t[...], lt).astype(BF)
        krt = kr.T
        for h in range(2):
            kc[h, j, :, 0:128] = kv[:, h * 128 : (h + 1) * 128]
            kc[h, j, :, 128:256] = jnp.where((lane_k < RD) == (h == 0), kr, zero)
            kct[h, j, 0:128] = kvt[h * 128 : (h + 1) * 128]
            kct[h, j, 128:256] = jnp.where((row_k < RD) == (h == 0), krt, zero)
            v[h, j] = kv[:, 256 + h * 128 : 256 + (h + 1) * 128]
            vt[h, j] = kvt[256 + h * 128 : 256 + (h + 1) * 128]

    fwd = []
    for e in range(NX):
        ups[e].wait_recv()
        b = blk(e, yd)
        if e < 2:
            fwd.append(go(rc(b, b, fs.at[e], fr.at[e], up)))
        swaps[4 + e] = go(rc(b, b, ws.at[4 + e], wr.at[4 + e], sib))
        downs[e].wait_recv()
        b = blk(e, yu)
        if e >= 2:
            fwd.append(go(rc(b, b, fs.at[e], fr.at[e], down)))
        swaps[8 + e] = go(rc(b, b, ws.at[8 + e], wr.at[8 + e], sib))
        if e == 1:
            qx.relay()
        if e >= 2:
            n = e - 2
            fwd[n].wait_recv()
            b = blk(n, yo)
            swaps[12 + n] = go(rc(b, b, ws.at[12 + n], wr.at[12 + n], sib))
            project(blocks[n], k)
    for n in (2, 3):
        fwd[n].wait_recv()
        b = blk(n, yo)
        swaps[12 + n] = go(rc(b, b, ws.at[12 + n], wr.at[12 + n], sib))
        project(blocks[n], k)
    for e in range(NX):
        for slot in (e, 4 + e, 8 + e, 12 + e):
            swaps[slot].wait_recv()
        project(blocks[e], 1 - k)
    qx.finish()

    for h in range(2):
        for c in range(NCTX):
            r = slice(c * TOK, (c + 1) * TOK)
            qc[h, r, 0:128] = q_all[c, :, h * 128 : (h + 1) * 128]
            qc[h, r, 128:256] = q_all[c, :, 512:640]
        qct[h] = qc[h].T
        dot_t[h] = q_all[:, :, 256 + h * 128 : 256 + (h + 1) * 128].reshape(NQ, 128).T
    for n in range(7, 10):
        loads[n].wait()
    lane_q = lax.broadcasted_iota(jnp.int32, (1, NQ), 1)
    grp = lane_q // TOK
    qdoc = jnp.zeros((1, NQ), jnp.int32)
    qcode = jnp.zeros((1, NQ), jnp.int32)
    for c in range(NCTX):
        b = NY * c + y
        qdoc = jnp.where(grp == c, doc_ref[0, b], qdoc)
        code = jnp.where(flag_ref[0, b] == 1, doc_ref[0, b] * 64 + img_ref[0, b], -1)
        qcode = jnp.where(grp == c, code, qcode)
    qpos = (NY * grp + y) * TOK + lane_q % TOK
    sub = lax.broadcasted_iota(jnp.int32, (TOK, 1), 0)

    spans = []
    for j in range(NCH):
        lo = max(0, j - 1) // 2 * 2
        hi = min(NCTX, (min(NCTX, j + 5) + 1) // 2 * 2)
        spans.append((lo * TOK, hi * TOK))

    def splice(full, part, a, b):
        pieces = [full[:, 0:a]] if a else []
        pieces.append(part)
        if b < NQ:
            pieces.append(full[:, b:])
        return jnp.concatenate(pieces, axis=1) if len(pieces) > 1 else part

    neg = jnp.full((1, NQ), NEG, F32)
    mx = [neg, neg]
    for j in range(NCH):
        a, b = spans[j]
        thr = []
        for i in range(CHUNK // TOK):
            kb = j * (CHUNK // TOK) + i
            kcode = jnp.where(flag_ref[0, kb] == 1, doc_ref[0, kb] * 64 + img_ref[0, kb], -2)
            t = jnp.where(qdoc[:, a:b] == doc_ref[0, kb], qpos[:, a:b] - kb * TOK, -1)
            thr.append(jnp.where(qcode[:, a:b] == kcode, NK, t))
        for h in range(2):
            raw = dot(kc[h, j], qct[h, :, a:b])
            part = None
            for i in range(CHUNK // TOK):
                rows = slice(i * TOK, (i + 1) * TOK)
                m = jnp.where(sub <= thr[i], raw[rows] * SCALE2, NEG)
                sc[h, j * CHUNK + i * TOK : j * CHUNK + (i + 1) * TOK, a:b] = m
                top = jnp.max(m, axis=0, keepdims=True)
                part = top if part is None else jnp.maximum(part, top)
            mx[h] = splice(mx[h], jnp.maximum(mx[h][:, a:b], part), a, b)

    tot = [jnp.zeros((1, NQ), F32)] * 2
    o_t[...] = jnp.zeros_like(o_t)
    dq_t[...] = jnp.zeros_like(dq_t)
    for j in range(NCH):
        a, b = spans[j]
        r = slice(j * CHUNK, (j + 1) * CHUNK)
        for h in range(2):
            p = jnp.exp2(sc[h, r, a:b] - mx[h][:, a:b])
            sc[h, r, a:b] = p
            tot[h] = splice(tot[h], tot[h][:, a:b] + jnp.sum(p, axis=0, keepdims=True), a, b)
            o_t[h, :, a:b] += dot(vt[h, j], p.astype(BF))
    inv = [1.0 / tot[h] for h in range(2)]
    delta = []
    for h in range(2):
        out = o_t[h] * inv[h]
        o_out[:, :, h * 128 : (h + 1) * 128] = out.T.astype(BF).reshape(NCTX, TOK, 128)
        delta.append(jnp.sum(out * dot_t[h].astype(F32), axis=0, keepdims=True))
    ox = Exchange(lambda c: o_out.at[c], lambda c: o_in.at[c], o_mid, os, ors, sends)
    ox.start_far()
    ox.start_near()
    o_in[ctx] = o_out[ctx]

    for j in range(NCH):
        a, b = spans[j]
        r = slice(j * CHUNK, (j + 1) * CHUNK)
        for h in range(2):
            p = sc[h, r, a:b] * inv[h][:, a:b]
            sc[h, r, a:b] = p
            do = q_all[a // TOK : b // TOK, :, 256 + h * 128 : 256 + (h + 1) * 128].reshape(b - a, 128)
            gv[r, h * 128 : (h + 1) * 128] = dot(p.astype(BF), do).astype(BF)

    def weight_grad(buf, g):
        for i in range(2):
            part = dot(lat_t[i * 256 : (i + 1) * 256, :], g[...]).astype(BF)
            buf[i * 4 : (i + 1) * 4] = part.reshape(4, TOK, 256)

    def send_z(buf, inbox, s_sem, r_sem):
        out = []
        for d in (4, 3, 5, 2, 6, 1, 7):
            to = lax.rem(z + d, NZ)
            out.append(go(rc(buf.at[to], inbox.at[d - 1], s_sem.at[d - 1], r_sem.at[d - 1], {"dp": to})))
        return out

    weight_grad(zv_out, gv)
    zv = send_z(zv_out, zv_in, zvs, zvr)

    swc = []
    ycp = {}

    def merge(xx):
        swc[xx].wait_recv()

        def add(i, carry):
            yb[xx, i] = (lk[xx, k, i].astype(F32) + sw_in[xx, i].astype(F32)).astype(BF)
            return carry

        lax.fori_loop(0, NY, add, 0)

    lo2, hi2 = pl.ds(0, 2), pl.ds(2, 2)
    for j in range(NCH):
        a, b = spans[j]
        r = slice(j * CHUNK, (j + 1) * CHUNK)
        kr_g = []
        for h in range(2):
            dp = dot(v[h, j], dot_t[h, :, a:b])
            g = (sc[h, r, a:b] * (dp - delta[h][:, a:b])).astype(BF)
            dk = dot(g, qc[h, a:b, :]) * SCALE
            dq_t[h, :, a:b] += dot(kct[h, j], g)
            gk[r, h * 128 : (h + 1) * 128] = dk[:, 0:128].astype(BF)
            kr_g.append(dk[:, 128:256])
        xx, kk = j // NC, j % NC
        kr_part = jnp.where(lane_k < RD, kr_g[0], kr_g[1]).astype(BF)
        lk[xx, kk, :, :, LAT:PACK] = kr_part.reshape(NY, TOK, 128)
        lat_part = (dot(gk[r, :], w_t[0:256, :]) + dot(gv[r, :], w_t[256:512, :])).astype(BF)
        lk[xx, kk, :, :, 0:LAT] = lat_part.reshape(NY, TOK, LAT)
        if kk == 1:
            swc.append(go(rc(lk.at[xx, 1 - k], sw_in.at[xx], ss.at[xx], sr.at[xx], sib)))
        if j == 2:
            ox.relay()
        if j == 4:
            merge(0)
        if j == 5:
            merge(1)
            ycp[0] = go(rc(yb.at[lo2, yo], y_mid.at[0], ys.at[0], yr.at[0], up))
            ycp[1] = go(rc(yb.at[lo2, yd], y_dn.at[lo2], ys.at[1], yr.at[1], down))
    d_cols = [(dq_t[h, 0:128, :] * SCALE).T.astype(BF) for h in range(2)]
    d_cols.append(((dq_t[0, 128:256, :] + dq_t[1, 128:256, :]) * SCALE).T.astype(BF))
    for n in range(3):
        d_out[:, :, n * 128 : (n + 1) * 128] = d_cols[n].reshape(NCTX, TOK, 128)
    dx = Exchange(lambda c: d_out.at[c], lambda c: d_in.at[c], d_mid, gs, grs, sends)
    dx.start_far()
    dx.start_near()
    d_in[ctx] = d_out[ctx]
    weight_grad(zk_out, gk)
    zk = send_z(zk_out, zk_in, zks, zkr)
    merge(2)
    merge(3)
    ycp[2] = go(rc(yb.at[hi2, yo], y_mid.at[1], ys.at[2], yr.at[2], down))
    ycp[3] = go(rc(yb.at[hi2, yu], y_up.at[hi2], ys.at[3], yr.at[3], up))
    ycp[0].wait_recv()
    for i in range(2):
        yb[i, yu] = (yb[i, yu].astype(F32) + y_mid[0, i].astype(F32)).astype(BF)
    ycp[4] = go(rc(yb.at[lo2, yu], y_up.at[lo2], ys.at[4], yr.at[4], up))
    dx.relay()
    ycp[2].wait_recv()
    for i in range(2):
        yb[2 + i, yd] = (yb[2 + i, yd].astype(F32) + y_mid[1, i].astype(F32)).astype(BF)
    ycp[5] = go(rc(yb.at[hi2, yd], y_dn.at[hi2], ys.at[5], yr.at[5], down))

    ox.finish()
    results = []

    def put(n, a, b):
        results.append(pltpu.make_async_copy(a, b, outs.at[n]))
        results[-1].start()

    for c in range(NCTX):
        att_ref[0, :, c * 256 : (c + 1) * 256] = o_in[c]
    put(0, att_ref, att_h)
    for n in (1, 3, 4, 5):
        ycp[n].wait_recv()

    def total_y(i, carry):
        t = yb[i, y].astype(F32) + y_up[i].astype(F32) + y_dn[i].astype(F32)
        xb[i] = t.astype(BF)
        return carry

    lax.fori_loop(0, NX, total_y, 0)
    top, bot = pl.ds(0, half), pl.ds(half, half)
    xcp = {}
    xcp[0] = go(rc(xb.at[xo, top], x_mid.at[0], x2s.at[0], x2r.at[0], right))
    xcp[1] = go(rc(xb.at[xo, bot], x_mid.at[1], x2s.at[1], x2r.at[1], left))
    xcp[2] = go(rc(xb.at[xu, bot], x_up.at[bot], x2s.at[2], x2r.at[2], right))
    xcp[3] = go(rc(xb.at[xd, top], x_dn.at[top], x2s.at[3], x2r.at[3], left))
    for copy in zv:
        copy.wait_recv()

    def total_z(buf, inbox):
        t = buf[z].astype(F32)
        for d in range(NZ - 1):
            t = t + inbox[d].astype(F32)
        return t.astype(BF).reshape(NY, 16, 256)

    z_out[:, :, 256:512] = total_z(zv_out, zv_in)
    xcp[0].wait_recv()
    xb[xu, top] = (xb[xu, top].astype(F32) + x_mid[0].astype(F32)).astype(BF)
    xcp[4] = go(rc(xb.at[xu, top], x_up.at[top], x2s.at[4], x2r.at[4], right))
    xcp[1].wait_recv()
    xb[xd, bot] = (xb[xd, bot].astype(F32) + x_mid[1].astype(F32)).astype(BF)
    xcp[5] = go(rc(xb.at[xd, bot], x_dn.at[bot], x2s.at[5], x2r.at[5], left))
    for copy in zk:
        copy.wait_recv()
    z_out[:, :, 0:256] = total_z(zk_out, zk_in)
    wc = []
    for d in range(1, NY):
        to = lax.rem(y + d, NY)
        wc.append(go(rc(z_out.at[to], w_in.at[d - 1], w2s.at[d - 1], w2r.at[d - 1], {"seq": to})))
    dx.finish()
    for c in range(NCTX):
        for h in range(2):
            rows_n[head(2 * c + h), :] = d_in[c, :, h * 128 : (h + 1) * 128].astype(F32)
        pair = d_in[c, :, 256:384].astype(F32)
        rows_r[head(2 * c), :] = pair
        rows_r[head(2 * c + 1), :] = pltpu.roll(pair, RD, 1)
    qng_ref[0] = rows_n[...].reshape(TOK, HEADS, HD).astype(BF)
    qrg_ref[0] = rows_r[:, 0:RD].reshape(TOK, HEADS, RD).astype(BF)
    put(1, qng_ref, qng_h)
    put(2, qrg_ref, qrg_h)
    for n in range(2, 6):
        xcp[n].wait_recv()
    t = xb[x].astype(F32) + x_up[...].astype(F32) + x_dn[...].astype(F32)
    latg_ref[0] = t[:, 0:LAT].astype(BF)
    krg_ref[0] = (t[:, LAT : LAT + RD] + t[:, LAT + RD :]).astype(BF)
    put(3, latg_ref, latg_h)
    put(4, krg_ref, krg_h)
    for copy in wc:
        copy.wait_recv()
    t = z_out[y].astype(F32)
    for d in range(NY - 1):
        t = t + w_in[d].astype(F32)
    wkg_ref[...] = t[:, 0:256]
    wvg_ref[...] = t[:, 256:512]
    put(5, wkg_ref, wkg_h)
    put(6, wvg_ref, wvg_h)
    for copy in sends:
        copy.wait_send()
    for copy in results:
        copy.wait()


OUTS = (
    ((1, TOK, HEADS * HD), BF),
    ((1, TOK, HEADS, HD), BF),
    ((1, TOK, HEADS, RD), BF),
    ((1, TOK, LAT), BF),
    ((1, TOK, RD), BF),
    ((16, 256), F32),
    ((16, 256), F32),
)


def core(*args):
    def vm(*shape, dtype=BF):
        return pltpu.VMEM(shape, dtype)

    table = pltpu.SMEM((1, NX * NC * NY), jnp.int32)
    return pl.pallas_call(
        core_kernel,
        out_shape=tuple(jax.ShapeDtypeStruct(s, d) for s, d in OUTS),
        in_specs=[ANY] * 10,
        out_specs=(ANY,) * 7,
        scratch_shapes=[
            *(pltpu.VMEM(s, d) for s, d in OUTS),
            vm(TOK * HEADS, 128, dtype=F32), vm(TOK * HEADS, 128, dtype=F32), DMA((7,)),
            vm(1, TOK, HEADS, HD), vm(1, TOK, HEADS, RD), vm(1, TOK, HEADS * HD),
            vm(1, TOK, LAT), vm(1, TOK, RD), vm(LAT, 256), vm(LAT, 256),
            table, table, table,
            vm(TOK, PACK), vm(NCTX, TOK, PACK), vm(NCTX, TOK, PACK), vm(2, TOK, PACK),
            vm(NX, NC, NY, TOK, PACK),
            vm(LAT, 512), vm(512, LAT), vm(LAT, NK),
            vm(2, NCH, CHUNK, 256), vm(2, NCH, 256, CHUNK),
            vm(2, NCH, CHUNK, 128), vm(2, NCH, 128, CHUNK),
            vm(2, NQ, 256), vm(2, 256, NQ), vm(2, 128, NQ),
            vm(2, NK, NQ, dtype=F32), vm(NK, 256), vm(NK, 256),
            vm(2, 128, NQ, dtype=F32), vm(2, 256, NQ, dtype=F32),
            vm(NCTX, TOK, 256), vm(NCTX, TOK, 256), vm(2, TOK, 256),
            vm(NCTX, TOK, 384), vm(NCTX, TOK, 384), vm(2, TOK, 384),
            vm(NX, NC, NY, TOK, PACK), vm(NX, NY, TOK, PACK), vm(NX, NY, TOK, PACK),
            vm(2, 2, TOK, PACK), vm(NX, TOK, PACK), vm(NX, TOK, PACK),
            vm(NX, TOK, PACK), vm(2, TOK // 2, PACK), vm(TOK, PACK), vm(TOK, PACK),
            vm(NZ, TOK, 256), vm(NZ, TOK, 256), vm(NZ - 1, TOK, 256), vm(NZ - 1, TOK, 256),
            vm(NY, 16, 512), vm(NY - 1, 16, 512),
            DMA((10,)), DMA((4,)), DMA((4,)), DMA((4,)), DMA((4,)), DMA((4,)), DMA((4,)),
            DMA((4,)), DMA((4,)), DMA((16,)), DMA((16,)),
            DMA((9,)), DMA((9,)), DMA((9,)), DMA((9,)), DMA((9,)), DMA((9,)),
            DMA((4,)), DMA((4,)), DMA((6,)), DMA((6,)), DMA((6,)), DMA((6,)),
            DMA((7,)), DMA((7,)), DMA((7,)), DMA((7,)), DMA((3,)), DMA((3,)),
        ],
        compiler_params=pltpu.CompilerParams(
            collective_id=0, has_side_effects=True, vmem_limit_bytes=60 * 2**20
        ),
        name="core",
    )(*args)


def store_kernel(*refs):
    src, dst, mid, lsem, ssem = refs[0:7], refs[7:14], refs[14:21], refs[21], refs[22]
    reads = [pltpu.make_async_copy(src[n], mid[n], lsem.at[n]) for n in range(7)]
    writes = [pltpu.make_async_copy(mid[n], dst[n], ssem.at[n]) for n in range(7)]
    for copy in reads:
        copy.start()
    for n in range(7):
        reads[n].wait()
        writes[n].start()
    for copy in writes:
        copy.wait()


def store(*arrays):
    return pl.pallas_call(
        store_kernel,
        out_shape=tuple(jax.ShapeDtypeStruct(s, d) for s, d in OUTS),
        in_specs=[ANY] * 7,
        out_specs=(ANY,) * 7,
        scratch_shapes=[*(pltpu.VMEM(s, d) for s, d in OUTS), DMA((7,)), DMA((7,))],
        compiler_params=pltpu.CompilerParams(vmem_limit_bytes=60 * 2**20),
        name="store",
    )(*arrays)


def on_device(
    query_nope, query_rope, latent, key_rope, out_grad,
    key_weight, value_weight, block_doc, block_image, block_flag,
):
    return store(*core(
        query_nope, query_rope, out_grad, latent, key_rope,
        key_weight, value_weight, block_doc, block_image, block_flag,
    ))


def solution(mesh):
    return jax.shard_map(
        on_device,
        mesh=mesh,
        in_specs=(
            P("dp", ("ctx", "seq"), None, None),
            P("dp", ("ctx", "seq"), None, None),
            P("dp", ("ctx", "seq"), None),
            P("dp", ("ctx", "seq"), None),
            P("dp", ("ctx", "seq"), None),
            P(None, "ctx"),
            P(None, "ctx"),
            P("dp", None),
            P("dp", None),
            P("dp", None),
        ),
        out_specs=(
            P("dp", ("ctx", "seq"), None),
            P("dp", ("ctx", "seq"), None, None),
            P("dp", ("ctx", "seq"), None, None),
            P("dp", ("ctx", "seq"), None),
            P("dp", ("ctx", "seq"), None),
            P(("dp", "seq"), "ctx"),
            P(("dp", "seq"), "ctx"),
        ),
        check_vma=False,
    )
```

time: 861 us -> 66.9 us (0.08)
  waiting for transfers between devices: 582 us -> 0 us
  matrix products: 77.5 us -> 0 us
  local copies, waits for them, and re-layouts: 74 us -> 0 us
  Pallas kernels: 0 us -> 65.8 us
  blocking collectives: 42.1 us -> 0 us
  starting transfers between devices: 32.1 us -> 0 us
  other arithmetic: 26.7 us -> 0 us
  between operations: 14.1 us -> 0.8 us
    unnamed x7 -> x0, waiting for transfers between devices: 433 us -> none
    reduce_scatter x2 -> x0, waiting for transfers between devices: 126 us -> none  [the longest x1 92.1 us: on_device(): lax.psum_scatter(lat_terms, ('ctx', 'seq'), scatter_dimension=0, tiled=True)]
    dot_general x54 -> x0, matrix products: 77.5 us -> none  [the longest x12 16.7 us: key_tile(): jnp.einsum('qhd,khd->hqk', query_n, kn_blk, preferred_element_type=jnp.fl...]
    pallas_call x0 -> x2, Pallas kernels: none -> 65.8 us  [the longest x1 63.9 us: core(): pl.pallas_call(core_kernel, out_shape=tuple((jax.ShapeDtypeStruct(s, d) f...]
    all_gather x1 -> x0, blocking collectives: 42.1 us -> none  [on_device(): lax.all_gather(key_rope[0], ('ctx', 'seq'), axis=0, tiled=True)]
    dynamic_slice x48 -> x0, local copies, waits for them, and re-layouts: 36.8 us -> none  [the longest x12 12.2 us: on_device(): lax.scan(max_step, (start_max, jnp.zeros((head_dev, query_rows), jnp.floa...]
    all_to_all x6 -> x0, starting transfers between devices: 31.7 us -> none  [the longest x1 7.16 us: on_device(): lax.all_to_all(query_nope[0], 'ctx', split_axis=1, concat_axis=0, tiled=T...]
    all_to_all x6 -> x0, waiting for transfers between devices: 23.3 us -> none  [the longest x1 5.96 us: on_device(): lax.all_to_all(query_nope[0], 'ctx', split_axis=1, concat_axis=0, tiled=T...]
  transfers between devices with their start and end apart: 11 -> 0, of which waited for: 9 -> 0; matrix products, arithmetic and copies ran while one was open for 4% -> 0% of each run, Pallas kernels for 0% -> 0%
where the time goes in v2:
time: 66.9 us; the launch traced here: 66.7 us
  Pallas kernels  65.8 us (98%)
  between operations  0.8 us (1%)
    pallas_call x1, Pallas kernels, core(): pl.pallas_call(core_kernel, out_shape=tuple((jax.ShapeDtypeStruct(s, d) f...  63.9 us
    pallas_call x1, Pallas kernels, store(): pl.pallas_call(store_kernel, out_shape=tuple((jax.ShapeDtypeStruct(s, d)...  1.97 us

profile of v2, /device:TPU:2, one launch (start us, length us, event | category | flops | bytes accessed | tf_op | source)
XLA Modules:
  0.0 66.7 jit_solution(1946975556149085077)
XLA Ops:
  0.6 63.9 %core.1 = (bf16[1,64,2048]{2,1,0:T(8,128)(2,1)}, bf16[1,64,16,128]{3,2,1,0:T(8,128)(2,1)}, bf16[1,64,16,64]{3,2,1,0:T(8,128)(2,1)}, bf16[1,64,512]{2,1,0:T(8,128...) custom-call(bf16[1,64,16,128]{3,2,1,0:T(8,128)(2,1)} %qn_h.1, ...), custom_call_target="tpu_custom_call" | custom-call | tf_op jit(solution)/shard_map/core/pallas_call | solution.py:504
  64.5 2.0 %store.1 = (bf16[1,64,2048]{2,1,0:T(8,128)(2,1)}, bf16[1,64,16,128]{3,2,1,0:T(8,128)(2,1)}, bf16[1,64,16,64]{3,2,1,0:T(8,128)(2,1)}, bf16[1,64,512]{2,1,0:T(8,12...) custom-call(bf16[1,64,2048]{2,1,0:T(8,128)(2,1)} %get-tuple-element.14.refs_0_, ...), custom_call_target="tpu_custom_call" | custom-call | tf_op jit(solution)/shard_map/store/pallas_call | solution.py:557

commit v3 on v2

--- a/solution.py
+++ b/solution.py
@@ -86,12 +86,13 @@
     att_ref, qng_ref, qrg_ref, latg_ref, krg_ref, wkg_ref, wvg_ref, rows_n, rows_r, outs,
     qn_v, qr_v, do_v, lat_v, kr_v, wk_v, wv_v, doc_ref, img_ref, flag_ref,
     comb, pack, q_all, q_mid, lat_all,
-    w_all, w_t, lat_t, kc, kct, v, vt, qc, qct, dot_t, sc, gk, gv, o_t, dq_t,
+    w_all, w_t, lat_t, kc, kct, v, vt, qc, qct, dot_t, sc, pb, mj, gs_b, gk, gv, o_t, dq_t,
     o_out, o_in, o_mid, d_out, d_in, d_mid,
     lk, sw_in, yb, y_mid, y_up, y_dn, xb, x_mid, x_up, x_dn,
     zk_out, zv_out, zk_in, zv_in, z_out, w_in,
     loc, xs, xr, us, ur, ds, dr, fs, fr, ws, wr,
-    qs, qrs, os, ors, gs, grs, ss, sr, ys, yr, x2s, x2r, zks, zkr, zvs, zvr, w2s, w2r,
+    qs, qrs, os, ors, gs, grs, ss, sr, ys, yr, x2s, x2r,
+    zks, zkr, zvs, zvr, w2s, w2r,
 ):
     ctx = lax.axis_index("ctx")
     y = lax.axis_index("seq")
@@ -113,7 +114,7 @@
         loads[-1].start()
 
     barrier = pltpu.get_barrier_semaphore()
-    greet = [sib, right, left, {"ctx": xu * NC + 1 - k}, {"ctx": xd * NC + 1 - k}]
+    greet = [{"ctx": lax.rem(ctx + d, NCTX)} for d in range(1, NCTX)]
     greet += [{"seq": lax.rem(y + d, NY)} for d in range(1, NY)]
     greet += [{"dp": lax.rem(z + d, NZ)} for d in range(1, NZ)]
     for dev in greet:
@@ -124,19 +125,6 @@
     comb[:, LAT : LAT + RD] = kr_v[0]
     comb[:, LAT + RD :] = kr_v[0]
     lat_all[x, k, y] = comb[...]
-    pl.semaphore_wait(barrier, len(greet))
-    sends = []
-
-    def go(copy):
-        copy.start()
-        sends.append(copy)
-        return copy
-
-    mine = lat_all.at[x, k, y]
-    xc = [go(rc(comb, mine, xs.at[0], xr.at[0], right)), go(rc(comb, mine, xs.at[1], xr.at[1], left))]
-    ups = [go(rc(comb, mine, us.at[0], ur.at[0], up))]
-    downs = [go(rc(comb, mine, ds.at[0], dr.at[0], down))]
-    swaps = {0: go(rc(comb, mine, ws.at[0], wr.at[0], sib))}
     for n in range(2, 5):
         loads[n].wait()
     rows_n[...] = qn_v[0].astype(F32).reshape(TOK * HEADS, HD)
@@ -154,43 +142,78 @@
             lane_t < RD, rows_r[head(2 * c), :], pltpu.roll(rows_r[head(2 * c + 1), :], RD, 1)
         )
         pack[c, :, 512:640] = pair.astype(BF)
+    q_all[ctx] = pack[ctx]
+    for n in range(5, 10):
+        loads[n].wait()
+    w_all[:, 0:256] = wk_v[...]
+    w_all[:, 256:512] = wv_v[...]
+    w_t[...] = w_all[...].T
+    o_t[...] = jnp.zeros_like(o_t)
+    dq_t[...] = jnp.zeros_like(dq_t)
+
+    lane_q = lax.broadcasted_iota(jnp.int32, (1, NQ), 1)
+    grp = lane_q // TOK
+    qdoc = jnp.zeros((1, NQ), jnp.int32)
+    qcode = jnp.zeros((1, NQ), jnp.int32)
+    for c in range(NCTX):
+        b = NY * c + y
+        qdoc = jnp.where(grp == c, doc_ref[0, b], qdoc)
+        code = jnp.where(flag_ref[0, b] == 1, doc_ref[0, b] * 64 + img_ref[0, b], -1)
+        qcode = jnp.where(grp == c, code, qcode)
+    qpos = (NY * grp + y) * TOK + lane_q % TOK
+    sub = lax.broadcasted_iota(jnp.int32, (TOK, 1), 0)
+    lane_k = lax.broadcasted_iota(jnp.int32, (CHUNK, 128), 1)
+    row_k = lax.broadcasted_iota(jnp.int32, (128, CHUNK), 0)
+    zero = jnp.zeros((), BF)
+
+    pl.semaphore_wait(barrier, len(greet))
+    sends = []
+
+    def go(copy):
+        copy.start()
+        sends.append(copy)
+        return copy
+
+    mine = lat_all.at[x, k, y]
+    xc = [go(rc(comb, mine, xs.at[0], xr.at[0], right)), go(rc(comb, mine, xs.at[1], xr.at[1], left))]
+    ups = [go(rc(comb, mine, us.at[0], ur.at[0], up))]
+    downs = [go(rc(comb, mine, ds.at[0], dr.at[0], down))]
+    swaps = {0: go(rc(comb, mine, ws.at[0], wr.at[0], sib))}
     qx = Exchange(lambda c: pack.at[c], lambda c: q_all.at[c], q_mid, qs, qrs, sends)
     qx.start_far()
-
     half = TOK // 2
+    top_r, bot_r = pl.ds(0, half), pl.ds(half, half)
     blocks = (x, xd, xu, xo)
 
     def blk(e, yy):
         return lat_all.at[blocks[e], k, yy]
+
+    def swap(slot, b):
+        swaps[slot] = go(rc(b, b, ws.at[slot], wr.at[slot], sib))
 
     def spread(e):
         b = blk(e, y)
         ups.append(go(rc(b, b, us.at[e], ur.at[e], up)))
         downs.append(go(rc(b, b, ds.at[e], dr.at[e], down)))
-        swaps[e] = go(rc(b, b, ws.at[e], wr.at[e], sib))
-
-    xc[0].wait_recv()
-    b = lat_all.at[xd, k, y, pl.ds(0, half)]
-    xc.append(go(rc(b, b, xs.at[2], xr.at[2], right)))
-    xc[1].wait_recv()
-    b = lat_all.at[xu, k, y, pl.ds(half, half)]
-    xc.append(go(rc(b, b, xs.at[3], xr.at[3], left)))
-    spread(1)
-    spread(2)
-    qx.start_near()
-    q_all[ctx] = pack[ctx]
-    for n in range(5, 7):
-        loads[n].wait()
-    w_all[:, 0:256] = wk_v[...]
-    w_all[:, 256:512] = wv_v[...]
-    w_t[...] = w_all[...].T
-    xc[2].wait_recv()
-    xc[3].wait_recv()
-    spread(3)
-
-    lane_k = lax.broadcasted_iota(jnp.int32, (CHUNK, 128), 1)
-    row_k = lax.broadcasted_iota(jnp.int32, (128, CHUNK), 0)
-    zero = jnp.zeros((), BF)
+        swap(e, b)
+
+    fwd = []
+
+    def onward(e):
+        ups[e].wait_recv()
+        b = blk(e, yd)
+        if e < 2:
+            fwd.append(go(rc(b, b, fs.at[e], fr.at[e], up)))
+        swap(4 + e, b)
+        downs[e].wait_recv()
+        b = blk(e, yu)
+        if e >= 2:
+            fwd.append(go(rc(b, b, fs.at[e], fr.at[e], down)))
+        swap(8 + e, b)
+
+    def last(e):
+        fwd[e].wait_recv()
+        swap(12 + e, blk(e, yo))
 
     def project(xx, kk):
         j = xx * NC + kk
@@ -209,103 +232,91 @@
             v[h, j] = kv[:, 256 + h * 128 : 256 + (h + 1) * 128]
             vt[h, j] = kvt[256 + h * 128 : 256 + (h + 1) * 128]
 
-    fwd = []
-    for e in range(NX):
-        ups[e].wait_recv()
-        b = blk(e, yd)
-        if e < 2:
-            fwd.append(go(rc(b, b, fs.at[e], fr.at[e], up)))
-        swaps[4 + e] = go(rc(b, b, ws.at[4 + e], wr.at[4 + e], sib))
-        downs[e].wait_recv()
-        b = blk(e, yu)
-        if e >= 2:
-            fwd.append(go(rc(b, b, fs.at[e], fr.at[e], down)))
-        swaps[8 + e] = go(rc(b, b, ws.at[8 + e], wr.at[8 + e], sib))
-        if e == 1:
-            qx.relay()
-        if e >= 2:
-            n = e - 2
-            fwd[n].wait_recv()
-            b = blk(n, yo)
-            swaps[12 + n] = go(rc(b, b, ws.at[12 + n], wr.at[12 + n], sib))
-            project(blocks[n], k)
-    for n in (2, 3):
-        fwd[n].wait_recv()
-        b = blk(n, yo)
-        swaps[12 + n] = go(rc(b, b, ws.at[12 + n], wr.at[12 + n], sib))
-        project(blocks[n], k)
+    def queries():
+        qx.finish()
+        for h in range(2):
+            for c in range(NCTX):
+                r = slice(c * TOK, (c + 1) * TOK)
+                qc[h, r, 0:128] = q_all[c, :, h * 128 : (h + 1) * 128]
+                qc[h, r, 128:256] = q_all[c, :, 512:640]
+            qct[h] = qc[h].T
+            dot_t[h] = q_all[:, :, 256 + h * 128 : 256 + (h + 1) * 128].reshape(NQ, 128).T
+
+    neg = jnp.full((1, NQ), NEG, F32)
+    mx = [neg, neg]
+    tot = [jnp.zeros((1, NQ), F32)] * 2
+
+    def soften(xx, kk):
+        j = xx * NC + kk
+        thr = []
+        for i in range(CHUNK // TOK):
+            kb = j * (CHUNK // TOK) + i
+            kcode = jnp.where(flag_ref[0, kb] == 1, doc_ref[0, kb] * 64 + img_ref[0, kb], -2)
+            t = jnp.where(qdoc == doc_ref[0, kb], qpos - kb * TOK, -1)
+            thr.append(jnp.where(qcode == kcode, NK, t))
+        for h in range(2):
+            raw = dot(kc[h, j], qct[h])
+            top = None
+            masked = []
+            for i in range(CHUNK // TOK):
+                m = jnp.where(sub <= thr[i], raw[i * TOK : (i + 1) * TOK] * SCALE2, NEG)
+                masked.append(m)
+                one = jnp.max(m, axis=0, keepdims=True)
+                top = one if top is None else jnp.maximum(top, one)
+            part = None
+            for i in range(CHUNK // TOK):
+                p = jnp.exp2(masked[i] - top)
+                sc[h, j, i * TOK : (i + 1) * TOK, :] = p
+                pb[h, i * TOK : (i + 1) * TOK, :] = p.astype(BF)
+                one = jnp.sum(p, axis=0, keepdims=True)
+                part = one if part is None else part + one
+            mj[h, j] = top
+            new = jnp.maximum(mx[h], top)
+            old_f, new_f = jnp.exp2(mx[h] - new), jnp.exp2(top - new)
+            o_t[h] = o_t[h] * old_f + dot(vt[h, j], pb[h]) * new_f
+            tot[h] = tot[h] * old_f + part * new_f
+            mx[h] = new
+
+    xc[0].wait_recv()
+    b = lat_all.at[xd, k, y, top_r]
+    xc.append(go(rc(b, b, xs.at[2], xr.at[2], right)))
+    xc[1].wait_recv()
+    b = lat_all.at[xu, k, y, bot_r]
+    xc.append(go(rc(b, b, xs.at[3], xr.at[3], left)))
+    spread(1)
+    spread(2)
+    qx.start_near()
+    onward(0)
+    xc[2].wait_recv()
+    xc[3].wait_recv()
+    spread(3)
+    qx.relay()
+    onward(1)
+    last(0)
+    project(blocks[0], k)
+    onward(2)
+    onward(3)
+    last(1)
+    project(blocks[1], k)
+    queries()
+    soften(blocks[0], k)
+    last(2)
+    last(3)
+    soften(blocks[1], k)
+    for e in (2, 3):
+        project(blocks[e], k)
+        soften(blocks[e], k)
     for e in range(NX):
         for slot in (e, 4 + e, 8 + e, 12 + e):
             swaps[slot].wait_recv()
         project(blocks[e], 1 - k)
-    qx.finish()
-
-    for h in range(2):
-        for c in range(NCTX):
-            r = slice(c * TOK, (c + 1) * TOK)
-            qc[h, r, 0:128] = q_all[c, :, h * 128 : (h + 1) * 128]
-            qc[h, r, 128:256] = q_all[c, :, 512:640]
-        qct[h] = qc[h].T
-        dot_t[h] = q_all[:, :, 256 + h * 128 : 256 + (h + 1) * 128].reshape(NQ, 128).T
-    for n in range(7, 10):
-        loads[n].wait()
-    lane_q = lax.broadcasted_iota(jnp.int32, (1, NQ), 1)
-    grp = lane_q // TOK
-    qdoc = jnp.zeros((1, NQ), jnp.int32)
-    qcode = jnp.zeros((1, NQ), jnp.int32)
-    for c in range(NCTX):
-        b = NY * c + y
-        qdoc = jnp.where(grp == c, doc_ref[0, b], qdoc)
-        code = jnp.where(flag_ref[0, b] == 1, doc_ref[0, b] * 64 + img_ref[0, b], -1)
-        qcode = jnp.where(grp == c, code, qcode)
-    qpos = (NY * grp + y) * TOK + lane_q % TOK
-    sub = lax.broadcasted_iota(jnp.int32, (TOK, 1), 0)
+        soften(blocks[e], 1 - k)
 
     spans = []
     for j in range(NCH):
         lo = max(0, j - 1) // 2 * 2
         hi = min(NCTX, (min(NCTX, j + 5) + 1) // 2 * 2)
         spans.append((lo * TOK, hi * TOK))
-
-    def splice(full, part, a, b):
-        pieces = [full[:, 0:a]] if a else []
-        pieces.append(part)
-        if b < NQ:
-            pieces.append(full[:, b:])
-        return jnp.concatenate(pieces, axis=1) if len(pieces) > 1 else part
-
-    neg = jnp.full((1, NQ), NEG, F32)
-    mx = [neg, neg]
-    for j in range(NCH):
-        a, b = spans[j]
-        thr = []
-        for i in range(CHUNK // TOK):
-            kb = j * (CHUNK // TOK) + i
-            kcode = jnp.where(flag_ref[0, kb] == 1, doc_ref[0, kb] * 64 + img_ref[0, kb], -2)
-            t = jnp.where(qdoc[:, a:b] == doc_ref[0, kb], qpos[:, a:b] - kb * TOK, -1)
-            thr.append(jnp.where(qcode[:, a:b] == kcode, NK, t))
-        for h in range(2):
-            raw = dot(kc[h, j], qct[h, :, a:b])
-            part = None
-            for i in range(CHUNK // TOK):
-                rows = slice(i * TOK, (i + 1) * TOK)
-                m = jnp.where(sub <= thr[i], raw[rows] * SCALE2, NEG)
-                sc[h, j * CHUNK + i * TOK : j * CHUNK + (i + 1) * TOK, a:b] = m
-                top = jnp.max(m, axis=0, keepdims=True)
-                part = top if part is None else jnp.maximum(part, top)
-            mx[h] = splice(mx[h], jnp.maximum(mx[h][:, a:b], part), a, b)
-
-    tot = [jnp.zeros((1, NQ), F32)] * 2
-    o_t[...] = jnp.zeros_like(o_t)
-    dq_t[...] = jnp.zeros_like(dq_t)
-    for j in range(NCH):
-        a, b = spans[j]
-        r = slice(j * CHUNK, (j + 1) * CHUNK)
-        for h in range(2):
-            p = jnp.exp2(sc[h, r, a:b] - mx[h][:, a:b])
-            sc[h, r, a:b] = p
-            tot[h] = splice(tot[h], tot[h][:, a:b] + jnp.sum(p, axis=0, keepdims=True), a, b)
-            o_t[h, :, a:b] += dot(vt[h, j], p.astype(BF))
     inv = [1.0 / tot[h] for h in range(2)]
     delta = []
     for h in range(2):
@@ -321,10 +332,23 @@
         a, b = spans[j]
         r = slice(j * CHUNK, (j + 1) * CHUNK)
         for h in range(2):
-            p = sc[h, r, a:b] * inv[h][:, a:b]
-            sc[h, r, a:b] = p
+            f = jnp.exp2(mj[h, j] - mx[h]) * inv[h]
+            p = sc[h, j, :, a:b] * f[:, a:b]
             do = q_all[a // TOK : b // TOK, :, 256 + h * 128 : 256 + (h + 1) * 128].reshape(b - a, 128)
             gv[r, h * 128 : (h + 1) * 128] = dot(p.astype(BF), do).astype(BF)
+            dp = dot(v[h, j], dot_t[h, :, a:b])
+            g = (p * (dp - delta[h][:, a:b])).astype(BF)
+            gs_b[h, j, :, a:b] = g
+            dq_t[h, :, a:b] += dot(kct[h, j], g)
+    d_cols = [(dq_t[h, 0:128, :] * SCALE).T.astype(BF) for h in range(2)]
+    d_cols.append(((dq_t[0, 128:256, :] + dq_t[1, 128:256, :]) * SCALE).T.astype(BF))
+    for n in range(3):
+        d_out[:, :, n * 128 : (n + 1) * 128] = d_cols[n].reshape(NCTX, TOK, 128)
+    dx = Exchange(lambda c: d_out.at[c], lambda c: d_in.at[c], d_mid, gs, grs, sends)
+    dx.start_far()
+    dx.start_near()
+    d_in[ctx] = d_out[ctx]
+    ox.relay()
 
     def weight_grad(buf, g):
         for i in range(2):
@@ -342,7 +366,7 @@
     zv = send_z(zv_out, zv_in, zvs, zvr)
 
     swc = []
-    ycp = {}
+    yc = {}
 
     def merge(xx):
         swc[xx].wait_recv()
@@ -352,17 +376,22 @@
             return carry
 
         lax.fori_loop(0, NY, add, 0)
-
-    lo2, hi2 = pl.ds(0, 2), pl.ds(2, 2)
+        far, near, box, back = (up, down, y_dn, yd) if xx % 2 == 0 else (down, up, y_up, yu)
+        yc[xx, 0] = go(rc(yb.at[xx, yo], y_mid.at[xx], ys.at[xx, 0], yr.at[xx, 0], far))
+        yc[xx, 1] = go(rc(yb.at[xx, back], box.at[xx], ys.at[xx, 1], yr.at[xx, 1], near))
+
+    def pass_on(xx):
+        far, box, to = (up, y_up, yu) if xx % 2 == 0 else (down, y_dn, yd)
+        yc[xx, 0].wait_recv()
+        yb[xx, to] = (yb[xx, to].astype(F32) + y_mid[xx].astype(F32)).astype(BF)
+        yc[xx, 2] = go(rc(yb.at[xx, to], box.at[xx], ys.at[xx, 2], yr.at[xx, 2], far))
+
     for j in range(NCH):
         a, b = spans[j]
         r = slice(j * CHUNK, (j + 1) * CHUNK)
         kr_g = []
         for h in range(2):
-            dp = dot(v[h, j], dot_t[h, :, a:b])
-            g = (sc[h, r, a:b] * (dp - delta[h][:, a:b])).astype(BF)
-            dk = dot(g, qc[h, a:b, :]) * SCALE
-            dq_t[h, :, a:b] += dot(kct[h, j], g)
+            dk = dot(gs_b[h, j, :, a:b], qc[h, a:b, :]) * SCALE
             gk[r, h * 128 : (h + 1) * 128] = dk[:, 0:128].astype(BF)
             kr_g.append(dk[:, 128:256])
         xx, kk = j // NC, j % NC
@@ -372,65 +401,28 @@
         lk[xx, kk, :, :, 0:LAT] = lat_part.reshape(NY, TOK, LAT)
         if kk == 1:
             swc.append(go(rc(lk.at[xx, 1 - k], sw_in.at[xx], ss.at[xx], sr.at[xx], sib)))
-        if j == 2:
-            ox.relay()
-        if j == 4:
-            merge(0)
-        if j == 5:
-            merge(1)
-            ycp[0] = go(rc(yb.at[lo2, yo], y_mid.at[0], ys.at[0], yr.at[0], up))
-            ycp[1] = go(rc(yb.at[lo2, yd], y_dn.at[lo2], ys.at[1], yr.at[1], down))
-    d_cols = [(dq_t[h, 0:128, :] * SCALE).T.astype(BF) for h in range(2)]
-    d_cols.append(((dq_t[0, 128:256, :] + dq_t[1, 128:256, :]) * SCALE).T.astype(BF))
-    for n in range(3):
-        d_out[:, :, n * 128 : (n + 1) * 128] = d_cols[n].reshape(NCTX, TOK, 128)
-    dx = Exchange(lambda c: d_out.at[c], lambda c: d_in.at[c], d_mid, gs, grs, sends)
-    dx.start_far()
-    dx.start_near()
-    d_in[ctx] = d_out[ctx]
+    merge(0)
     weight_grad(zk_out, gk)
     zk = send_z(zk_out, zk_in, zks, zkr)
+    merge(1)
+    pass_on(0)
     merge(2)
     merge(3)
-    ycp[2] = go(rc(yb.at[hi2, yo], y_mid.at[1], ys.at[2], yr.at[2], down))
-    ycp[3] = go(rc(yb.at[hi2, yu], y_up.at[hi2], ys.at[3], yr.at[3], up))
-    ycp[0].wait_recv()
-    for i in range(2):
-        yb[i, yu] = (yb[i, yu].astype(F32) + y_mid[0, i].astype(F32)).astype(BF)
-    ycp[4] = go(rc(yb.at[lo2, yu], y_up.at[lo2], ys.at[4], yr.at[4], up))
+    pass_on(1)
     dx.relay()
-    ycp[2].wait_recv()
-    for i in range(2):
-        yb[2 + i, yd] = (yb[2 + i, yd].astype(F32) + y_mid[1, i].astype(F32)).astype(BF)
-    ycp[5] = go(rc(yb.at[hi2, yd], y_dn.at[hi2], ys.at[5], yr.at[5], down))
-
-    ox.finish()
+    pass_on(2)
+    pass_on(3)
+
     results = []
 
     def put(n, a, b):
         results.append(pltpu.make_async_copy(a, b, outs.at[n]))
         results[-1].start()
 
+    ox.finish()
     for c in range(NCTX):
         att_ref[0, :, c * 256 : (c + 1) * 256] = o_in[c]
     put(0, att_ref, att_h)
-    for n in (1, 3, 4, 5):
-        ycp[n].wait_recv()
-
-    def total_y(i, carry):
-        t = yb[i, y].astype(F32) + y_up[i].astype(F32) + y_dn[i].astype(F32)
-        xb[i] = t.astype(BF)
-        return carry
-
-    lax.fori_loop(0, NX, total_y, 0)
-    top, bot = pl.ds(0, half), pl.ds(half, half)
-    xcp = {}
-    xcp[0] = go(rc(xb.at[xo, top], x_mid.at[0], x2s.at[0], x2r.at[0], right))
-    xcp[1] = go(rc(xb.at[xo, bot], x_mid.at[1], x2s.at[1], x2r.at[1], left))
-    xcp[2] = go(rc(xb.at[xu, bot], x_up.at[bot], x2s.at[2], x2r.at[2], right))
-    xcp[3] = go(rc(xb.at[xd, top], x_dn.at[top], x2s.at[3], x2r.at[3], left))
-    for copy in zv:
-        copy.wait_recv()
 
     def total_z(buf, inbox):
         t = buf[z].astype(F32)
@@ -438,20 +430,40 @@
             t = t + inbox[d].astype(F32)
         return t.astype(BF).reshape(NY, 16, 256)
 
+    for copy in zv:
+        copy.wait_recv()
     z_out[:, :, 256:512] = total_z(zv_out, zv_in)
-    xcp[0].wait_recv()
-    xb[xu, top] = (xb[xu, top].astype(F32) + x_mid[0].astype(F32)).astype(BF)
-    xcp[4] = go(rc(xb.at[xu, top], x_up.at[top], x2s.at[4], x2r.at[4], right))
-    xcp[1].wait_recv()
-    xb[xd, bot] = (xb[xd, bot].astype(F32) + x_mid[1].astype(F32)).astype(BF)
-    xcp[5] = go(rc(xb.at[xd, bot], x_dn.at[bot], x2s.at[5], x2r.at[5], left))
+
+    done = len(sends)
+    for copy in sends[: done - 21]:
+        copy.wait_send()
+    for xx in range(NX):
+        yc[xx, 1].wait_recv()
+        yc[xx, 2].wait_recv()
+        t = yb[xx, y].astype(F32) + y_up[xx].astype(F32) + y_dn[xx].astype(F32)
+        xb[xx] = t.astype(BF)
+    xcp = {}
+
+    def x_go(n, src, dst, dev):
+        xcp[n] = go(rc(src, dst, x2s.at[n], x2r.at[n], dev))
+
+    x_go(0, xb.at[xo, top_r], x_mid.at[0], right)
+    x_go(1, xb.at[xo, bot_r], x_mid.at[1], left)
+    x_go(2, xb.at[xu, bot_r], x_up.at[bot_r], right)
+    x_go(3, xb.at[xd, top_r], x_dn.at[top_r], left)
     for copy in zk:
         copy.wait_recv()
     z_out[:, :, 0:256] = total_z(zk_out, zk_in)
     wc = []
-    for d in range(1, NY):
+    for d in (2, 1, 3):
         to = lax.rem(y + d, NY)
         wc.append(go(rc(z_out.at[to], w_in.at[d - 1], w2s.at[d - 1], w2r.at[d - 1], {"seq": to})))
+    xcp[0].wait_recv()
+    xb[xu, top_r] = (xb[xu, top_r].astype(F32) + x_mid[0].astype(F32)).astype(BF)
+    x_go(4, xb.at[xu, top_r], x_up.at[top_r], right)
+    xcp[1].wait_recv()
+    xb[xd, bot_r] = (xb[xd, bot_r].astype(F32) + x_mid[1].astype(F32)).astype(BF)
+    x_go(5, xb.at[xd, bot_r], x_dn.at[bot_r], left)
     dx.finish()
     for c in range(NCTX):
         for h in range(2):
@@ -479,7 +491,7 @@
     wvg_ref[...] = t[:, 256:512]
     put(5, wkg_ref, wkg_h)
     put(6, wvg_ref, wvg_h)
-    for copy in sends:
+    for copy in sends[done - 21 :]:
         copy.wait_send()
     for copy in results:
         copy.wait()
@@ -500,6 +512,7 @@
     def vm(*shape, dtype=BF):
         return pltpu.VMEM(shape, dtype)
 
+    half = TOK // 2
     table = pltpu.SMEM((1, NX * NC * NY), jnp.int32)
     return pl.pallas_call(
         core_kernel,
@@ -518,19 +531,20 @@
             vm(2, NCH, CHUNK, 256), vm(2, NCH, 256, CHUNK),
             vm(2, NCH, CHUNK, 128), vm(2, NCH, 128, CHUNK),
             vm(2, NQ, 256), vm(2, 256, NQ), vm(2, 128, NQ),
-            vm(2, NK, NQ, dtype=F32), vm(NK, 256), vm(NK, 256),
+            vm(2, NCH, CHUNK, NQ, dtype=F32), vm(2, CHUNK, NQ), vm(2, NCH, 1, NQ, dtype=F32),
+            vm(2, NCH, CHUNK, NQ), vm(NK, 256), vm(NK, 256),
             vm(2, 128, NQ, dtype=F32), vm(2, 256, NQ, dtype=F32),
             vm(NCTX, TOK, 256), vm(NCTX, TOK, 256), vm(2, TOK, 256),
             vm(NCTX, TOK, 384), vm(NCTX, TOK, 384), vm(2, TOK, 384),
             vm(NX, NC, NY, TOK, PACK), vm(NX, NY, TOK, PACK), vm(NX, NY, TOK, PACK),
-            vm(2, 2, TOK, PACK), vm(NX, TOK, PACK), vm(NX, TOK, PACK),
-            vm(NX, TOK, PACK), vm(2, TOK // 2, PACK), vm(TOK, PACK), vm(TOK, PACK),
+            vm(NX, TOK, PACK), vm(NX, TOK, PACK), vm(NX, TOK, PACK),
+            vm(NX, TOK, PACK), vm(2, half, PACK), vm(TOK, PACK), vm(TOK, PACK),
             vm(NZ, TOK, 256), vm(NZ, TOK, 256), vm(NZ - 1, TOK, 256), vm(NZ - 1, TOK, 256),
             vm(NY, 16, 512), vm(NY - 1, 16, 512),
             DMA((10,)), DMA((4,)), DMA((4,)), DMA((4,)), DMA((4,)), DMA((4,)), DMA((4,)),
             DMA((4,)), DMA((4,)), DMA((16,)), DMA((16,)),
             DMA((9,)), DMA((9,)), DMA((9,)), DMA((9,)), DMA((9,)), DMA((9,)),
-            DMA((4,)), DMA((4,)), DMA((6,)), DMA((6,)), DMA((6,)), DMA((6,)),
+            DMA((4,)), DMA((4,)), DMA((4, 3)), DMA((4, 3)), DMA((6,)), DMA((6,)),
             DMA((7,)), DMA((7,)), DMA((7,)), DMA((7,)), DMA((3,)), DMA((3,)),
         ],
         compiler_params=pltpu.CompilerParams(

time: 66.9 us -> 68.6 us (1.025); the launches traced: 66.7 us -> 67.6 us
  Pallas kernels: 65.8 us -> 66.8 us
    pallas_call x1, Pallas kernels: 63.9 us -> 64.8 us  [core(): pl.pallas_call(core_kernel, out_shape=tuple((jax.ShapeDtypeStruct(s, d) f...]
where the time goes in v3:
time: 68.6 us; the launch traced here: 67.6 us
  Pallas kernels  66.8 us (97%)
  between operations  0.8 us (1%)
    pallas_call x1, Pallas kernels, core(): pl.pallas_call(core_kernel, out_shape=tuple((jax.ShapeDtypeStruct(s, d) f...  64.8 us
    pallas_call x1, Pallas kernels, store(): pl.pallas_call(store_kernel, out_shape=tuple((jax.ShapeDtypeStruct(s, d)...  1.97 us

profile of v3, /device:TPU:2, one launch (start us, length us, event | category | flops | bytes accessed | tf_op | source)
XLA Modules:
  0.0 67.6 jit_solution(11256299818907377393)
XLA Ops:
  0.6 64.8 %core.1 = (bf16[1,64,2048]{2,1,0:T(8,128)(2,1)}, bf16[1,64,16,128]{3,2,1,0:T(8,128)(2,1)}, bf16[1,64,16,64]{3,2,1,0:T(8,128)(2,1)}, bf16[1,64,512]{2,1,0:T(8,128...) custom-call(bf16[1,64,16,128]{3,2,1,0:T(8,128)(2,1)} %qn_h.1, ...), custom_call_target="tpu_custom_call" | custom-call | tf_op jit(solution)/shard_map/core/pallas_call | solution.py:517
  65.4 2.0 %store.1 = (bf16[1,64,2048]{2,1,0:T(8,128)(2,1)}, bf16[1,64,16,128]{3,2,1,0:T(8,128)(2,1)}, bf16[1,64,16,64]{3,2,1,0:T(8,128)(2,1)}, bf16[1,64,512]{2,1,0:T(8,12...) custom-call(bf16[1,64,2048]{2,1,0:T(8,128)(2,1)} %get-tuple-element.14.refs_0_, ...), custom_call_target="tpu_custom_call" | custom-call | tf_op jit(solution)/shard_map/store/pallas_call | solution.py:571

commit v4 on v2

v4 whole, which is shorter than its diff:
```python
import math

import jax
import jax.numpy as jnp
from jax import lax
from jax.experimental import pallas as pl
from jax.experimental.pallas import tpu as pltpu
from jax.sharding import PartitionSpec as P

NEG = -1e30
MESH = pl.DeviceIdType.MESH
ANY = pl.BlockSpec(memory_space=pl.ANY)
DMA = pltpu.SemaphoreType.DMA
BF = jnp.bfloat16
F32 = jnp.float32

NX, NC, NY, NZ = 4, 2, 4, 8
NCTX = NX * NC
TOK, HEADS, HD, RD, LAT = 64, 16, 128, 64, 512
PACK = 640
NQ = NCTX * TOK
NK = NX * NC * NY * TOK
CHUNK = 256
NCH = NK // CHUNK
SCALE = 1.0 / math.sqrt(HD + RD)
SCALE2 = SCALE * math.log2(math.e)


def rc(src, dst, send, recv, dev):
    return pltpu.make_async_remote_copy(
        src_ref=src, dst_ref=dst, send_sem=send, recv_sem=recv, device_id=dev, device_id_type=MESH
    )


def dot(a, b):
    return jnp.dot(a, b, preferred_element_type=F32)


class Exchange:
    def __init__(self, src, dst, relay, ss, rs, sends):
        ctx = lax.axis_index("ctx")
        self.me = ctx
        x, k = ctx // NC, lax.rem(ctx, NC)
        self.right, self.left = lax.rem(x + 1, NX) * NC, lax.rem(x + NX - 1, NX) * NC
        self.far = lax.rem(x + 2, NX) * NC
        self.x, self.k = x * NC, k
        self.src, self.dst, self.mid = src, dst, relay
        self.ss, self.rs, self.sends = ss, rs, sends
        self.slots = {}

    def go(self, slot, src, dst, send, recv, to):
        copy = rc(src, dst, self.ss.at[send], self.rs.at[recv], {"ctx": to})
        copy.start()
        self.sends.append(copy)
        self.slots[slot] = copy

    def start_far(self):
        k = self.k
        self.go(7, self.src(self.far + k), self.mid.at[0], 5, 7, self.right + k)
        self.go(8, self.src(self.far + 1 - k), self.mid.at[1], 6, 8, self.left + k)

    def start_near(self):
        k, me = self.k, self.me
        for slot, to in (
            (1, self.right + k), (3, self.left + k),
            (2, self.right + 1 - k), (4, self.left + 1 - k),
            (0, self.x + 1 - k),
        ):
            self.go(slot, self.src(to), self.dst(me), slot, slot, to)

    def relay(self):
        k = self.k
        self.slots[7].wait_recv()
        self.go(5, self.mid.at[0], self.dst(self.left + k), 7, 5, self.right + k)
        self.slots[8].wait_recv()
        self.go(6, self.mid.at[1], self.dst(self.right + k), 8, 6, self.left + 1 - k)

    def finish(self):
        for slot in range(7):
            self.slots[slot].wait_recv()


def vm(*shape, dtype=BF):
    return pltpu.VMEM(shape, dtype)


def greet_and_wait(devices):
    barrier = pltpu.get_barrier_semaphore()
    for dev in devices:
        pl.semaphore_signal(barrier, inc=1, device_id=dev, device_id_type=MESH)
    return barrier


def gather_kernel(
    qn_h, qr_h, do_h, lat_h, kr_h, q_all, lat_all,
    rows_n, rows_r, qn_v, qr_v, do_v, lat_v, kr_v, comb, pack, q_mid,
    loc, xs, xr, us, ur, ds, dr, fs, fr, ws, wr, qs, qrs,
):
    ctx = lax.axis_index("ctx")
    y = lax.axis_index("seq")
    x = ctx // NC
    k = lax.rem(ctx, NC)
    xu, xd, xo = lax.rem(x + 1, NX), lax.rem(x + NX - 1, NX), lax.rem(x + 2, NX)
    yu, yd, yo = lax.rem(y + 1, NY), lax.rem(y + NY - 1, NY), lax.rem(y + 2, NY)
    sib = {"ctx": x * NC + 1 - k}
    right, left = {"ctx": xu * NC + k}, {"ctx": xd * NC + k}
    up, down = {"seq": yu}, {"seq": yd}
    loads = []
    for n, (a, b) in enumerate((
        (lat_h, lat_v), (kr_h, kr_v), (qn_h, qn_v), (qr_h, qr_v), (do_h, do_v),
    )):
        loads.append(pltpu.make_async_copy(a, b, loc.at[n]))
        loads[-1].start()
    devices = [sib, right, left, {"ctx": xu * NC + 1 - k}, {"ctx": xd * NC + 1 - k}, up, down]
    devices += [{"seq": yy, "ctx": x * NC + 1 - k} for yy in (yu, yd)]
    barrier = greet_and_wait(devices)
    loads[0].wait()
    loads[1].wait()
    comb[:, 0:LAT] = lat_v[0]
    comb[:, LAT : LAT + RD] = kr_v[0]
    comb[:, LAT + RD :] = kr_v[0]
    pl.semaphore_wait(barrier, len(devices))
    sends = []

    def go(copy):
        copy.start()
        sends.append(copy)
        return copy

    mine = lat_all.at[x, k, y]
    xc = [go(rc(comb, mine, xs.at[0], xr.at[0], right)), go(rc(comb, mine, xs.at[1], xr.at[1], left))]
    ups = {0: go(rc(comb, mine, us.at[0], ur.at[0], up))}
    downs = {0: go(rc(comb, mine, ds.at[0], dr.at[0], down))}
    swaps = {0: go(rc(comb, mine, ws.at[0], wr.at[0], sib))}
    own = pltpu.make_async_copy(comb, mine, loc.at[5])
    own.start()
    for n in range(2, 5):
        loads[n].wait()
    rows_n[...] = qn_v[0].astype(F32).reshape(TOK * HEADS, HD)
    rows_r[:, 0:RD] = qr_v[0].astype(F32).reshape(TOK * HEADS, RD)
    lane_t = lax.broadcasted_iota(jnp.int32, (TOK, 128), 1)

    def head(n):
        return pl.ds(n, TOK, stride=HEADS)

    for c in range(NCTX):
        for h in range(2):
            pack[c, :, h * 128 : (h + 1) * 128] = rows_n[head(2 * c + h), :].astype(BF)
        pack[c, :, 256:512] = do_v[0, :, c * 256 : (c + 1) * 256]
        pair = jnp.where(
            lane_t < RD, rows_r[head(2 * c), :], pltpu.roll(rows_r[head(2 * c + 1), :], RD, 1)
        )
        pack[c, :, 512:640] = pair.astype(BF)
    qx = Exchange(lambda c: pack.at[c], lambda c: q_all.at[c], q_mid, qs, qrs, sends)
    qx.start_far()
    ownq = pltpu.make_async_copy(pack.at[ctx], q_all.at[ctx], loc.at[6])
    ownq.start()
    half = TOK // 2
    top_r, bot_r = pl.ds(0, half), pl.ds(half, half)
    turn = (k, 1 - k)
    blocks = (x, xd, xo, xu)

    def blk(e, yy):
        return lat_all.at[blocks[e], k, yy]

    def swap(slot, b):
        swaps[slot] = go(rc(b, b, ws.at[slot], wr.at[slot], sib))

    def spread(e):
        b = blk(e, y)
        ups[e] = go(rc(b, b, us.at[e], ur.at[e], up))
        downs[e] = go(rc(b, b, ds.at[e], dr.at[e], down))
        swap(e, b)

    fwd = {}

    def onward(e):
        way = turn[e // 2]
        ups[e].wait_recv()
        downs[e].wait_recv()
        b = blk(e, lax.rem(y + 3 + 2 * way, NY))
        to = lax.rem(y + 1 + 2 * way, NY)
        fwd[e] = go(rc(b, b, fs.at[e], fr.at[e], {"seq": to}))
        swaps[12 + e] = go(rc(b, b, ws.at[12 + e], wr.at[12 + e], {"seq": to, "ctx": x * NC + 1 - k}))
        swap(4 + e, blk(e, yd))
        swap(8 + e, blk(e, yu))

    xc[0].wait_recv()
    b = lat_all.at[xd, k, y, top_r]
    xc.append(go(rc(b, b, xs.at[2], xr.at[2], right)))
    xc[1].wait_recv()
    b = lat_all.at[xu, k, y, bot_r]
    xc.append(go(rc(b, b, xs.at[3], xr.at[3], left)))
    spread(1)
    spread(3)
    qx.start_near()
    onward(0)
    xc[2].wait_recv()
    xc[3].wait_recv()
    spread(2)
    qx.relay()
    onward(1)
    onward(3)
    onward(2)
    for e in (0, 1, 3, 2):
        fwd[e].wait_recv()
    for slot in range(16):
        swaps[slot].wait_recv()
    qx.finish()
    for copy in sends:
        copy.wait_send()
    own.wait()
    ownq.wait()


def gather(*args):
    return pl.pallas_call(
        gather_kernel,
        out_shape=(
            jax.ShapeDtypeStruct((NCTX, TOK, PACK), BF),
            jax.ShapeDtypeStruct((NX, NC, NY, TOK, PACK), BF),
        ),
        in_specs=[ANY] * 5,
        out_specs=(ANY, ANY),
        scratch_shapes=[
            vm(TOK * HEADS, 128, dtype=F32), vm(TOK * HEADS, 128, dtype=F32),
            vm(1, TOK, HEADS, HD), vm(1, TOK, HEADS, RD), vm(1, TOK, HEADS * HD),
            vm(1, TOK, LAT), vm(1, TOK, RD),
            vm(TOK, PACK), vm(NCTX, TOK, PACK), vm(2, TOK, PACK),
            DMA((7,)), DMA((4,)), DMA((4,)), DMA((4,)), DMA((4,)), DMA((4,)), DMA((4,)),
            DMA((4,)), DMA((4,)), DMA((16,)), DMA((16,)), DMA((9,)), DMA((9,)),
        ],
        compiler_params=pltpu.CompilerParams(
            collective_id=0, has_side_effects=True, vmem_limit_bytes=60 * 2**20
        ),
        name="gather",
    )(*args)


def attend_kernel(
    doc_h, img_h, flag_h, q_h, lat_h, wk_h, wv_h, oq_h, lk_h, wg_h,
    doc_ref, img_ref, flag_ref, q_v, lat_v, w_all, w_t, lat_t, kc, kct, v, vt,
    qc, qct, do_s, dot_t, qdoc, qcode, qpos, sc, pb, mj, mx, tot, delta, gk, gv, o_t, dq_t,
    oq, lk, wg, loc, latsem, outsem, lksem,
):
    y = lax.axis_index("seq")
    loads = []
    for n, (a, b) in enumerate((
        (wk_h, w_all.at[:, pl.ds(0, 256)]), (wv_h, w_all.at[:, pl.ds(256, 256)]), (q_h, q_v),
        (doc_h, doc_ref), (img_h, img_ref), (flag_h, flag_ref),
    )):
        loads.append(pltpu.make_async_copy(a, b, loc.at[n]))
        loads[-1].start()

    def lat_copy(j):
        return pltpu.make_async_copy(lat_h.at[j], lat_v.at[j], latsem.at[j])

    for j in range(NCH):
        lat_copy(j).start()
    for copy in loads:
        copy.wait()
    w_t[...] = w_all[...].T
    o_t[...] = jnp.zeros_like(o_t)
    dq_t[...] = jnp.zeros_like(dq_t)
    mx[...] = jnp.full_like(mx, NEG)
    tot[...] = jnp.zeros_like(tot)
    for h in range(2):
        qc[h, :, 0:128] = q_v[:, h * 128 : (h + 1) * 128]
        qc[h, :, 128:256] = q_v[:, 512:640]
        qct[h] = qc[h].T
        do_s[h] = q_v[:, 256 + h * 128 : 256 + (h + 1) * 128]
        dot_t[h] = do_s[h].T
    lane_q = lax.broadcasted_iota(jnp.int32, (1, NQ), 1)
    grp = lane_q // TOK
    one_doc = jnp.zeros((1, NQ), jnp.int32)
    one_code = jnp.zeros((1, NQ), jnp.int32)
    for c in range(NCTX):
        b = NY * c + y
        one_doc = jnp.where(grp == c, doc_ref[0, b], one_doc)
        code = jnp.where(flag_ref[0, b] == 1, doc_ref[0, b] * 64 + img_ref[0, b], -1)
        one_code = jnp.where(grp == c, code, one_code)
    qdoc[...] = one_doc
    qcode[...] = one_code
    qpos[...] = (NY * grp + y) * TOK + lane_q % TOK
    sub = lax.broadcasted_iota(jnp.int32, (TOK, 1), 0)
    lane_k = lax.broadcasted_iota(jnp.int32, (CHUNK, 128), 1)
    row_k = lax.broadcasted_iota(jnp.int32, (128, CHUNK), 0)
    zero = jnp.zeros((), BF)

    def by_width(body):
        for j in range(NCH):
            lo = max(0, j - 1) // 2 * 2
            hi = min(NCTX, (min(NCTX, j + 5) + 1) // 2 * 2)
            body(j, lo * TOK, (hi - lo) * TOK)

    def project(j):
        lat_copy(j).wait()
        lat = lat_v[j, :, 0:LAT]
        kr = lat_v[j, :, LAT:PACK]
        lt = lat.T
        lat_t[:, j * CHUNK : (j + 1) * CHUNK] = lt
        kv = dot(lat, w_all[...]).astype(BF)
        kvt = dot(w_t[...], lt).astype(BF)
        krt = kr.T
        for h in range(2):
            kc[h, j, :, 0:128] = kv[:, h * 128 : (h + 1) * 128]
            kc[h, j, :, 128:256] = jnp.where((lane_k < RD) == (h == 0), kr, zero)
            kct[h, j, 0:128] = kvt[h * 128 : (h + 1) * 128]
            kct[h, j, 128:256] = jnp.where((row_k < RD) == (h == 0), krt, zero)
            v[h, j] = kv[:, 256 + h * 128 : 256 + (h + 1) * 128]
            vt[h, j] = kvt[256 + h * 128 : 256 + (h + 1) * 128]

    def soften(j, a, width):
        q = pl.ds(a, width)
        thr = []
        for i in range(CHUNK // TOK):
            kb = j * (CHUNK // TOK) + i
            kcode = jnp.where(flag_ref[0, kb] == 1, doc_ref[0, kb] * 64 + img_ref[0, kb], -2)
            t = jnp.where(qdoc[:, q] == doc_ref[0, kb], qpos[:, q] - kb * TOK, -1)
            thr.append(jnp.where(qcode[:, q] == kcode, NK, t))
        for h in range(2):
            raw = dot(kc[h, j], qct[h, :, q])
            top = None
            masked = []
            for i in range(CHUNK // TOK):
                m = jnp.where(sub <= thr[i], raw[i * TOK : (i + 1) * TOK] * SCALE2, NEG)
                masked.append(m)
                one = jnp.max(m, axis=0, keepdims=True)
                top = one if top is None else jnp.maximum(top, one)
            part = None
            for i in range(CHUNK // TOK):
                p = jnp.exp2(masked[i] - top)
                sc[h, j, i * TOK : (i + 1) * TOK, q] = p
                pb[h, i * TOK : (i + 1) * TOK, 0:width] = p.astype(BF)
                one = jnp.sum(p, axis=0, keepdims=True)
                part = one if part is None else part + one
            mj[h, j, :, q] = top
            old = mx[h, :, q]
            new = jnp.maximum(old, top)
            old_f, new_f = jnp.exp2(old - new), jnp.exp2(top - new)
            o_t[h, :, q] = o_t[h, :, q] * old_f + dot(vt[h, j], pb[h, :, 0:width]) * new_f
            tot[h, :, q] = tot[h, :, q] * old_f + part * new_f
            mx[h, :, q] = new

    for j in range(NCH):
        project(j)
    by_width(soften)
    for h in range(2):
        tot[h] = 1.0 / tot[h]
        out = o_t[h] * tot[h]
        oq[:, h * 128 : (h + 1) * 128] = out.T.astype(BF)
        delta[h] = jnp.sum(out * dot_t[h].astype(F32), axis=0, keepdims=True)

    def grads(j, a, width):
        q = pl.ds(a, width)
        kr_g = []
        for h in range(2):
            f = jnp.exp2(mj[h, j, :, q] - mx[h, :, q]) * tot[h, :, q]
            p = sc[h, j, :, q] * f
            gv[j, :, h * 128 : (h + 1) * 128] = dot(p.astype(BF), do_s[h, q, :]).astype(BF)
            dp = dot(v[h, j], dot_t[h, :, q])
            g = (p * (dp - delta[h, :, q])).astype(BF)
            dk = dot(g, qc[h, q, :]) * SCALE
            dq_t[h, :, q] += dot(kct[h, j], g)
            gk[j, :, h * 128 : (h + 1) * 128] = dk[:, 0:128].astype(BF)
            kr_g.append(dk[:, 128:256])
        lk[j, :, LAT:PACK] = jnp.where(lane_k < RD, kr_g[0], kr_g[1]).astype(BF)

    by_width(grads)

    def lk_copy(j):
        return pltpu.make_async_copy(lk.at[j], lk_h.at[j], lksem.at[j])

    for j in range(NCH):
        lk[j, :, 0:LAT] = (dot(gk[j], w_t[0:256, :]) + dot(gv[j], w_t[256:512, :])).astype(BF)
        lk_copy(j).start()
    for n, g in enumerate((gk, gv)):
        for i in range(2):
            rows = slice(i * 256, (i + 1) * 256)
            wg[rows, n * 256 : (n + 1) * 256] = dot(lat_t[rows, :], g[...].reshape(NK, 256)).astype(BF)
    wg_copy = pltpu.make_async_copy(wg, wg_h, outsem.at[0])
    wg_copy.start()
    for h in range(2):
        oq[:, 256 + h * 128 : 256 + (h + 1) * 128] = (dq_t[h, 0:128, :] * SCALE).T.astype(BF)
    oq[:, 512:640] = ((dq_t[0, 128:256, :] + dq_t[1, 128:256, :]) * SCALE).T.astype(BF)
    oq_copy = pltpu.make_async_copy(oq, oq_h, outsem.at[1])
    oq_copy.start()
    for j in range(NCH):
        lk_copy(j).wait()
    wg_copy.wait()
    oq_copy.wait()


def attend(*args):
    table = pltpu.SMEM((1, NX * NC * NY), jnp.int32)
    row = vm(1, NQ, dtype=jnp.int32)
    return pl.pallas_call(
        attend_kernel,
        out_shape=(
            jax.ShapeDtypeStruct((NQ, PACK), BF),
            jax.ShapeDtypeStruct((NCH, CHUNK, PACK), BF),
            jax.ShapeDtypeStruct((LAT, 512), BF),
        ),
        in_specs=[ANY] * 7,
        out_specs=(ANY,) * 3,
        scratch_shapes=[
            table, table, table,
            vm(NQ, PACK), vm(NCH, CHUNK, PACK), vm(LAT, 512), vm(512, LAT), vm(LAT, NK),
            vm(2, NCH, CHUNK, 256), vm(2, NCH, 256, CHUNK),
            vm(2, NCH, CHUNK, 128), vm(2, NCH, 128, CHUNK),
            vm(2, NQ, 256), vm(2, 256, NQ), vm(2, NQ, 128), vm(2, 128, NQ),
            row, row, row,
            vm(2, NCH, CHUNK, NQ, dtype=F32), vm(2, CHUNK, NQ), vm(2, NCH, 1, NQ, dtype=F32),
            vm(2, 1, NQ, dtype=F32), vm(2, 1, NQ, dtype=F32), vm(2, 1, NQ, dtype=F32),
            vm(NCH, CHUNK, 256), vm(NCH, CHUNK, 256),
            vm(2, 128, NQ, dtype=F32), vm(2, 256, NQ, dtype=F32),
            vm(NQ, PACK), vm(NCH, CHUNK, PACK), vm(LAT, 512),
            DMA((6,)), DMA((NCH,)), DMA((2,)), DMA((NCH,)),
        ],
        compiler_params=pltpu.CompilerParams(vmem_limit_bytes=60 * 2**20),
        name="attend",
    )(*args)


def scatter_kernel(
    oq_h, lk_h, wg_h, att_h, qng_h, qrg_h, latg_h, krg_h, wkg_h, wvg_h,
    att_ref, qng_ref, qrg_ref, latg_ref, krg_ref, wkg_ref, wvg_ref, rows_n, rows_r, outs,
    lk, sw_in, yb, y_mid, y_up, y_dn, x_mid, x_up, x_dn, tb, ub, t_in, u_in,
    d_in, d_mid, wg, z_in, z_out, w_in,
    loc, ss, sr, ys, yr, x2s, x2r, ts, tr, vs, vr, gs, grs, zs, zr, w2s, w2r,
):
    ctx = lax.axis_index("ctx")
    y = lax.axis_index("seq")
    z = lax.axis_index("dp")
    x = ctx // NC
    k = lax.rem(ctx, NC)
    xu, xd, xo = lax.rem(x + 1, NX), lax.rem(x + NX - 1, NX), lax.rem(x + 2, NX)
    yo = lax.rem(y + 2, NY)
    sib = {"ctx": x * NC + 1 - k}
    right, left = {"ctx": xu * NC + k}, {"ctx": xd * NC + k}
    devices = [sib, right, left, {"ctx": xu * NC + 1 - k}, {"ctx": xd * NC + 1 - k}]
    devices += [{"ctx": xo * NC + k}]
    devices += [{"seq": lax.rem(y + d, NY)} for d in range(1, NY)]
    devices += [{"dp": lax.rem(z + d, NZ)} for d in range(1, NZ)]
    barrier = greet_and_wait(devices)
    loads = [pltpu.make_async_copy(lk_h.at[xx, k], lk.at[xx], loc.at[xx]) for xx in range(NX)]
    loads.append(pltpu.make_async_copy(wg_h.at[z], wg, loc.at[4]))
    loads.append(pltpu.make_async_copy(oq_h.at[ctx], d_in.at[ctx], loc.at[5]))
    for copy in loads:
        copy.start()
    pl.semaphore_wait(barrier, len(devices))
    sends = []

    def go(copy):
        copy.start()
        sends.append(copy)
        return copy

    swc = [
        go(rc(lk_h.at[xx, 1 - k], sw_in.at[xx], ss.at[xx], sr.at[xx], sib)) for xx in range(NX)
    ]
    zc = []
    for d in (4, 3, 5, 2, 6, 1, 7):
        to = lax.rem(z + d, NZ)
        zc.append(go(rc(wg_h.at[to], z_in.at[d - 1], zs.at[d - 1], zr.at[d - 1], {"dp": to})))
    dx = Exchange(lambda c: oq_h.at[c], lambda c: d_in.at[c], d_mid, gs, grs, sends)
    dx.start_far()
    dx.start_near()
    half = TOK // 2
    top_r, bot_r = pl.ds(0, half), pl.ds(half, half)
    turn = (k, 1 - k)
    yc = {}

    def merge(xx):
        loads[xx].wait()
        swc[xx].wait_recv()

        def add(i, carry):
            yb[xx, i] = (lk[xx, i].astype(F32) + sw_in[xx, i].astype(F32)).astype(BF)
            return carry

        lax.fori_loop(0, NY, add, 0)
        way = turn[xx % 2]
        far, back = lax.rem(y + 1 + 2 * way, NY), lax.rem(y + 3 + 2 * way, NY)
        yc[xx, 0] = go(rc(yb.at[xx, yo, top_r], y_mid.at[xx], ys.at[xx, 0], yr.at[xx, 0], {"seq": far}))
        yc[xx, 1] = go(rc(yb.at[xx, back, top_r], y_dn.at[xx], ys.at[xx, 1], yr.at[xx, 1], {"seq": back}))

    def pass_on(xx):
        far = lax.rem(y + 1 + 2 * turn[xx % 2], NY)
        yc[xx, 0].wait_recv()
        yb[xx, far, top_r] = (yb[xx, far, top_r].astype(F32) + y_mid[xx].astype(F32)).astype(BF)
        yc[xx, 2] = go(rc(yb.at[xx, far, top_r], y_up.at[xx], ys.at[xx, 2], yr.at[xx, 2], {"seq": far}))

    for xx in range(NX):
        merge(xx)
    xcp = {}

    def x_go(n, src, dst, dev):
        xcp[n] = go(rc(src, dst, x2s.at[n], x2r.at[n], dev))

    one, two = pl.ds(0, 2), pl.ds(2, 2)
    x_go(0, yb.at[xo, one, bot_r], x_mid.at[0], right)
    x_go(1, yb.at[xo, two, bot_r], x_mid.at[1], left)
    x_go(2, yb.at[xu, two, bot_r], x_up.at[two], right)
    x_go(3, yb.at[xd, one, bot_r], x_dn.at[one], left)
    for xx in range(NX):
        pass_on(xx)
    xcp[0].wait_recv()
    yb[xu, one, bot_r] = (yb[xu, one, bot_r].astype(F32) + x_mid[0].astype(F32)).astype(BF)
    x_go(4, yb.at[xu, one, bot_r], x_up.at[one], right)
    xcp[1].wait_recv()
    yb[xd, two, bot_r] = (yb[xd, two, bot_r].astype(F32) + x_mid[1].astype(F32)).astype(BF)
    x_go(5, yb.at[xd, two, bot_r], x_dn.at[two], left)
    dx.relay()
    for xx in range(NX):
        yc[xx, 1].wait_recv()
        yc[xx, 2].wait_recv()
        t = yb[xx, y, top_r].astype(F32) + y_up[xx].astype(F32) + y_dn[xx].astype(F32)
        tb[xx] = t.astype(BF)
    tc, uc = [], []
    for d in (2, 1, 3):
        to = lax.rem(x + d, NX)
        tc.append(go(rc(tb.at[to], t_in.at[d - 1], ts.at[d - 1], tr.at[d - 1], {"ctx": to * NC + k})))
    for n in range(2, 6):
        xcp[n].wait_recv()
    for i in range(NY):
        t = yb[x, i, bot_r].astype(F32) + x_up[i].astype(F32) + x_dn[i].astype(F32)
        ub[i] = t.astype(BF)
    for d in (2, 1, 3):
        to = lax.rem(y + d, NY)
        uc.append(go(rc(ub.at[to], u_in.at[d - 1], vs.at[d - 1], vr.at[d - 1], {"seq": to})))
    loads[4].wait()
    for copy in zc:
        copy.wait_recv()
    t = wg[...].astype(F32)
    for d in range(NZ - 1):
        t = t + z_in[d].astype(F32)
    z_out[...] = t.astype(BF).reshape(NY, 16, 512)
    wc = []
    for d in (2, 1, 3):
        to = lax.rem(y + d, NY)
        wc.append(go(rc(z_out.at[to], w_in.at[d - 1], w2s.at[d - 1], w2r.at[d - 1], {"seq": to})))
    results = []

    def put(n, a, b):
        results.append(pltpu.make_async_copy(a, b, outs.at[n]))
        results[-1].start()

    def head(n):
        return pl.ds(n, TOK, stride=HEADS)

    loads[5].wait()
    dx.finish()
    for c in range(NCTX):
        att_ref[0, :, c * 256 : (c + 1) * 256] = d_in[c, :, 0:256]
        for h in range(2):
            rows_n[head(2 * c + h), :] = d_in[c, :, 256 + h * 128 : 256 + (h + 1) * 128].astype(F32)
        pair = d_in[c, :, 512:640].astype(F32)
        rows_r[head(2 * c), :] = pair
        rows_r[head(2 * c + 1), :] = pltpu.roll(pair, RD, 1)
    qng_ref[0] = rows_n[...].reshape(TOK, HEADS, HD).astype(BF)
    qrg_ref[0] = rows_r[:, 0:RD].reshape(TOK, HEADS, RD).astype(BF)
    put(0, att_ref, att_h)
    put(1, qng_ref, qng_h)
    put(2, qrg_ref, qrg_h)
    for copy in wc:
        copy.wait_recv()
    t = z_out[y].astype(F32)
    for d in range(NY - 1):
        t = t + w_in[d].astype(F32)
    wkg_ref[...] = t[:, 0:256]
    wvg_ref[...] = t[:, 256:512]
    put(5, wkg_ref, wkg_h)
    put(6, wvg_ref, wvg_h)
    for own, inbox, copies, rows in ((tb.at[x], t_in, tc, top_r), (ub.at[y], u_in, uc, bot_r)):
        for copy in copies:
            copy.wait_recv()
        t = own[...].astype(F32)
        for d in range(3):
            t = t + inbox[d].astype(F32)
        latg_ref[0, rows] = t[:, 0:LAT].astype(BF)
        krg_ref[0, rows] = (t[:, LAT : LAT + RD] + t[:, LAT + RD :]).astype(BF)
    put(3, latg_ref, latg_h)
    put(4, krg_ref, krg_h)
    for copy in sends:
        copy.wait_send()
    for copy in results:
        copy.wait()


OUTS = (
    ((1, TOK, HEADS * HD), BF),
    ((1, TOK, HEADS, HD), BF),
    ((1, TOK, HEADS, RD), BF),
    ((1, TOK, LAT), BF),
    ((1, TOK, RD), BF),
    ((16, 256), F32),
    ((16, 256), F32),
)


def scatter(oq, lk, wg):
    half = TOK // 2
    return pl.pallas_call(
        scatter_kernel,
        out_shape=tuple(jax.ShapeDtypeStruct(s, d) for s, d in OUTS),
        in_specs=[ANY] * 3,
        out_specs=(ANY,) * 7,
        scratch_shapes=[
            *(pltpu.VMEM(s, d) for s, d in OUTS),
            vm(TOK * HEADS, 128, dtype=F32), vm(TOK * HEADS, 128, dtype=F32), DMA((7,)),
            vm(NX, NY, TOK, PACK), vm(NX, NY, TOK, PACK), vm(NX, NY, TOK, PACK),
            vm(NX, half, PACK), vm(NX, half, PACK), vm(NX, half, PACK),
            vm(2, 2, half, PACK), vm(NY, half, PACK), vm(NY, half, PACK),
            vm(NX, half, PACK), vm(NY, half, PACK), vm(3, half, PACK), vm(3, half, PACK),
            vm(NCTX, TOK, PACK), vm(2, TOK, PACK),
            vm(TOK, 512), vm(NZ - 1, TOK, 512), vm(NY, 16, 512), vm(NY - 1, 16, 512),
            DMA((6,)), DMA((4,)), DMA((4,)), DMA((4, 3)), DMA((4, 3)), DMA((6,)), DMA((6,)),
            DMA((3,)), DMA((3,)), DMA((3,)), DMA((3,)),
            DMA((9,)), DMA((9,)), DMA((7,)), DMA((7,)), DMA((3,)), DMA((3,)),
        ],
        compiler_params=pltpu.CompilerParams(
            collective_id=1, has_side_effects=True, vmem_limit_bytes=60 * 2**20
        ),
        name="scatter",
    )(
        oq.reshape(NCTX, TOK, PACK),
        lk.reshape(NX, NC, NY, TOK, PACK),
        wg.reshape(NZ, LAT // NZ, 512),
    )


def store_kernel(*refs):
    src, dst, mid, lsem, ssem = refs[0:7], refs[7:14], refs[14:21], refs[21], refs[22]
    reads = [pltpu.make_async_copy(src[n], mid[n], lsem.at[n]) for n in range(7)]
    writes = [pltpu.make_async_copy(mid[n], dst[n], ssem.at[n]) for n in range(7)]
    for copy in reads:
        copy.start()
    for n in range(7):
        reads[n].wait()
        writes[n].start()
    for copy in writes:
        copy.wait()


def store(*arrays):
    return pl.pallas_call(
        store_kernel,
        out_shape=tuple(jax.ShapeDtypeStruct(s, d) for s, d in OUTS),
        in_specs=[ANY] * 7,
        out_specs=(ANY,) * 7,
        scratch_shapes=[*(pltpu.VMEM(s, d) for s, d in OUTS), DMA((7,)), DMA((7,))],
        compiler_params=pltpu.CompilerParams(vmem_limit_bytes=60 * 2**20),
        name="store",
    )(*arrays)


def on_device(
    query_nope, query_rope, latent, key_rope, out_grad,
    key_weight, value_weight, block_doc, block_image, block_flag,
):
    q_all, lat_all = gather(query_nope, query_rope, out_grad, latent, key_rope)
    oq, lk, wg = attend(
        block_doc, block_image, block_flag,
        q_all.reshape(NQ, PACK), lat_all.reshape(NCH, CHUNK, PACK), key_weight, value_weight,
    )
    return store(*scatter(oq, lk, wg))


def solution(mesh):
    return jax.shard_map(
        on_device,
        mesh=mesh,
        in_specs=(
            P("dp", ("ctx", "seq"), None, None),
            P("dp", ("ctx", "seq"), None, None),
            P("dp", ("ctx", "seq"), None),
            P("dp", ("ctx", "seq"), None),
            P("dp", ("ctx", "seq"), None),
            P(None, "ctx"),
            P(None, "ctx"),
            P("dp", None),
            P("dp", None),
            P("dp", None),
        ),
        out_specs=(
            P("dp", ("ctx", "seq"), None),
            P("dp", ("ctx", "seq"), None, None),
            P("dp", ("ctx", "seq"), None, None),
            P("dp", ("ctx", "seq"), None),
            P("dp", ("ctx", "seq"), None),
            P(("dp", "seq"), "ctx"),
            P(("dp", "seq"), "ctx"),
        ),
        check_vma=False,
    )
```

time: 66.9 us -> 76.1 us (1.14)
  Pallas kernels: 65.8 us -> 74.3 us
    pallas_call x1 -> x3, Pallas kernels: 63.9 us -> 72.4 us  [the longest x1 30 us: scatter(): pl.pallas_call(scatter_kernel, out_shape=tuple((jax.ShapeDtypeStruct(s, d...]
where the time goes in v4:
time: 76.1 us; the launch traced here: 75.1 us
  Pallas kernels  74.3 us (98%)
  between operations  0.82 us (1%)
    pallas_call x1, Pallas kernels, scatter(): pl.pallas_call(scatter_kernel, out_shape=tuple((jax.ShapeDtypeStruct(s, d...  30 us
    pallas_call x1, Pallas kernels, gather(): pl.pallas_call(gather_kernel, out_shape=(jax.ShapeDtypeStruct((NCTX, TOK,...  23.2 us
    pallas_call x1, Pallas kernels, attend(): pl.pallas_call(attend_kernel, out_shape=(jax.ShapeDtypeStruct((NQ, PACK),...  19.1 us
    pallas_call x1, Pallas kernels, store(): pl.pallas_call(store_kernel, out_shape=tuple((jax.ShapeDtypeStruct(s, d)...  1.97 us

profile of v4, /device:TPU:2, one launch (start us, length us, event | category | flops | bytes accessed | tf_op | source)
XLA Modules:
  0.0 75.1 jit_solution(16164661604215785922)
XLA Ops:
  0.6 23.2 %gather.1 = (bf16[8,64,640]{2,1,0:T(8,128)(2,1)}, bf16[4,2,4,64,640]{4,3,2,1,0:T(8,128)(2,1)}) custom-call(bf16[1,64,16,128]{3,2,1,0:T(8,128)(2,1)} %qn_h.1, bf16[1,64,16,64]{3,2,1,0:T(8,128)(2,1)} %qr_h.1, bf16[1,64,2048]{2,1,0:T(8,128)(2,1)} %do_h.1, bf16[1,64,512]{2,1,0:T(8,128)(2,1)} %lat_h.1, bf16[1,64,64]{2,1,0:T(8,128)(2,1)} %kr_h.1), custom_call_target="tpu_custom_call" | custom-call | tf_op jit(solution)/shard_map/gather/pallas_call | solution.py:217
  23.9 19.1 %attend.1 = (bf16[512,640]{1,0:T(8,128)(2,1)}, bf16[8,256,640]{2,1,0:T(8,128)(2,1)}, bf16[512,512]{1,0:T(8,128)(2,1)}) custom-call(s32[1,32]{1,0:T(1,128)} %doc_h.1, s32[1,32]{1,0:T(1,128)} %img_h.1, s32[1,32]{1,0:T(1,128)} %flag_h.1, bf16[512,640]{1,0:T(8,128)(2,1)} %bitcast.7, bf16[8,256,640]{2,1,0:T(8,128)(2,1)} %bitcast.5, bf16[512,256]{1,0:T(8,128)(2,1)} %wk_h.1, ...), custom_call_target="tpu_custom_call" | custom-call | tf_op jit(solution)/shard_map/attend/pallas_call | solution.py:397
  43.0 30.0 %scatter.1 = (bf16[1,64,2048]{2,1,0:T(8,128)(2,1)}, bf16[1,64,16,128]{3,2,1,0:T(8,128)(2,1)}, bf16[1,64,16,64]{3,2,1,0:T(8,128)(2,1)}, bf16[1,64,512]{2,1,0:T(8,...) custom-call(bf16[8,64,640]{2,1,0:T(8,128)(2,1)} %bitcast.8, ...), custom_call_target="tpu_custom_call" | custom-call | tf_op jit(solution)/shard_map/scatter/pallas_call | solution.py:604
  73.0 2.0 %store.1 = (bf16[1,64,2048]{2,1,0:T(8,128)(2,1)}, bf16[1,64,16,128]{3,2,1,0:T(8,128)(2,1)}, bf16[1,64,16,64]{3,2,1,0:T(8,128)(2,1)}, bf16[1,64,512]{2,1,0:T(8,12...) custom-call(bf16[1,64,2048]{2,1,0:T(8,128)(2,1)} %get-tuple-element.24.refs_0_, ...), custom_call_target="tpu_custom_call" | custom-call | tf_op jit(solution)/shard_map/store/pallas_call | solution.py:647

commit v5 on v2

--- a/solution.py
+++ b/solution.py
@@ -88,10 +88,11 @@
     comb, pack, q_all, q_mid, lat_all,
     w_all, w_t, lat_t, kc, kct, v, vt, qc, qct, dot_t, sc, gk, gv, o_t, dq_t,
     o_out, o_in, o_mid, d_out, d_in, d_mid,
-    lk, sw_in, yb, y_mid, y_up, y_dn, xb, x_mid, x_up, x_dn,
+    lk, sw_in, yb, y_mid, y_up, y_dn, x_mid, x_up, x_dn, tb, ub, t_in, u_in,
     zk_out, zv_out, zk_in, zv_in, z_out, w_in,
     loc, xs, xr, us, ur, ds, dr, fs, fr, ws, wr,
-    qs, qrs, os, ors, gs, grs, ss, sr, ys, yr, x2s, x2r, zks, zkr, zvs, zvr, w2s, w2r,
+    qs, qrs, os, ors, gs, grs, ss, sr, ys, yr, x2s, x2r, ts, tr, vs, vr,
+    zks, zkr, zvs, zvr, w2s, w2r,
 ):
     ctx = lax.axis_index("ctx")
     y = lax.axis_index("seq")
@@ -113,7 +114,7 @@
         loads[-1].start()
 
     barrier = pltpu.get_barrier_semaphore()
-    greet = [sib, right, left, {"ctx": xu * NC + 1 - k}, {"ctx": xd * NC + 1 - k}]
+    greet = [{"ctx": lax.rem(ctx + d, NCTX)} for d in range(1, NCTX)]
     greet += [{"seq": lax.rem(y + d, NY)} for d in range(1, NY)]
     greet += [{"dp": lax.rem(z + d, NZ)} for d in range(1, NZ)]
     for dev in greet:
@@ -154,43 +155,40 @@
             lane_t < RD, rows_r[head(2 * c), :], pltpu.roll(rows_r[head(2 * c + 1), :], RD, 1)
         )
         pack[c, :, 512:640] = pair.astype(BF)
+    q_all[ctx] = pack[ctx]
     qx = Exchange(lambda c: pack.at[c], lambda c: q_all.at[c], q_mid, qs, qrs, sends)
     qx.start_far()
-
     half = TOK // 2
+    top_r, bot_r = pl.ds(0, half), pl.ds(half, half)
+    turn = (k, 1 - k)
     blocks = (x, xd, xu, xo)
 
     def blk(e, yy):
         return lat_all.at[blocks[e], k, yy]
+
+    def swap(slot, b):
+        swaps[slot] = go(rc(b, b, ws.at[slot], wr.at[slot], sib))
 
     def spread(e):
         b = blk(e, y)
         ups.append(go(rc(b, b, us.at[e], ur.at[e], up)))
         downs.append(go(rc(b, b, ds.at[e], dr.at[e], down)))
-        swaps[e] = go(rc(b, b, ws.at[e], wr.at[e], sib))
-
-    xc[0].wait_recv()
-    b = lat_all.at[xd, k, y, pl.ds(0, half)]
-    xc.append(go(rc(b, b, xs.at[2], xr.at[2], right)))
-    xc[1].wait_recv()
-    b = lat_all.at[xu, k, y, pl.ds(half, half)]
-    xc.append(go(rc(b, b, xs.at[3], xr.at[3], left)))
-    spread(1)
-    spread(2)
-    qx.start_near()
-    q_all[ctx] = pack[ctx]
-    for n in range(5, 7):
-        loads[n].wait()
-    w_all[:, 0:256] = wk_v[...]
-    w_all[:, 256:512] = wv_v[...]
-    w_t[...] = w_all[...].T
-    xc[2].wait_recv()
-    xc[3].wait_recv()
-    spread(3)
-
-    lane_k = lax.broadcasted_iota(jnp.int32, (CHUNK, 128), 1)
-    row_k = lax.broadcasted_iota(jnp.int32, (128, CHUNK), 0)
-    zero = jnp.zeros((), BF)
+        swap(e, b)
+
+    fwd = []
+
+    def onward(e):
+        way = turn[e // 2]
+        ups[e].wait_recv()
+        downs[e].wait_recv()
+        b = blk(e, lax.rem(y + 3 + 2 * way, NY))
+        fwd.append(go(rc(b, b, fs.at[e], fr.at[e], {"seq": lax.rem(y + 1 + 2 * way, NY)})))
+        swap(4 + e, blk(e, yd))
+        swap(8 + e, blk(e, yu))
+
+    def last(e):
+        fwd[e].wait_recv()
+        swap(12 + e, blk(e, yo))
 
     def project(xx, kk):
         j = xx * NC + kk
@@ -209,46 +207,33 @@
             v[h, j] = kv[:, 256 + h * 128 : 256 + (h + 1) * 128]
             vt[h, j] = kvt[256 + h * 128 : 256 + (h + 1) * 128]
 
-    fwd = []
-    for e in range(NX):
-        ups[e].wait_recv()
-        b = blk(e, yd)
-        if e < 2:
-            fwd.append(go(rc(b, b, fs.at[e], fr.at[e], up)))
-        swaps[4 + e] = go(rc(b, b, ws.at[4 + e], wr.at[4 + e], sib))
-        downs[e].wait_recv()
-        b = blk(e, yu)
-        if e >= 2:
-            fwd.append(go(rc(b, b, fs.at[e], fr.at[e], down)))
-        swaps[8 + e] = go(rc(b, b, ws.at[8 + e], wr.at[8 + e], sib))
-        if e == 1:
-            qx.relay()
-        if e >= 2:
-            n = e - 2
-            fwd[n].wait_recv()
-            b = blk(n, yo)
-            swaps[12 + n] = go(rc(b, b, ws.at[12 + n], wr.at[12 + n], sib))
-            project(blocks[n], k)
-    for n in (2, 3):
-        fwd[n].wait_recv()
-        b = blk(n, yo)
-        swaps[12 + n] = go(rc(b, b, ws.at[12 + n], wr.at[12 + n], sib))
-        project(blocks[n], k)
-    for e in range(NX):
-        for slot in (e, 4 + e, 8 + e, 12 + e):
-            swaps[slot].wait_recv()
-        project(blocks[e], 1 - k)
-    qx.finish()
-
-    for h in range(2):
-        for c in range(NCTX):
-            r = slice(c * TOK, (c + 1) * TOK)
-            qc[h, r, 0:128] = q_all[c, :, h * 128 : (h + 1) * 128]
-            qc[h, r, 128:256] = q_all[c, :, 512:640]
-        qct[h] = qc[h].T
-        dot_t[h] = q_all[:, :, 256 + h * 128 : 256 + (h + 1) * 128].reshape(NQ, 128).T
-    for n in range(7, 10):
+    def queries():
+        qx.finish()
+        for h in range(2):
+            for c in range(NCTX):
+                r = slice(c * TOK, (c + 1) * TOK)
+                qc[h, r, 0:128] = q_all[c, :, h * 128 : (h + 1) * 128]
+                qc[h, r, 128:256] = q_all[c, :, 512:640]
+            qct[h] = qc[h].T
+            dot_t[h] = q_all[:, :, 256 + h * 128 : 256 + (h + 1) * 128].reshape(NQ, 128).T
+
+    xc[0].wait_recv()
+    b = lat_all.at[xd, k, y, top_r]
+    xc.append(go(rc(b, b, xs.at[2], xr.at[2], right)))
+    xc[1].wait_recv()
+    b = lat_all.at[xu, k, y, bot_r]
+    xc.append(go(rc(b, b, xs.at[3], xr.at[3], left)))
+    spread(1)
+    spread(2)
+    qx.start_near()
+    for n in range(5, 10):
         loads[n].wait()
+    w_all[:, 0:256] = wk_v[...]
+    w_all[:, 256:512] = wv_v[...]
+    w_t[...] = w_all[...].T
+    o_t[...] = jnp.zeros_like(o_t)
+    dq_t[...] = jnp.zeros_like(dq_t)
+
     lane_q = lax.broadcasted_iota(jnp.int32, (1, NQ), 1)
     grp = lane_q // TOK
     qdoc = jnp.zeros((1, NQ), jnp.int32)
@@ -260,6 +245,32 @@
         qcode = jnp.where(grp == c, code, qcode)
     qpos = (NY * grp + y) * TOK + lane_q % TOK
     sub = lax.broadcasted_iota(jnp.int32, (TOK, 1), 0)
+    lane_k = lax.broadcasted_iota(jnp.int32, (CHUNK, 128), 1)
+    row_k = lax.broadcasted_iota(jnp.int32, (128, CHUNK), 0)
+    zero = jnp.zeros((), BF)
+
+    qx.relay()
+    onward(0)
+    xc[2].wait_recv()
+    xc[3].wait_recv()
+    spread(3)
+    onward(1)
+    last(0)
+    project(blocks[0], k)
+    onward(2)
+    onward(3)
+    last(1)
+    project(blocks[1], k)
+    last(2)
+    project(blocks[2], k)
+    last(3)
+    project(blocks[3], k)
+    for e in range(NX):
+        for slot in (e, 4 + e, 8 + e, 12 + e):
+            swaps[slot].wait_recv()
+        project(blocks[e], 1 - k)
+
+    queries()
 
     spans = []
     for j in range(NCH):
@@ -286,26 +297,22 @@
             thr.append(jnp.where(qcode[:, a:b] == kcode, NK, t))
         for h in range(2):
             raw = dot(kc[h, j], qct[h, :, a:b])
-            part = None
+            top = None
             for i in range(CHUNK // TOK):
-                rows = slice(i * TOK, (i + 1) * TOK)
-                m = jnp.where(sub <= thr[i], raw[rows] * SCALE2, NEG)
-                sc[h, j * CHUNK + i * TOK : j * CHUNK + (i + 1) * TOK, a:b] = m
-                top = jnp.max(m, axis=0, keepdims=True)
-                part = top if part is None else jnp.maximum(part, top)
-            mx[h] = splice(mx[h], jnp.maximum(mx[h][:, a:b], part), a, b)
-
+                m = jnp.where(sub <= thr[i], raw[i * TOK : (i + 1) * TOK] * SCALE2, NEG)
+                sc[h, j, i * TOK : (i + 1) * TOK, a:b] = m
+                one = jnp.max(m, axis=0, keepdims=True)
+                top = one if top is None else jnp.maximum(top, one)
+            mx[h] = splice(mx[h], jnp.maximum(mx[h][:, a:b], top), a, b)
     tot = [jnp.zeros((1, NQ), F32)] * 2
-    o_t[...] = jnp.zeros_like(o_t)
-    dq_t[...] = jnp.zeros_like(dq_t)
     for j in range(NCH):
         a, b = spans[j]
-        r = slice(j * CHUNK, (j + 1) * CHUNK)
-        for h in range(2):
-            p = jnp.exp2(sc[h, r, a:b] - mx[h][:, a:b])
-            sc[h, r, a:b] = p
+        for h in range(2):
+            p = jnp.exp2(sc[h, j, :, a:b] - mx[h][:, a:b])
+            sc[h, j, :, a:b] = p
             tot[h] = splice(tot[h], tot[h][:, a:b] + jnp.sum(p, axis=0, keepdims=True), a, b)
             o_t[h, :, a:b] += dot(vt[h, j], p.astype(BF))
+
     inv = [1.0 / tot[h] for h in range(2)]
     delta = []
     for h in range(2):
@@ -321,8 +328,7 @@
         a, b = spans[j]
         r = slice(j * CHUNK, (j + 1) * CHUNK)
         for h in range(2):
-            p = sc[h, r, a:b] * inv[h][:, a:b]
-            sc[h, r, a:b] = p
+            p = sc[h, j, :, a:b] * inv[h][:, a:b]
             do = q_all[a // TOK : b // TOK, :, 256 + h * 128 : 256 + (h + 1) * 128].reshape(b - a, 128)
             gv[r, h * 128 : (h + 1) * 128] = dot(p.astype(BF), do).astype(BF)
 
@@ -342,7 +348,7 @@
     zv = send_z(zv_out, zv_in, zvs, zvr)
 
     swc = []
-    ycp = {}
+    yc = {}
 
     def merge(xx):
         swc[xx].wait_recv()
@@ -352,15 +358,24 @@
             return carry
 
         lax.fori_loop(0, NY, add, 0)
-
-    lo2, hi2 = pl.ds(0, 2), pl.ds(2, 2)
+        way = turn[xx % 2]
+        far, back = lax.rem(y + 1 + 2 * way, NY), lax.rem(y + 3 + 2 * way, NY)
+        yc[xx, 0] = go(rc(yb.at[xx, yo, top_r], y_mid.at[xx], ys.at[xx, 0], yr.at[xx, 0], {"seq": far}))
+        yc[xx, 1] = go(rc(yb.at[xx, back, top_r], y_dn.at[xx], ys.at[xx, 1], yr.at[xx, 1], {"seq": back}))
+
+    def pass_on(xx):
+        far = lax.rem(y + 1 + 2 * turn[xx % 2], NY)
+        yc[xx, 0].wait_recv()
+        yb[xx, far, top_r] = (yb[xx, far, top_r].astype(F32) + y_mid[xx].astype(F32)).astype(BF)
+        yc[xx, 2] = go(rc(yb.at[xx, far, top_r], y_up.at[xx], ys.at[xx, 2], yr.at[xx, 2], {"seq": far}))
+
     for j in range(NCH):
         a, b = spans[j]
         r = slice(j * CHUNK, (j + 1) * CHUNK)
         kr_g = []
         for h in range(2):
             dp = dot(v[h, j], dot_t[h, :, a:b])
-            g = (sc[h, r, a:b] * (dp - delta[h][:, a:b])).astype(BF)
+            g = (sc[h, j, :, a:b] * ((dp - delta[h][:, a:b]) * inv[h][:, a:b])).astype(BF)
             dk = dot(g, qc[h, a:b, :]) * SCALE
             dq_t[h, :, a:b] += dot(kct[h, j], g)
             gk[r, h * 128 : (h + 1) * 128] = dk[:, 0:128].astype(BF)
@@ -372,65 +387,57 @@
         lk[xx, kk, :, :, 0:LAT] = lat_part.reshape(NY, TOK, LAT)
         if kk == 1:
             swc.append(go(rc(lk.at[xx, 1 - k], sw_in.at[xx], ss.at[xx], sr.at[xx], sib)))
-        if j == 2:
+        if j == 3:
             ox.relay()
         if j == 4:
             merge(0)
-        if j == 5:
+        if j == 6:
             merge(1)
-            ycp[0] = go(rc(yb.at[lo2, yo], y_mid.at[0], ys.at[0], yr.at[0], up))
-            ycp[1] = go(rc(yb.at[lo2, yd], y_dn.at[lo2], ys.at[1], yr.at[1], down))
+        if j == 7:
+            pass_on(0)
     d_cols = [(dq_t[h, 0:128, :] * SCALE).T.astype(BF) for h in range(2)]
     d_cols.append(((dq_t[0, 128:256, :] + dq_t[1, 128:256, :]) * SCALE).T.astype(BF))
     for n in range(3):
         d_out[:, :, n * 128 : (n + 1) * 128] = d_cols[n].reshape(NCTX, TOK, 128)
     dx = Exchange(lambda c: d_out.at[c], lambda c: d_in.at[c], d_mid, gs, grs, sends)
     dx.start_far()
-    dx.start_near()
     d_in[ctx] = d_out[ctx]
+    merge(2)
     weight_grad(zk_out, gk)
     zk = send_z(zk_out, zk_in, zks, zkr)
-    merge(2)
+    pass_on(1)
     merge(3)
-    ycp[2] = go(rc(yb.at[hi2, yo], y_mid.at[1], ys.at[2], yr.at[2], down))
-    ycp[3] = go(rc(yb.at[hi2, yu], y_up.at[hi2], ys.at[3], yr.at[3], up))
-    ycp[0].wait_recv()
-    for i in range(2):
-        yb[i, yu] = (yb[i, yu].astype(F32) + y_mid[0, i].astype(F32)).astype(BF)
-    ycp[4] = go(rc(yb.at[lo2, yu], y_up.at[lo2], ys.at[4], yr.at[4], up))
+    xcp = {}
+
+    def x_go(n, src, dst, dev):
+        xcp[n] = go(rc(src, dst, x2s.at[n], x2r.at[n], dev))
+
+    one, two = pl.ds(0, 2), pl.ds(2, 2)
+    x_go(0, yb.at[xo, one, bot_r], x_mid.at[0], right)
+    x_go(1, yb.at[xo, two, bot_r], x_mid.at[1], left)
+    x_go(2, yb.at[xu, two, bot_r], x_up.at[two], right)
+    x_go(3, yb.at[xd, one, bot_r], x_dn.at[one], left)
+    dx.start_near()
+    pass_on(2)
+    pass_on(3)
+    xcp[0].wait_recv()
+    yb[xu, one, bot_r] = (yb[xu, one, bot_r].astype(F32) + x_mid[0].astype(F32)).astype(BF)
+    x_go(4, yb.at[xu, one, bot_r], x_up.at[one], right)
+    xcp[1].wait_recv()
+    yb[xd, two, bot_r] = (yb[xd, two, bot_r].astype(F32) + x_mid[1].astype(F32)).astype(BF)
+    x_go(5, yb.at[xd, two, bot_r], x_dn.at[two], left)
     dx.relay()
-    ycp[2].wait_recv()
-    for i in range(2):
-        yb[2 + i, yd] = (yb[2 + i, yd].astype(F32) + y_mid[1, i].astype(F32)).astype(BF)
-    ycp[5] = go(rc(yb.at[hi2, yd], y_dn.at[hi2], ys.at[5], yr.at[5], down))
-
-    ox.finish()
+
     results = []
 
     def put(n, a, b):
         results.append(pltpu.make_async_copy(a, b, outs.at[n]))
         results[-1].start()
 
+    ox.finish()
     for c in range(NCTX):
         att_ref[0, :, c * 256 : (c + 1) * 256] = o_in[c]
     put(0, att_ref, att_h)
-    for n in (1, 3, 4, 5):
-        ycp[n].wait_recv()
-
-    def total_y(i, carry):
-        t = yb[i, y].astype(F32) + y_up[i].astype(F32) + y_dn[i].astype(F32)
-        xb[i] = t.astype(BF)
-        return carry
-
-    lax.fori_loop(0, NX, total_y, 0)
-    top, bot = pl.ds(0, half), pl.ds(half, half)
-    xcp = {}
-    xcp[0] = go(rc(xb.at[xo, top], x_mid.at[0], x2s.at[0], x2r.at[0], right))
-    xcp[1] = go(rc(xb.at[xo, bot], x_mid.at[1], x2s.at[1], x2r.at[1], left))
-    xcp[2] = go(rc(xb.at[xu, bot], x_up.at[bot], x2s.at[2], x2r.at[2], right))
-    xcp[3] = go(rc(xb.at[xd, top], x_dn.at[top], x2s.at[3], x2r.at[3], left))
-    for copy in zv:
-        copy.wait_recv()
 
     def total_z(buf, inbox):
         t = buf[z].astype(F32)
@@ -438,18 +445,32 @@
             t = t + inbox[d].astype(F32)
         return t.astype(BF).reshape(NY, 16, 256)
 
+    for copy in zv:
+        copy.wait_recv()
     z_out[:, :, 256:512] = total_z(zv_out, zv_in)
-    xcp[0].wait_recv()
-    xb[xu, top] = (xb[xu, top].astype(F32) + x_mid[0].astype(F32)).astype(BF)
-    xcp[4] = go(rc(xb.at[xu, top], x_up.at[top], x2s.at[4], x2r.at[4], right))
-    xcp[1].wait_recv()
-    xb[xd, bot] = (xb[xd, bot].astype(F32) + x_mid[1].astype(F32)).astype(BF)
-    xcp[5] = go(rc(xb.at[xd, bot], x_dn.at[bot], x2s.at[5], x2r.at[5], left))
+
+    for xx in range(NX):
+        yc[xx, 1].wait_recv()
+        yc[xx, 2].wait_recv()
+        t = yb[xx, y, top_r].astype(F32) + y_up[xx].astype(F32) + y_dn[xx].astype(F32)
+        tb[xx] = t.astype(BF)
+    tc, uc = [], []
+    for d in (2, 1, 3):
+        to = lax.rem(x + d, NX)
+        tc.append(go(rc(tb.at[to], t_in.at[d - 1], ts.at[d - 1], tr.at[d - 1], {"ctx": to * NC + k})))
+    for n in range(2, 6):
+        xcp[n].wait_recv()
+    for i in range(NY):
+        t = yb[x, i, bot_r].astype(F32) + x_up[i].astype(F32) + x_dn[i].astype(F32)
+        ub[i] = t.astype(BF)
+    for d in (2, 1, 3):
+        to = lax.rem(y + d, NY)
+        uc.append(go(rc(ub.at[to], u_in.at[d - 1], vs.at[d - 1], vr.at[d - 1], {"seq": to})))
     for copy in zk:
         copy.wait_recv()
     z_out[:, :, 0:256] = total_z(zk_out, zk_in)
     wc = []
-    for d in range(1, NY):
+    for d in (2, 1, 3):
         to = lax.rem(y + d, NY)
         wc.append(go(rc(z_out.at[to], w_in.at[d - 1], w2s.at[d - 1], w2r.at[d - 1], {"seq": to})))
     dx.finish()
@@ -463,11 +484,14 @@
     qrg_ref[0] = rows_r[:, 0:RD].reshape(TOK, HEADS, RD).astype(BF)
     put(1, qng_ref, qng_h)
     put(2, qrg_ref, qrg_h)
-    for n in range(2, 6):
-        xcp[n].wait_recv()
-    t = xb[x].astype(F32) + x_up[...].astype(F32) + x_dn[...].astype(F32)
-    latg_ref[0] = t[:, 0:LAT].astype(BF)
-    krg_ref[0] = (t[:, LAT : LAT + RD] + t[:, LAT + RD :]).astype(BF)
+    for own, inbox, copies, rows in ((tb.at[x], t_in, tc, top_r), (ub.at[y], u_in, uc, bot_r)):
+        for copy in copies:
+            copy.wait_recv()
+        t = own[...].astype(F32)
+        for d in range(3):
+            t = t + inbox[d].astype(F32)
+        latg_ref[0, rows] = t[:, 0:LAT].astype(BF)
+        krg_ref[0, rows] = (t[:, LAT : LAT + RD] + t[:, LAT + RD :]).astype(BF)
     put(3, latg_ref, latg_h)
     put(4, krg_ref, krg_h)
     for copy in wc:
@@ -500,6 +524,7 @@
     def vm(*shape, dtype=BF):
         return pltpu.VMEM(shape, dtype)
 
+    half = TOK // 2
     table = pltpu.SMEM((1, NX * NC * NY), jnp.int32)
     return pl.pallas_call(
         core_kernel,
@@ -518,19 +543,22 @@
             vm(2, NCH, CHUNK, 256), vm(2, NCH, 256, CHUNK),
             vm(2, NCH, CHUNK, 128), vm(2, NCH, 128, CHUNK),
             vm(2, NQ, 256), vm(2, 256, NQ), vm(2, 128, NQ),
-            vm(2, NK, NQ, dtype=F32), vm(NK, 256), vm(NK, 256),
+            vm(2, NCH, CHUNK, NQ, dtype=F32),
+            vm(NK, 256), vm(NK, 256),
             vm(2, 128, NQ, dtype=F32), vm(2, 256, NQ, dtype=F32),
             vm(NCTX, TOK, 256), vm(NCTX, TOK, 256), vm(2, TOK, 256),
             vm(NCTX, TOK, 384), vm(NCTX, TOK, 384), vm(2, TOK, 384),
             vm(NX, NC, NY, TOK, PACK), vm(NX, NY, TOK, PACK), vm(NX, NY, TOK, PACK),
-            vm(2, 2, TOK, PACK), vm(NX, TOK, PACK), vm(NX, TOK, PACK),
-            vm(NX, TOK, PACK), vm(2, TOK // 2, PACK), vm(TOK, PACK), vm(TOK, PACK),
+            vm(NX, half, PACK), vm(NX, half, PACK), vm(NX, half, PACK),
+            vm(2, 2, half, PACK), vm(NY, half, PACK), vm(NY, half, PACK),
+            vm(NX, half, PACK), vm(NY, half, PACK), vm(3, half, PACK), vm(3, half, PACK),
             vm(NZ, TOK, 256), vm(NZ, TOK, 256), vm(NZ - 1, TOK, 256), vm(NZ - 1, TOK, 256),
             vm(NY, 16, 512), vm(NY - 1, 16, 512),
             DMA((10,)), DMA((4,)), DMA((4,)), DMA((4,)), DMA((4,)), DMA((4,)), DMA((4,)),
             DMA((4,)), DMA((4,)), DMA((16,)), DMA((16,)),
             DMA((9,)), DMA((9,)), DMA((9,)), DMA((9,)), DMA((9,)), DMA((9,)),
-            DMA((4,)), DMA((4,)), DMA((6,)), DMA((6,)), DMA((6,)), DMA((6,)),
+            DMA((4,)), DMA((4,)), DMA((4, 3)), DMA((4, 3)), DMA((6,)), DMA((6,)),
+            DMA((3,)), DMA((3,)), DMA((3,)), DMA((3,)),
             DMA((7,)), DMA((7,)), DMA((7,)), DMA((7,)), DMA((3,)), DMA((3,)),
         ],
         compiler_params=pltpu.CompilerParams(

time: 66.9 us -> 63.7 us (0.952)
  Pallas kernels: 65.8 us -> 62.3 us
    pallas_call x1, Pallas kernels: 63.9 us -> 60.3 us  [core(): pl.pallas_call(core_kernel, out_shape=tuple((jax.ShapeDtypeStruct(s, d) f...]
where the time goes in v5:
time: 63.7 us; the launch traced here: 63.1 us
  Pallas kernels  62.3 us (98%)
  between operations  0.8 us (1%)
    pallas_call x1, Pallas kernels, core(): pl.pallas_call(core_kernel, out_shape=tuple((jax.ShapeDtypeStruct(s, d) f...  60.3 us
    pallas_call x1, Pallas kernels, store(): pl.pallas_call(store_kernel, out_shape=tuple((jax.ShapeDtypeStruct(s, d)...  1.97 us

profile of v5, /device:TPU:2, one launch (start us, length us, event | category | flops | bytes accessed | tf_op | source)
XLA Modules:
  0.0 63.1 jit_solution(13738958033658614273)
XLA Ops:
  0.6 60.3 %core.1 = (bf16[1,64,2048]{2,1,0:T(8,128)(2,1)}, bf16[1,64,16,128]{3,2,1,0:T(8,128)(2,1)}, bf16[1,64,16,64]{3,2,1,0:T(8,128)(2,1)}, bf16[1,64,512]{2,1,0:T(8,128...) custom-call(bf16[1,64,16,128]{3,2,1,0:T(8,128)(2,1)} %qn_h.1, ...), custom_call_target="tpu_custom_call" | custom-call | tf_op jit(solution)/shard_map/core/pallas_call | solution.py:529
  60.9 2.0 %store.1 = (bf16[1,64,2048]{2,1,0:T(8,128)(2,1)}, bf16[1,64,16,128]{3,2,1,0:T(8,128)(2,1)}, bf16[1,64,16,64]{3,2,1,0:T(8,128)(2,1)}, bf16[1,64,512]{2,1,0:T(8,12...) custom-call(bf16[1,64,2048]{2,1,0:T(8,128)(2,1)} %get-tuple-element.14.refs_0_, ...), custom_call_target="tpu_custom_call" | custom-call | tf_op jit(solution)/shard_map/store/pallas_call | solution.py:585

commit v6 on v5

--- a/solution.py
+++ b/solution.py
@@ -86,7 +86,7 @@
     att_ref, qng_ref, qrg_ref, latg_ref, krg_ref, wkg_ref, wvg_ref, rows_n, rows_r, outs,
     qn_v, qr_v, do_v, lat_v, kr_v, wk_v, wv_v, doc_ref, img_ref, flag_ref,
     comb, pack, q_all, q_mid, lat_all,
-    w_all, w_t, lat_t, kc, kct, v, vt, qc, qct, dot_t, sc, gk, gv, o_t, dq_t,
+    w_all, w_t, lat_t, kc, kct, v, vt, qc, qct, dot_t, sc, mx, gk, gv, o_t, dq_t,
     o_out, o_in, o_mid, d_out, d_in, d_mid,
     lk, sw_in, yb, y_mid, y_up, y_dn, x_mid, x_up, x_dn, tb, ub, t_in, u_in,
     zk_out, zv_out, zk_in, zv_in, z_out, w_in,
@@ -217,6 +217,23 @@
             qct[h] = qc[h].T
             dot_t[h] = q_all[:, :, 256 + h * 128 : 256 + (h + 1) * 128].reshape(NQ, 128).T
 
+    def score(xx, kk):
+        j = xx * NC + kk
+        thr = []
+        for i in range(CHUNK // TOK):
+            kb = j * (CHUNK // TOK) + i
+            kcode = jnp.where(flag_ref[0, kb] == 1, doc_ref[0, kb] * 64 + img_ref[0, kb], -2)
+            t = jnp.where(qdoc == doc_ref[0, kb], qpos - kb * TOK, -1)
+            thr.append(jnp.where(qcode == kcode, NK, t))
+        for h in range(2):
+            raw = dot(kc[h, j], qct[h])
+            top = mx[h]
+            for i in range(CHUNK // TOK):
+                m = jnp.where(sub <= thr[i], raw[i * TOK : (i + 1) * TOK] * SCALE2, NEG)
+                sc[h, j, i * TOK : (i + 1) * TOK, :] = m
+                top = jnp.maximum(top, jnp.max(m, axis=0, keepdims=True))
+            mx[h] = top
+
     xc[0].wait_recv()
     b = lat_all.at[xd, k, y, top_r]
     xc.append(go(rc(b, b, xs.at[2], xr.at[2], right)))
@@ -232,6 +249,7 @@
     w_all[:, 256:512] = wv_v[...]
     w_t[...] = w_all[...].T
     o_t[...] = jnp.zeros_like(o_t)
+    mx[...] = jnp.full_like(mx, NEG)
     dq_t[...] = jnp.zeros_like(dq_t)
 
     lane_q = lax.broadcasted_iota(jnp.int32, (1, NQ), 1)
@@ -265,12 +283,15 @@
     project(blocks[2], k)
     last(3)
     project(blocks[3], k)
+    queries()
+    for e in range(NX):
+        score(blocks[e], k)
     for e in range(NX):
         for slot in (e, 4 + e, 8 + e, 12 + e):
             swaps[slot].wait_recv()
         project(blocks[e], 1 - k)
-
-    queries()
+        score(blocks[e], 1 - k)
+
 
     spans = []
     for j in range(NCH):
@@ -285,30 +306,12 @@
             pieces.append(full[:, b:])
         return jnp.concatenate(pieces, axis=1) if len(pieces) > 1 else part
 
-    neg = jnp.full((1, NQ), NEG, F32)
-    mx = [neg, neg]
-    for j in range(NCH):
-        a, b = spans[j]
-        thr = []
-        for i in range(CHUNK // TOK):
-            kb = j * (CHUNK // TOK) + i
-            kcode = jnp.where(flag_ref[0, kb] == 1, doc_ref[0, kb] * 64 + img_ref[0, kb], -2)
-            t = jnp.where(qdoc[:, a:b] == doc_ref[0, kb], qpos[:, a:b] - kb * TOK, -1)
-            thr.append(jnp.where(qcode[:, a:b] == kcode, NK, t))
-        for h in range(2):
-            raw = dot(kc[h, j], qct[h, :, a:b])
-            top = None
-            for i in range(CHUNK // TOK):
-                m = jnp.where(sub <= thr[i], raw[i * TOK : (i + 1) * TOK] * SCALE2, NEG)
-                sc[h, j, i * TOK : (i + 1) * TOK, a:b] = m
-                one = jnp.max(m, axis=0, keepdims=True)
-                top = one if top is None else jnp.maximum(top, one)
-            mx[h] = splice(mx[h], jnp.maximum(mx[h][:, a:b], top), a, b)
+    top_s = [mx[h] for h in range(2)]
     tot = [jnp.zeros((1, NQ), F32)] * 2
     for j in range(NCH):
         a, b = spans[j]
         for h in range(2):
-            p = jnp.exp2(sc[h, j, :, a:b] - mx[h][:, a:b])
+            p = jnp.exp2(sc[h, j, :, a:b] - top_s[h][:, a:b])
             sc[h, j, :, a:b] = p
             tot[h] = splice(tot[h], tot[h][:, a:b] + jnp.sum(p, axis=0, keepdims=True), a, b)
             o_t[h, :, a:b] += dot(vt[h, j], p.astype(BF))
@@ -345,6 +348,7 @@
         return out
 
     weight_grad(zv_out, gv)
+    before = len(sends)
     zv = send_z(zv_out, zv_in, zvs, zvr)
 
     swc = []
@@ -418,6 +422,8 @@
     x_go(2, yb.at[xu, two, bot_r], x_up.at[two], right)
     x_go(3, yb.at[xd, one, bot_r], x_dn.at[one], left)
     dx.start_near()
+    for copy in sends[:before]:
+        copy.wait_send()
     pass_on(2)
     pass_on(3)
     xcp[0].wait_recv()
@@ -503,7 +509,7 @@
     wvg_ref[...] = t[:, 256:512]
     put(5, wkg_ref, wkg_h)
     put(6, wvg_ref, wvg_h)
-    for copy in sends:
+    for copy in sends[before:]:
         copy.wait_send()
     for copy in results:
         copy.wait()
@@ -543,7 +549,7 @@
             vm(2, NCH, CHUNK, 256), vm(2, NCH, 256, CHUNK),
             vm(2, NCH, CHUNK, 128), vm(2, NCH, 128, CHUNK),
             vm(2, NQ, 256), vm(2, 256, NQ), vm(2, 128, NQ),
-            vm(2, NCH, CHUNK, NQ, dtype=F32),
+            vm(2, NCH, CHUNK, NQ, dtype=F32), vm(2, 1, NQ, dtype=F32),
             vm(NK, 256), vm(NK, 256),
             vm(2, 128, NQ, dtype=F32), vm(2, 256, NQ, dtype=F32),
             vm(NCTX, TOK, 256), vm(NCTX, TOK, 256), vm(2, TOK, 256),

time: 63.7 us -> 63.5 us (level)
  no operation moved by 1% of the time
where the time goes in v6:
time: 63.5 us; the launch traced here: 62.7 us
  Pallas kernels  61.9 us (97%)
  between operations  0.8 us (1%)
    pallas_call x1, Pallas kernels, core(): pl.pallas_call(core_kernel, out_shape=tuple((jax.ShapeDtypeStruct(s, d) f...  59.9 us
    pallas_call x1, Pallas kernels, store(): pl.pallas_call(store_kernel, out_shape=tuple((jax.ShapeDtypeStruct(s, d)...  1.97 us

profile of v6, /device:TPU:2, one launch (start us, length us, event | category | flops | bytes accessed | tf_op | source)
XLA Modules:
  0.0 62.7 jit_solution(18351756594135401444)
XLA Ops:
  0.6 59.9 %core.1 = (bf16[1,64,2048]{2,1,0:T(8,128)(2,1)}, bf16[1,64,16,128]{3,2,1,0:T(8,128)(2,1)}, bf16[1,64,16,64]{3,2,1,0:T(8,128)(2,1)}, bf16[1,64,512]{2,1,0:T(8,128...) custom-call(bf16[1,64,16,128]{3,2,1,0:T(8,128)(2,1)} %qn_h.1, ...), custom_call_target="tpu_custom_call" | custom-call | tf_op jit(solution)/shard_map/core/pallas_call | solution.py:535
  60.6 2.0 %store.1 = (bf16[1,64,2048]{2,1,0:T(8,128)(2,1)}, bf16[1,64,16,128]{3,2,1,0:T(8,128)(2,1)}, bf16[1,64,16,64]{3,2,1,0:T(8,128)(2,1)}, bf16[1,64,512]{2,1,0:T(8,12...) custom-call(bf16[1,64,2048]{2,1,0:T(8,128)(2,1)} %get-tuple-element.14.refs_0_, ...), custom_call_target="tpu_custom_call" | custom-call | tf_op jit(solution)/shard_map/store/pallas_call | solution.py:591

commit v7 on v6

--- a/solution.py
+++ b/solution.py
@@ -18,6 +18,8 @@
 NCTX = NX * NC
 TOK, HEADS, HD, RD, LAT = 64, 16, 128, 64, 512
 PACK = 640
+ROWS = TOK * LAT // 128 + TOK * RD // 128
+KROW = TOK * LAT // 128
 NQ = NCTX * TOK
 NK = NX * NC * NY * TOK
 CHUNK = 256
@@ -86,7 +88,7 @@
     att_ref, qng_ref, qrg_ref, latg_ref, krg_ref, wkg_ref, wvg_ref, rows_n, rows_r, outs,
     qn_v, qr_v, do_v, lat_v, kr_v, wk_v, wv_v, doc_ref, img_ref, flag_ref,
     comb, pack, q_all, q_mid, lat_all,
-    w_all, w_t, lat_t, kc, kct, v, vt, qc, qct, dot_t, sc, mx, gk, gv, o_t, dq_t,
+    w_all, w_t, lat_t, kc, kct, v, vt, qc, qct, dot_t, sc, mx, pb, do_s, gk, gv, o_t, dq_t,
     o_out, o_in, o_mid, d_out, d_in, d_mid,
     lk, sw_in, yb, y_mid, y_up, y_dn, x_mid, x_up, x_dn, tb, ub, t_in, u_in,
     zk_out, zv_out, zk_in, zv_in, z_out, w_in,
@@ -121,9 +123,10 @@
         pl.semaphore_signal(barrier, inc=1, device_id=dev, device_id_type=MESH)
     loads[0].wait()
     loads[1].wait()
-    comb[:, 0:LAT] = lat_v[0]
-    comb[:, LAT : LAT + RD] = kr_v[0]
-    comb[:, LAT + RD :] = kr_v[0]
+    for t in range(LAT // 128):
+        comb[t * TOK : (t + 1) * TOK, :] = lat_v[0, :, t * 128 : (t + 1) * 128]
+    comb[KROW:ROWS, 0:RD] = kr_v[0, 0 : TOK // 2]
+    comb[KROW:ROWS, RD:] = kr_v[0, TOK // 2 :]
     lat_all[x, k, y] = comb[...]
     pl.semaphore_wait(barrier, len(greet))
     sends = []
@@ -158,7 +161,7 @@
     q_all[ctx] = pack[ctx]
     qx = Exchange(lambda c: pack.at[c], lambda c: q_all.at[c], q_mid, qs, qrs, sends)
     qx.start_far()
-    half = TOK // 2
+    half = ROWS // 2
     top_r, bot_r = pl.ds(0, half), pl.ds(half, half)
     turn = (k, 1 - k)
     blocks = (x, xd, xu, xo)
@@ -192,8 +195,15 @@
 
     def project(xx, kk):
         j = xx * NC + kk
-        lat = lat_all[xx, kk, :, :, 0:LAT].reshape(CHUNK, LAT)
-        kr = lat_all[xx, kk, :, :, LAT:PACK].reshape(CHUNK, 128)
+        lat = jnp.concatenate(
+            [lat_all[xx, kk, :, t * TOK : (t + 1) * TOK, :].reshape(CHUNK, 128) for t in range(LAT // 128)],
+            axis=1,
+        )
+        side = lat_all[xx, kk, :, KROW:ROWS, :].reshape(128, 128).astype(F32)
+        swung = pltpu.roll(side, RD, 1)
+        first = jnp.where(lane_h < RD, side, swung).reshape(NY, TOK // 2, 128)
+        second = jnp.where(lane_h < RD, swung, side).reshape(NY, TOK // 2, 128)
+        kr = jnp.concatenate([first, second], axis=1).reshape(CHUNK, 128).astype(BF)
         lt = lat.T
         lat_t[:, pl.ds(pl.multiple_of(j * CHUNK, CHUNK), CHUNK)] = lt
         kv = dot(lat, w_all[...]).astype(BF)
@@ -265,6 +275,7 @@
     sub = lax.broadcasted_iota(jnp.int32, (TOK, 1), 0)
     lane_k = lax.broadcasted_iota(jnp.int32, (CHUNK, 128), 1)
     row_k = lax.broadcasted_iota(jnp.int32, (128, CHUNK), 0)
+    lane_h = lax.broadcasted_iota(jnp.int32, (128, 128), 1)
     zero = jnp.zeros((), BF)
 
     qx.relay()
@@ -312,16 +323,19 @@
         a, b = spans[j]
         for h in range(2):
             p = jnp.exp2(sc[h, j, :, a:b] - top_s[h][:, a:b])
-            sc[h, j, :, a:b] = p
+            pb[h, j, :, a:b] = p.astype(BF)
             tot[h] = splice(tot[h], tot[h][:, a:b] + jnp.sum(p, axis=0, keepdims=True), a, b)
-            o_t[h, :, a:b] += dot(vt[h, j], p.astype(BF))
+            o_t[h, :, a:b] += dot(vt[h, j], pb[h, j, :, a:b])
 
     inv = [1.0 / tot[h] for h in range(2)]
     delta = []
     for h in range(2):
         out = o_t[h] * inv[h]
         o_out[:, :, h * 128 : (h + 1) * 128] = out.T.astype(BF).reshape(NCTX, TOK, 128)
-        delta.append(jnp.sum(out * dot_t[h].astype(F32), axis=0, keepdims=True))
+        cot = dot_t[h].astype(F32)
+        delta.append(jnp.sum(out * cot, axis=0, keepdims=True))
+        do_s[h] = (cot * inv[h]).astype(BF).T
+    scaled = [inv[h] * SCALE for h in range(2)]
     ox = Exchange(lambda c: o_out.at[c], lambda c: o_in.at[c], o_mid, os, ors, sends)
     ox.start_far()
     ox.start_near()
@@ -331,9 +345,8 @@
         a, b = spans[j]
         r = slice(j * CHUNK, (j + 1) * CHUNK)
         for h in range(2):
-            p = sc[h, j, :, a:b] * inv[h][:, a:b]
-            do = q_all[a // TOK : b // TOK, :, 256 + h * 128 : 256 + (h + 1) * 128].reshape(b - a, 128)
-            gv[r, h * 128 : (h + 1) * 128] = dot(p.astype(BF), do).astype(BF)
+            part = dot(pb[h, j, :, a:b], do_s[h, a:b, :])
+            gv[r, h * 128 : (h + 1) * 128] = part.astype(BF)
 
     def weight_grad(buf, g):
         for i in range(2):
@@ -379,16 +392,22 @@
         kr_g = []
         for h in range(2):
             dp = dot(v[h, j], dot_t[h, :, a:b])
-            g = (sc[h, j, :, a:b] * ((dp - delta[h][:, a:b]) * inv[h][:, a:b])).astype(BF)
-            dk = dot(g, qc[h, a:b, :]) * SCALE
+            g = pb[h, j, :, a:b].astype(F32) * ((dp - delta[h][:, a:b]) * scaled[h][:, a:b])
+            g = g.astype(BF)
+            dk = dot(g, qc[h, a:b, :])
             dq_t[h, :, a:b] += dot(kct[h, j], g)
             gk[r, h * 128 : (h + 1) * 128] = dk[:, 0:128].astype(BF)
             kr_g.append(dk[:, 128:256])
         xx, kk = j // NC, j % NC
-        kr_part = jnp.where(lane_k < RD, kr_g[0], kr_g[1]).astype(BF)
-        lk[xx, kk, :, :, LAT:PACK] = kr_part.reshape(NY, TOK, 128)
+        both = kr_g[0] + pltpu.roll(kr_g[1], RD, 1)
+        moved = pltpu.roll(both, RD, 1).reshape(NY, TOK, 128)[:, TOK // 2 :]
+        both = both.reshape(NY, TOK, 128)[:, : TOK // 2]
+        kr_part = jnp.where(lane_h < RD, both.reshape(128, 128), moved.reshape(128, 128)).astype(BF)
+        lk[xx, kk, :, KROW:ROWS, :] = kr_part.reshape(NY, TOK // 2, 128)
         lat_part = (dot(gk[r, :], w_t[0:256, :]) + dot(gv[r, :], w_t[256:512, :])).astype(BF)
-        lk[xx, kk, :, :, 0:LAT] = lat_part.reshape(NY, TOK, LAT)
+        for t in range(LAT // 128):
+            tile = lat_part[:, t * 128 : (t + 1) * 128].reshape(NY, TOK, 128)
+            lk[xx, kk, :, t * TOK : (t + 1) * TOK, :] = tile
         if kk == 1:
             swc.append(go(rc(lk.at[xx, 1 - k], sw_in.at[xx], ss.at[xx], sr.at[xx], sib)))
         if j == 3:
@@ -399,16 +418,16 @@
             merge(1)
         if j == 7:
             pass_on(0)
-    d_cols = [(dq_t[h, 0:128, :] * SCALE).T.astype(BF) for h in range(2)]
-    d_cols.append(((dq_t[0, 128:256, :] + dq_t[1, 128:256, :]) * SCALE).T.astype(BF))
+    merge(2)
+    weight_grad(zk_out, gk)
+    zk = send_z(zk_out, zk_in, zks, zkr)
+    d_cols = [dq_t[h, 0:128, :].T.astype(BF) for h in range(2)]
+    d_cols.append((dq_t[0, 128:256, :] + dq_t[1, 128:256, :]).T.astype(BF))
     for n in range(3):
         d_out[:, :, n * 128 : (n + 1) * 128] = d_cols[n].reshape(NCTX, TOK, 128)
     dx = Exchange(lambda c: d_out.at[c], lambda c: d_in.at[c], d_mid, gs, grs, sends)
     dx.start_far()
     d_in[ctx] = d_out[ctx]
-    merge(2)
-    weight_grad(zk_out, gk)
-    zk = send_z(zk_out, zk_in, zks, zkr)
     pass_on(1)
     merge(3)
     xcp = {}
@@ -496,8 +515,11 @@
         t = own[...].astype(F32)
         for d in range(3):
             t = t + inbox[d].astype(F32)
-        latg_ref[0, rows] = t[:, 0:LAT].astype(BF)
-        krg_ref[0, rows] = (t[:, LAT : LAT + RD] + t[:, LAT + RD :]).astype(BF)
+        rows_n[rows] = t
+    for t in range(LAT // 128):
+        latg_ref[0, :, t * 128 : (t + 1) * 128] = rows_n[t * TOK : (t + 1) * TOK, :].astype(BF)
+    krg_ref[0, 0 : TOK // 2] = rows_n[KROW:ROWS, 0:RD].astype(BF)
+    krg_ref[0, TOK // 2 :] = rows_n[KROW:ROWS, RD:].astype(BF)
     put(3, latg_ref, latg_h)
     put(4, krg_ref, krg_h)
     for copy in wc:
@@ -530,7 +552,7 @@
     def vm(*shape, dtype=BF):
         return pltpu.VMEM(shape, dtype)
 
-    half = TOK // 2
+    half = ROWS // 2
     table = pltpu.SMEM((1, NX * NC * NY), jnp.int32)
     return pl.pallas_call(
         core_kernel,
@@ -543,21 +565,22 @@
             vm(1, TOK, HEADS, HD), vm(1, TOK, HEADS, RD), vm(1, TOK, HEADS * HD),
             vm(1, TOK, LAT), vm(1, TOK, RD), vm(LAT, 256), vm(LAT, 256),
             table, table, table,
-            vm(TOK, PACK), vm(NCTX, TOK, PACK), vm(NCTX, TOK, PACK), vm(2, TOK, PACK),
-            vm(NX, NC, NY, TOK, PACK),
+            vm(ROWS, 128), vm(NCTX, TOK, PACK), vm(NCTX, TOK, PACK), vm(2, TOK, PACK),
+            vm(NX, NC, NY, ROWS, 128),
             vm(LAT, 512), vm(512, LAT), vm(LAT, NK),
             vm(2, NCH, CHUNK, 256), vm(2, NCH, 256, CHUNK),
             vm(2, NCH, CHUNK, 128), vm(2, NCH, 128, CHUNK),
             vm(2, NQ, 256), vm(2, 256, NQ), vm(2, 128, NQ),
             vm(2, NCH, CHUNK, NQ, dtype=F32), vm(2, 1, NQ, dtype=F32),
+            vm(2, NCH, CHUNK, NQ), vm(2, NQ, 128),
             vm(NK, 256), vm(NK, 256),
             vm(2, 128, NQ, dtype=F32), vm(2, 256, NQ, dtype=F32),
             vm(NCTX, TOK, 256), vm(NCTX, TOK, 256), vm(2, TOK, 256),
             vm(NCTX, TOK, 384), vm(NCTX, TOK, 384), vm(2, TOK, 384),
-            vm(NX, NC, NY, TOK, PACK), vm(NX, NY, TOK, PACK), vm(NX, NY, TOK, PACK),
-            vm(NX, half, PACK), vm(NX, half, PACK), vm(NX, half, PACK),
-            vm(2, 2, half, PACK), vm(NY, half, PACK), vm(NY, half, PACK),
-            vm(NX, half, PACK), vm(NY, half, PACK), vm(3, half, PACK), vm(3, half, PACK),
+            vm(NX, NC, NY, ROWS, 128), vm(NX, NY, ROWS, 128), vm(NX, NY, ROWS, 128),
+            vm(NX, half, 128), vm(NX, half, 128), vm(NX, half, 128),
+            vm(2, 2, half, 128), vm(NY, half, 128), vm(NY, half, 128),
+            vm(NX, half, 128), vm(NY, half, 128), vm(3, half, 128), vm(3, half, 128),
             vm(NZ, TOK, 256), vm(NZ, TOK, 256), vm(NZ - 1, TOK, 256), vm(NZ - 1, TOK, 256),
             vm(NY, 16, 512), vm(NY - 1, 16, 512),
             DMA((10,)), DMA((4,)), DMA((4,)), DMA((4,)), DMA((4,)), DMA((4,)), DMA((4,)),

time: 63.5 us -> 62.1 us (0.978)
  Pallas kernels: 61.9 us -> 61.1 us
    pallas_call x1, Pallas kernels: 59.9 us -> 59.1 us  [core(): pl.pallas_call(core_kernel, out_shape=tuple((jax.ShapeDtypeStruct(s, d) f...]
where the time goes in v7:
time: 62.1 us; the launch traced here: 61.9 us
  Pallas kernels  61.1 us (98%)
  between operations  0.8 us (1%)
    pallas_call x1, Pallas kernels, core(): pl.pallas_call(core_kernel, out_shape=tuple((jax.ShapeDtypeStruct(s, d) f...  59.1 us
    pallas_call x1, Pallas kernels, store(): pl.pallas_call(store_kernel, out_shape=tuple((jax.ShapeDtypeStruct(s, d)...  1.97 us

profile of v7, /device:TPU:2, one launch (start us, length us, event | category | flops | bytes accessed | tf_op | source)
XLA Modules:
  0.0 61.9 jit_solution(8754816336826856878)
XLA Ops:
  0.6 59.1 %core.1 = (bf16[1,64,2048]{2,1,0:T(8,128)(2,1)}, bf16[1,64,16,128]{3,2,1,0:T(8,128)(2,1)}, bf16[1,64,16,64]{3,2,1,0:T(8,128)(2,1)}, bf16[1,64,512]{2,1,0:T(8,128...) custom-call(bf16[1,64,16,128]{3,2,1,0:T(8,128)(2,1)} %qn_h.1, ...), custom_call_target="tpu_custom_call" | custom-call | tf_op jit(solution)/shard_map/core/pallas_call | solution.py:557
  59.7 2.0 %store.1 = (bf16[1,64,2048]{2,1,0:T(8,128)(2,1)}, bf16[1,64,16,128]{3,2,1,0:T(8,128)(2,1)}, bf16[1,64,16,64]{3,2,1,0:T(8,128)(2,1)}, bf16[1,64,512]{2,1,0:T(8,12...) custom-call(bf16[1,64,2048]{2,1,0:T(8,128)(2,1)} %get-tuple-element.14.refs_0_, ...), custom_call_target="tpu_custom_call" | custom-call | tf_op jit(solution)/shard_map/store/pallas_call | solution.py:614
